TPU v7x, 1024 devices: a whole 8x8x8 slice. The times are simulated.
1024 devices in a mesh: shot: 4 (over x_hi), gx: 32 (over z, x_lo, core), gy: 8 (over y).
Axes of the slice: x: 8 (x_hi: 4, x_lo: 2; x = x_hi * 2 + x_lo), y: 8, z: 8, core: 2. Of those that a mesh axis runs over, the one named last changes fastest.
Arguments:
- p_adjoint: float32 [4, 128, 128, 128], P('shot', 'gx', 'gy'), may hold values from -6 to 6
- q_adjoint: float32 [4, 128, 128, 128], P('shot', 'gx', 'gy'), may hold values from -6 to 6
- p_previous: float32 [4, 128, 128, 128], P('shot', 'gx', 'gy'), may hold values from -6 to 6
- q_previous: float32 [4, 128, 128, 128], P('shot', 'gx', 'gy'), may hold values from -6 to 6
- forward_p: float32 [4, 2, 128, 128, 128], P('shot', None, 'gx', 'gy'), may hold values from -6 to 6
- courant: float32 [128, 128, 128], P('gx', 'gy'), may hold values from 0.04 to 0.12
- epsilon: float32 [128, 128, 128], P('gx', 'gy'), may hold values from 0.12 to 0.3
- delta_field: float32 [128, 128, 128], P('gx', 'gy'), may hold values from -0.08 to 0.1
- tilt_angle: float32 [128, 128, 128], P('gx', 'gy'), may hold values from -3.140625 to 3.140625
- azimuth: float32 [128, 128, 128], P('gx', 'gy'), may hold values from -3.140625 to 3.140625
- receiver_cells: int32 [4, 2048], P('shot'), may hold values from 0 to 16383
- receiver_values: float32 [4, 2, 2048], P('shot'), may hold values from -6 to 6
- boundary_cells: int32 [2048], replicated, may hold values from 0 to 2097151
- boundary_force: float32 [4, 2, 2048], P('shot'), may hold values from -6 to 6
- source_cells: int32 [4], P('shot'), may hold values from 0 to 16383
Outputs:
- p_final: float32 [4, 128, 128, 128], P('shot', 'gx', 'gy')
- q_final: float32 [4, 128, 128, 128], P('shot', 'gx', 'gy')
- grad_epsilon: float32 [128, 128, 128], P('gx', 'gy')
- grad_delta: float32 [128, 128, 128], P('gx', 'gy')
Inputs may be any that keep to these rules, and one draw needn't show every extreme that they name: `receiver_cells`: x * 128 + y of a receiver at depth index 0. `boundary_cells`: (x * 128 + y) * 128 + z of a boundary layer cell; a cell may repeat. `source_cells`: x * 128 + y of the shot's source.
All inputs are finite; a program needn't handle non-finite values.
Results may differ from a plain program's by a relative error of at most 0.0003.
Values sent between devices are 32-bit elements; how exact they have to be, the bound alone decides.
No kernel may reach another device: no remote copies, remote signals or barrier semaphores. Data moves between devices by JAX's collectives and lax.ppermute only.
A program may use at most 32 MiB of HBM per device.

v0:
```python
import jax
import jax.numpy as jnp
from jax import lax
from jax.sharding import PartitionSpec as P

ITERS = 2
TAPER = 32


FIRST_WEIGHTS = (1.0 / 12.0, -2.0 / 3.0, 0.0, 2.0 / 3.0, -1.0 / 12.0)
SECOND_WEIGHTS = (-1.0 / 12.0, 4.0 / 3.0, -2.5, 4.0 / 3.0, -1.0 / 12.0)
AXIS_PAIRS = ((0, 0), (1, 1), (2, 2), (0, 1), (0, 2), (1, 2))


def with_halo(cells, sides, width):
    for axis, dim in sides:
        count = lax.axis_size(axis)
        ends = count - 1
        head = lax.slice_in_dim(cells, 0, width, axis=dim)
        tail = lax.slice_in_dim(cells, cells.shape[dim] - width, cells.shape[dim], axis=dim)
        cells = jnp.concatenate(
            [
                lax.ppermute(tail, axis, [(i, (i + 1) % count) for i in range(ends)]),
                cells,
                lax.ppermute(head, axis, [((i + 1) % count, i) for i in range(ends)]),
            ],
            axis=dim,
        )
    return cells


def depth_table(weights, length):
    rows = jnp.arange(length, dtype=jnp.int32)[:, None]
    cols = jnp.arange(length, dtype=jnp.int32)[None, :]
    offset = rows - cols
    table = jnp.zeros((length, length), jnp.float32)
    for number in range(5):
        if weights[number] != 0.0:
            table = table + jnp.where(
                offset == number - 2, jnp.float32(weights[number]), jnp.float32(0.0)
            )
    return table


def stencil(field, along, weights):
    if along == field.ndim - 1:
        table = depth_table(weights, field.shape[along])
        return jnp.dot(
            field, table, precision=lax.Precision.HIGHEST, preferred_element_type=jnp.float32
        )
    length = field.shape[along] - 4
    summed = None
    for offset in range(5):
        if weights[offset] != 0.0:
            piece_term = weights[offset] * lax.slice_in_dim(
                field, offset, offset + length, axis=along
            )
            summed = piece_term if summed is None else summed + piece_term
    return summed


def trimmed(field, alongs):
    for along in alongs:
        field = lax.slice_in_dim(field, 2, field.shape[along] - 2, axis=along)
    return field


def pair_part(field, first_axis, second_axis):
    base_axis = field.ndim - 3
    if first_axis == second_axis:
        others = [base_axis + other for other in range(2) if other != first_axis]
        return trimmed(stencil(field, base_axis + first_axis, SECOND_WEIGHTS), others)
    remaining = 3 - first_axis - second_axis
    inner_part = stencil(field, base_axis + first_axis, FIRST_WEIGHTS)
    outer_part = stencil(inner_part, base_axis + second_axis, FIRST_WEIGHTS)
    alongs = [base_axis + remaining] if remaining < 2 else []
    return 2.0 * trimmed(outer_part, alongs)


def laplace(field):
    return pair_part(field, 0, 0) + pair_part(field, 1, 1) + pair_part(field, 2, 2)


def axis_products(tilt_angle, azimuth):
    sine = jnp.sin(tilt_angle)
    normal = (sine * jnp.cos(azimuth), sine * jnp.sin(azimuth), jnp.cos(tilt_angle))
    return [normal[first_axis] * normal[second_axis] for first_axis, second_axis in AXIS_PAIRS]


def axial_forward(field, products):
    summed = None
    for number, pair in enumerate(AXIS_PAIRS):
        piece_term = products[number] * pair_part(field, pair[0], pair[1])
        summed = piece_term if summed is None else summed + piece_term
    return summed


def axial_adjoint(field, products):
    summed = None
    for number, pair in enumerate(AXIS_PAIRS):
        piece_term = pair_part(products[number] * field, pair[0], pair[1])
        summed = piece_term if summed is None else summed + piece_term
    return summed


def inject(field, cell_x, cell_y, cell_z, values, start_x, start_y):
    shot_count, size_x, size_y, size_z = field.shape
    local_x = cell_x - start_x
    local_y = cell_y - start_y
    inside = (local_x >= 0) & (local_x < size_x) & (local_y >= 0) & (local_y < size_y)
    beyond = size_x * size_y * size_z
    flat = jnp.where(inside, (local_x * size_y + local_y) * size_z + cell_z, beyond)
    rows = jnp.broadcast_to(jnp.arange(shot_count, dtype=jnp.int32)[:, None], flat.shape)
    return (
        field.reshape(shot_count, -1).at[rows, flat].add(values, mode="drop").reshape(field.shape)
    )


def source_taper(source_cells, start_x, start_y, size_x, size_y, width_y, radius):
    source_x = source_cells // width_y
    source_y = source_cells % width_y
    coord_x = start_x + jnp.arange(size_x, dtype=jnp.int32)
    coord_y = start_y + jnp.arange(size_y, dtype=jnp.int32)
    offset_x = coord_x[None, :, None] - source_x[:, None, None]
    offset_y = coord_y[None, None, :] - source_y[:, None, None]
    squared = (offset_x * offset_x + offset_y * offset_y).astype(jnp.float32)
    return jnp.minimum(squared / float(radius * radius), 1.0)[..., None]


def body(
    p_adjoint,
    q_adjoint,
    p_previous,
    q_previous,
    forward_p,
    courant,
    epsilon,
    delta_field,
    tilt_angle,
    azimuth,
    receiver_cells,
    receiver_values,
    boundary_cells,
    boundary_force,
    source_cells,
):
    shot_count, size_x, size_y, size_z = p_adjoint.shape
    width_y = size_y * lax.axis_size("gy")
    start_x = lax.axis_index("gx") * size_x
    start_y = lax.axis_index("gy") * size_y
    angle_pad = with_halo(jnp.stack([tilt_angle, azimuth]), (("gx", 1), ("gy", 2)), 2)
    pad_products = axis_products(angle_pad[0], angle_pad[1])
    inner_products = axis_products(tilt_angle, azimuth)
    p_weight = courant * (1.0 + 2.0 * epsilon)
    q_weight = courant * (1.0 + 2.0 * delta_field)
    twice = 2.0 * courant
    recv_x = receiver_cells // width_y
    recv_y = receiver_cells % width_y
    recv_z = jnp.zeros_like(receiver_cells)
    bound_x = (boundary_cells // (width_y * size_z))[None, :]
    bound_y = (boundary_cells // size_z % width_y)[None, :]
    bound_z = (boundary_cells % size_z)[None, :]
    taper = source_taper(source_cells, start_x, start_y, size_x, size_y, width_y, TAPER)
    grad_e = jnp.zeros((size_x, size_y, size_z), jnp.float32)
    grad_d = jnp.zeros((size_x, size_y, size_z), jnp.float32)
    illum = jnp.zeros((size_x, size_y, size_z), jnp.float32)
    p_now, q_now, p_old, q_old = (p_adjoint, q_adjoint, p_previous, q_previous)
    for step in range(ITERS):
        snapshot = forward_p[:, step]
        weighted = p_weight * p_now + q_weight * q_now
        mixed = courant * (p_now + q_now)
        three_pad = with_halo(jnp.stack([weighted, mixed, snapshot]), (("gx", 2), ("gy", 3)), 2)
        source_pad, mix_pad, forward_pad = (three_pad[0], three_pad[1], three_pad[2])
        image = twice * (laplace(forward_pad) - axial_forward(forward_pad, inner_products))
        grad_e = grad_e + jnp.sum(taper * p_now * image, axis=0)
        grad_d = grad_d + jnp.sum(taper * q_now * image, axis=0)
        illum = illum + jnp.sum(snapshot * snapshot, axis=0)
        p_next = 2.0 * p_now - p_old + laplace(source_pad) - axial_adjoint(source_pad, pad_products)
        p_next = inject(p_next, recv_x, recv_y, recv_z, receiver_values[:, step], start_x, start_y)
        p_next = inject(
            p_next, bound_x, bound_y, bound_z, boundary_force[:, step], start_x, start_y
        )
        q_next = 2.0 * q_now - q_old + axial_adjoint(mix_pad, pad_products)
        p_old, q_old, p_now, q_now = (p_now, q_now, p_next, q_next)
    total_e, total_d, total_illum = lax.psum((grad_e, grad_d, illum), "shot")
    scale = jnp.sqrt(total_illum + 1.0)
    result_e = total_e / scale
    result_d = total_d / scale
    return (p_now, q_now, result_e, result_d)


def solution(mesh):
    in_specs = (
        P("shot", "gx", "gy", None),
        P("shot", "gx", "gy", None),
        P("shot", "gx", "gy", None),
        P("shot", "gx", "gy", None),
        P("shot", None, "gx", "gy", None),
        P("gx", "gy", None),
        P("gx", "gy", None),
        P("gx", "gy", None),
        P("gx", "gy", None),
        P("gx", "gy", None),
        P("shot", None),
        P("shot", None, None),
        P(),
        P("shot", None, None),
        P("shot"),
    )
    out_specs = (
        P("shot", "gx", "gy", None),
        P("shot", "gx", "gy", None),
        P("gx", "gy", None),
        P("gx", "gy", None),
    )
    return jax.shard_map(body, mesh=mesh, in_specs=in_specs, out_specs=out_specs, check_vma=False)
```

profile of v0, /device:TPU:4, one launch (start us, length us, event | category | flops | bytes accessed | tf_op | source)
XLA Modules:
  0.0 176.1 jit_solution(6966949767966594357)
XLA Ops:
  7.3 1.4 add_bitcast_fusion.1
  8.8 1.7 collective-permute-start
  10.5 1.3 collective-permute-start.1
  11.9 4.3 %collective-permute-start.4 = (f32[2,2,16,128]{3,2,1,0:T(8,128)S(1)}, f32[2,2,16,128]{3,2,1,0:T(8,128)S(1)}, u32[]{:S(2)}, u32[]{:S(2)}) collective-permute-start(f32[2,2,16,128]{3,2,1,0:T(8,128)S(1)} %get-tuple-element.155), channel_id=1, source_target_pairs={{0,8},{8,16},{16,24},{24,32},{32,40},{40,48},{48,56},{56,64},{64,7... | collective-permute-start | bytes 98312 | tf_op jit(solution)/shard_map/ppermute | solution.py:23
  16.2 1.3 collective-permute-start.5
  18.3 0.7 copy-done.12
  19.0 0.7 copy-done.13
  19.8 0.6 copy-done.14
  20.5 0.5 copy-done.15
  21.2 0.6 copy-done.10
  21.8 0.7 copy-done.11
  22.7 3.6 %collective-permute-start.6 = (f32[2,8,2,128]{3,2,1,0:T(2,128)S(1)}, f32[2,8,2,128]{3,2,1,0:T(2,128)S(1)}, u32[]{:S(2)}, u32[]{:S(2)}) collective-permute-start(f32[2,8,2,128]{3,2,1,0:T(2,128)S(1)} %get-tuple-element.62), channel_id=1, source_target_pairs={{0,1},{1,2},{2,3},{3,4},{4,5},{5,6},{6,7},{8,9},{9,10},{10,11},{11... | collective-permute-start | bytes 49160 | tf_op jit(solution)/shard_map/ppermute | solution.py:23
  26.3 1.3 collective-permute-start.7
  27.7 4.5 %collective-permute-start.2 = (f32[3,1,8,2,128]{4,3,2,1,0:T(2,128)S(1)}, f32[3,1,8,2,128]{4,3,2,1,0:T(2,128)S(1)}, u32[]{:S(2)}, u32[]{:S(2)}) collective-permute-start(f32[3,1,8,2,128]{4,3,2,1,0:T(2,128)S(1)} %get-tuple-element.60), channel_id=1, source_target_pairs={{0,1},{1,2},{2,3},{3,4},{4,5},{5,6},{6,7},{8,9},{9,10},{10,11},{11... | collective-permute-start | bytes 73736 | tf_op jit(solution)/shard_map/ppermute | solution.py:23
  32.2 1.3 collective-permute-start.3
  33.7 4.2 %collective-permute-done.3 = f32[3,1,8,2,128]{4,3,2,1,0:T(2,128)S(1)} collective-permute-done((f32[3,1,8,2,128]{4,3,2,1,0:T(2,128)S(1)}, f32[3,1,8,2,128]{4,3,2,1,0:T(2,128)S(1)}, u32[]{:S(2)}, u32[]{:S(2)}) %collective-permute-start.3) | collective-permute-done | bytes 24608 | tf_op jit(solution)/shard_map/ppermute | solution.py:25
  38.0 0.6 multiply_multiply_fusion.6
  38.6 0.6 convolution_bitcast_fusion.6
  39.3 0.3 convolution_bitcast_fusion.7
  39.6 0.6 convolution_bitcast_fusion.5
  40.2 0.2 convolution_bitcast_fusion.9
  40.5 0.7 fusion.21
  41.2 0.3 fusion.22
  41.6 0.2 convolution_bitcast_fusion.13
  42.1 0.2 convolution_bitcast_fusion.12
  42.6 0.7 copy-done.8
  43.5 11.6 %scatter_fusion = f32[8192]{0:T(1024)S(1)} fusion(f32[8192]{0:T(1024)S(1)} %bitcast.297, s32[2048]{0:T(1024)S(1)} %get-tuple-element.167, f32[2048]{0:T(1024)S(1)} %bitcast.315), kind=kCustom, calls=%fused_computation | custom fusion | flops 2048 | bytes 32768
  55.1 11.6 %scatter_fusion.1 = f32[8192]{0:T(1024)S(1)} fusion(f32[8192]{0:T(1024)S(1)} %scatter_fusion, s32[2048]{0:T(1024)S(1)} %get-tuple-element.166, f32[2048]{0:T(1024)S(1)} %bitcast.314), kind=kCustom, calls=%fused_computation.1 | custom fusion | flops 2048 | bytes 32768
  66.8 2.3 %collective-permute-start.8 = (f32[3,1,2,16,128]{4,3,2,1,0:T(8,128)S(1)}, f32[3,1,2,16,128]{4,3,2,1,0:T(8,128)S(1)}, u32[]{:S(2)}, u32[]{:S(2)}) collective-permute-start(f32[3,1,2,16,128]{4,3,2,1,0:T(8,128)S(1)} %get-tuple-element.116), channel_id=1, source_target_pairs={{0,8},{8,16},{16,24},{24,32},{32,40},{40,48},{48,56},{56,64},{64,7... | collective-permute-start | bytes 147464 | tf_op jit(solution)/shard_map/ppermute | solution.py:23
  69.1 1.3 collective-permute-start.9
  70.4 0.3 convolution_bitcast_fusion.1
  70.7 4.8 %collective-permute-done.9 = f32[3,1,2,16,128]{4,3,2,1,0:T(8,128)S(1)} collective-permute-done((f32[3,1,2,16,128]{4,3,2,1,0:T(8,128)S(1)}, f32[3,1,2,16,128]{4,3,2,1,0:T(8,128)S(1)}, u32[]{:S(2)}, u32[]{:S(2)}) %collective-permute-start.9) | collective-permute-done | bytes 49184 | tf_op jit(solution)/shard_map/ppermute | solution.py:25
  75.5 4.2 %collective-permute-start.10 = (f32[3,1,8,2,128]{4,3,2,1,0:T(2,128)S(1)}, f32[3,1,8,2,128]{4,3,2,1,0:T(2,128)S(1)}, u32[]{:S(2)}, u32[]{:S(2)}) collective-permute-start(f32[3,1,8,2,128]{4,3,2,1,0:T(2,128)S(1)} %get-tuple-element.58), channel_id=1, source_target_pairs={{0,1},{1,2},{2,3},{3,4},{4,5},{5,6},{6,7},{8,9},{9,10},{10,11},{11... | collective-permute-start | bytes 73736 | tf_op jit(solution)/shard_map/ppermute | solution.py:23
  79.6 1.5 collective-permute-start.11
  81.4 5.2 %collective-permute-done.11 = f32[3,1,8,2,128]{4,3,2,1,0:T(2,128)S(1)} collective-permute-done((f32[3,1,8,2,128]{4,3,2,1,0:T(2,128)S(1)}, f32[3,1,8,2,128]{4,3,2,1,0:T(2,128)S(1)}, u32[]{:S(2)}, u32[]{:S(2)}) %collective-permute-start.11) | collective-permute-done | bytes 24608 | tf_op jit(solution)/shard_map/ppermute | solution.py:25
  86.7 0.2 convolution_bitcast_fusion.8
  87.0 0.3 convolution_bitcast_fusion
  87.3 0.6 convolution_bitcast_fusion.2
  87.9 0.6 convolution_bitcast_fusion.3
  88.6 0.3 convolution_bitcast_fusion.4
  89.1 0.2 convolution_bitcast_fusion.10
  90.2 0.9 add_bitcast_fusion
  91.1 0.7 add_bitcast_fusion.2
  91.9 0.7 fusion.157
  92.6 11.5 %scatter_fusion.2 = f32[8192]{0:T(1024)S(1)} fusion(f32[8192]{0:T(1024)S(1)} %bitcast.302, s32[2048]{0:T(1024)S(1)} %get-tuple-element.167, f32[2048]{0:T(1024)S(1)} %bitcast.313), kind=kCustom, calls=%fused_computation.2 | custom fusion | flops 2048 | bytes 32768
  104.2 11.6 %scatter_fusion.3 = f32[8192]{0:T(1024)S(1)} fusion(f32[8192]{0:T(1024)S(1)} %scatter_fusion.2, s32[2048]{0:T(1024)S(1)} %get-tuple-element.166, f32[2048]{0:T(1024)S(1)} %bitcast.312), kind=kCustom, calls=%fused_computation.3 | custom fusion | flops 2048 | bytes 32768
  115.7 52.1 %all-reduce.5.cloned.1.call-done = (f32[4,16,128]{2,1,0:T(8,128)}, f32[4,16,128]{2,1,0:T(8,128)}, f32[4,16,128]{2,1,0:T(8,128)}) async-done(((f32[4,16,128]{2,1,0:T(8,128)}, f32[4,16,128]{2,1,0:T(8,128)}, f32[4,16,128]{2,1,0:T(8,128)}), (f32[4,16,128]{2,1,0:T(8,128)}, f32[4,16,128]{2,1,0:T(8,128)}, f32[4,16,128]{2,1,0:T(8,128)})) %all-reduce.5.cloned.1.call-update) | async-done | bytes 98320 | tf_op jit(solution)/shard_map/psum | solution.py:185
  167.8 1.4 fusion.455
  (92 shorter events, 3.5 us)
Async XLA Ops:
  7.2 1.5 copy-start.3
  7.2 1.5 copy-start.1
  7.2 1.5 copy-start.2
  7.2 1.5 copy-start.6
  7.2 1.5 copy-start.7
  7.2 160.6 %all-reduce.5.cloned.1.call-start = ((), (), s32[]{:S(2)}) async-start(), calls=%async_computation | async-start | bytes 196608 | tf_op jit(solution)/shard_map/psum | solution.py:185
  8.7 3.1 %copy-start.4 = (f32[4,16,128]{2,1,0:T(8,128)S(1)}, f32[4,16,128]{2,1,0:T(8,128)}, u32[]{:S(2)}) copy-start(f32[4,16,128]{2,1,0:T(8,128)} %param.23) | copy-start | bytes 98308
  8.7 3.1 %copy-start.5 = (f32[4,16,128]{2,1,0:T(8,128)S(1)}, f32[4,16,128]{2,1,0:T(8,128)}, u32[]{:S(2)}) copy-start(f32[4,16,128]{2,1,0:T(8,128)} %param.24) | copy-start | bytes 98308
  8.8 18.8 %collective-permute-start = (f32[3,1,2,16,128]{4,3,2,1,0:T(8,128)S(1)}, f32[3,1,2,16,128]{4,3,2,1,0:T(8,128)S(1)}, u32[]{:S(2)}, u32[]{:S(2)}) collective-permute-start(f32[3,1,2,16,128]{4,3,2,1,0:T(8,128)S(1)} %get-tuple-element.148), channel_id=1, source_target_pairs={{0,8},{8,16},{16,24},{24,32},{32,40},{40,48},{48,56},{56,64},{64,7... | collective-permute-start | bytes 147464 | tf_op jit(solution)/shard_map/ppermute | solution.py:23
  10.5 17.1 %collective-permute-start.1 = (f32[3,1,2,16,128]{4,3,2,1,0:T(8,128)S(1)}, f32[3,1,2,16,128]{4,3,2,1,0:T(8,128)S(1)}, u32[]{:S(2)}, u32[]{:S(2)}) collective-permute-start(f32[3,1,2,16,128]{4,3,2,1,0:T(8,128)S(1)} %get-tuple-element.149), channel_id=1, source_target_pairs={{8,0},{16,8},{24,16},{32,24},{40,32},{48,40},{56,48},{64,56},{72,6... | collective-permute-start | bytes 147464 | tf_op jit(solution)/shard_map/ppermute | solution.py:25
  11.9 10.8 %collective-permute-start.4 = (f32[2,2,16,128]{3,2,1,0:T(8,128)S(1)}, f32[2,2,16,128]{3,2,1,0:T(8,128)S(1)}, u32[]{:S(2)}, u32[]{:S(2)}) collective-permute-start(f32[2,2,16,128]{3,2,1,0:T(8,128)S(1)} %get-tuple-element.155), channel_id=1, source_target_pairs={{0,8},{8,16},{16,24},{24,32},{32,40},{40,48},{48,56},{56,64},{64,7... | collective-permute-start | bytes 98312 | tf_op jit(solution)/shard_map/ppermute | solution.py:23
  16.2 6.5 %collective-permute-start.5 = (f32[2,2,16,128]{3,2,1,0:T(8,128)S(1)}, f32[2,2,16,128]{3,2,1,0:T(8,128)S(1)}, u32[]{:S(2)}, u32[]{:S(2)}) collective-permute-start(f32[2,2,16,128]{3,2,1,0:T(8,128)S(1)} %get-tuple-element.156), channel_id=1, source_target_pairs={{8,0},{16,8},{24,16},{32,24},{40,32},{48,40},{56,48},{64,56},{72,6... | collective-permute-start | bytes 98312 | tf_op jit(solution)/shard_map/ppermute | solution.py:25
  18.3 0.7 copy-start.12
  19.0 0.7 copy-start.13
  19.8 0.7 copy-start.14
  20.4 0.7 copy-start.15
  21.1 0.7 copy-start.10
  21.8 0.7 copy-start.11
  22.7 10.8 %collective-permute-start.6 = (f32[2,8,2,128]{3,2,1,0:T(2,128)S(1)}, f32[2,8,2,128]{3,2,1,0:T(2,128)S(1)}, u32[]{:S(2)}, u32[]{:S(2)}) collective-permute-start(f32[2,8,2,128]{3,2,1,0:T(2,128)S(1)} %get-tuple-element.62), channel_id=1, source_target_pairs={{0,1},{1,2},{2,3},{3,4},{4,5},{5,6},{6,7},{8,9},{9,10},{10,11},{11... | collective-permute-start | bytes 49160 | tf_op jit(solution)/shard_map/ppermute | solution.py:23
  26.3 7.2 %collective-permute-start.7 = (f32[2,8,2,128]{3,2,1,0:T(2,128)S(1)}, f32[2,8,2,128]{3,2,1,0:T(2,128)S(1)}, u32[]{:S(2)}, u32[]{:S(2)}) collective-permute-start(f32[2,8,2,128]{3,2,1,0:T(2,128)S(1)} %get-tuple-element.63), channel_id=1, source_target_pairs={{1,0},{2,1},{3,2},{4,3},{5,4},{6,5},{7,6},{9,8},{10,9},{11,10},{12... | collective-permute-start | bytes 49160 | tf_op jit(solution)/shard_map/ppermute | solution.py:25
  27.7 6.1 %collective-permute-start.2 = (f32[3,1,8,2,128]{4,3,2,1,0:T(2,128)S(1)}, f32[3,1,8,2,128]{4,3,2,1,0:T(2,128)S(1)}, u32[]{:S(2)}, u32[]{:S(2)}) collective-permute-start(f32[3,1,8,2,128]{4,3,2,1,0:T(2,128)S(1)} %get-tuple-element.60), channel_id=1, source_target_pairs={{0,1},{1,2},{2,3},{3,4},{4,5},{5,6},{6,7},{8,9},{9,10},{10,11},{11... | collective-permute-start | bytes 73736 | tf_op jit(solution)/shard_map/ppermute | solution.py:23
  32.2 5.7 %collective-permute-start.3 = (f32[3,1,8,2,128]{4,3,2,1,0:T(2,128)S(1)}, f32[3,1,8,2,128]{4,3,2,1,0:T(2,128)S(1)}, u32[]{:S(2)}, u32[]{:S(2)}) collective-permute-start(f32[3,1,8,2,128]{4,3,2,1,0:T(2,128)S(1)} %get-tuple-element.61), channel_id=1, source_target_pairs={{1,0},{2,1},{3,2},{4,3},{5,4},{6,5},{7,6},{9,8},{10,9},{11,10},{12... | collective-permute-start | bytes 73736 | tf_op jit(solution)/shard_map/ppermute | solution.py:25
  42.6 0.8 copy-start.8
  55.1 11.6 %copy-start.9 = (f32[1,4,16,128]{3,2,1,0:T(8,128)S(1)}, f32[1,4,16,128]{3,2,1,0:T(8,128)}, u32[]{:S(2)}) copy-start(f32[1,4,16,128]{3,2,1,0:T(8,128)} %param.18) | copy-start | bytes 98308
  66.8 3.9 %collective-permute-start.8 = (f32[3,1,2,16,128]{4,3,2,1,0:T(8,128)S(1)}, f32[3,1,2,16,128]{4,3,2,1,0:T(8,128)S(1)}, u32[]{:S(2)}, u32[]{:S(2)}) collective-permute-start(f32[3,1,2,16,128]{4,3,2,1,0:T(8,128)S(1)} %get-tuple-element.116), channel_id=1, source_target_pairs={{0,8},{8,16},{16,24},{24,32},{32,40},{40,48},{48,56},{56,64},{64,7... | collective-permute-start | bytes 147464 | tf_op jit(solution)/shard_map/ppermute | solution.py:23
  69.1 6.4 %collective-permute-start.9 = (f32[3,1,2,16,128]{4,3,2,1,0:T(8,128)S(1)}, f32[3,1,2,16,128]{4,3,2,1,0:T(8,128)S(1)}, u32[]{:S(2)}, u32[]{:S(2)}) collective-permute-start(f32[3,1,2,16,128]{4,3,2,1,0:T(8,128)S(1)} %get-tuple-element.117), channel_id=1, source_target_pairs={{8,0},{16,8},{24,16},{32,24},{40,32},{48,40},{56,48},{64,56},{72,6... | collective-permute-start | bytes 147464 | tf_op jit(solution)/shard_map/ppermute | solution.py:25
  75.5 5.9 %collective-permute-start.10 = (f32[3,1,8,2,128]{4,3,2,1,0:T(2,128)S(1)}, f32[3,1,8,2,128]{4,3,2,1,0:T(2,128)S(1)}, u32[]{:S(2)}, u32[]{:S(2)}) collective-permute-start(f32[3,1,8,2,128]{4,3,2,1,0:T(2,128)S(1)} %get-tuple-element.58), channel_id=1, source_target_pairs={{0,1},{1,2},{2,3},{3,4},{4,5},{5,6},{6,7},{8,9},{9,10},{10,11},{11... | collective-permute-start | bytes 73736 | tf_op jit(solution)/shard_map/ppermute | solution.py:23
  79.6 6.9 %collective-permute-start.11 = (f32[3,1,8,2,128]{4,3,2,1,0:T(2,128)S(1)}, f32[3,1,8,2,128]{4,3,2,1,0:T(2,128)S(1)}, u32[]{:S(2)}, u32[]{:S(2)}) collective-permute-start(f32[3,1,8,2,128]{4,3,2,1,0:T(2,128)S(1)} %get-tuple-element.59), channel_id=1, source_target_pairs={{1,0},{2,1},{3,2},{4,3},{5,4},{6,5},{7,6},{9,8},{10,9},{11,10},{12... | collective-permute-start | bytes 73736 | tf_op jit(solution)/shard_map/ppermute | solution.py:25
  115.7 53.5 %copy-start = (f32[8192]{0:T(1024)}, f32[8192]{0:T(1024)S(1)}, u32[]{:S(2)}) copy-start(f32[8192]{0:T(1024)S(1)} %scatter_fusion.3) | copy-start | bytes 98308
Sparse Core Ops, SparseCore 0:
  91.9 75.8 all-reduce.4
where the time goes:
time: 177 us; the launch traced here: 176 us
  waiting for transfers between devices  66.5 us (38%)
  other arithmetic  54.4 us (31%)
  starting transfers between devices  28.6 us (16%)
  between operations  15.5 us (9%)
  matrix products  6.08 us (3%)
  local copies, waits for them, and re-layouts  5.06 us (3%)
    psum x1, waiting for transfers between devices, body(): total_e, total_d, total_illum = lax.psum((grad_e, grad_d, illum), 'shot')  52.1 us
    unnamed x7, other arithmetic  46.4 us
    ppermute x6, starting transfers between devices, with_halo(): lax.ppermute(tail, axis, [(i, (i + 1) % count) for i in range(ends)])  20.6 us
    ppermute x6, waiting for transfers between devices, with_halo(): lax.ppermute(head, axis, [((i + 1) % count, i) for i in range(ends)])  14.2 us
    ppermute x6, starting transfers between devices, with_halo(): lax.ppermute(head, axis, [((i + 1) % count, i) for i in range(ends)])  7.93 us
    dot_general x20, matrix products, stencil(): jnp.dot(field, table, precision=lax.Precision.HIGHEST, preferred_element_...  6.08 us
    unnamed x32, local copies, waits for them, and re-layouts  4.63 us
  transfers between devices with their start and end apart: 13, of which 5 were waited for; matrix products, arithmetic and copies ran while one was open for 14% of the time, Pallas kernels for 0%

commit v1 on v0

v1 whole, which is shorter than its diff:
```python
import functools

import jax
import jax.numpy as jnp
from jax import lax
from jax.experimental import pallas as pl
from jax.experimental.pallas import tpu as pltpu
from jax.sharding import PartitionSpec as P

TAPER = 32
WIDE = 5
NARROW = 7
PAIRS = ((0, 0), (1, 1), (2, 2), (0, 1), (0, 2), (1, 2))


def call(kernel, outs, args, scratch=(), smem=(), flops=2_000_000):
    specs = [
        pl.BlockSpec(memory_space=pltpu.SMEM if i in smem else pltpu.VMEM) for i in range(len(args))
    ]
    shapes = [jax.ShapeDtypeStruct(shape, jnp.float32) for shape in outs]
    return pl.pallas_call(
        kernel,
        out_shape=shapes,
        in_specs=specs,
        out_specs=[pl.BlockSpec(memory_space=pltpu.VMEM)] * len(outs),
        scratch_shapes=list(scratch),
        compiler_params=pltpu.CompilerParams(vmem_limit_bytes=24 * 1024 * 1024),
        cost_estimate=pl.CostEstimate(flops=flops, bytes_accessed=2_000_000, transcendentals=0),
    )(*args)


def row_mask(shape, below):
    return lax.broadcasted_iota(jnp.int32, shape, len(shape) - 2) < below


def shift_y(tiles, step, keep=3):
    if step > 0:
        rolled = [pltpu.roll(tile, 8 - step, 1) for tile in tiles]
        mask = row_mask(tiles[0].shape, 8 - step)
        return [jnp.where(mask, rolled[i], rolled[(i + 1) % 3]) for i in range(keep)]
    rolled = [pltpu.roll(tile, -step, 1) for tile in tiles]
    mask = row_mask(tiles[0].shape, -step)
    return [jnp.where(mask, rolled[(i + 2) % 3], rolled[i]) for i in range(keep)]


def shift_z(tile, step):
    lane = lax.broadcasted_iota(jnp.int32, tile.shape, 2)
    rolled = pltpu.roll(tile, (-step) % 128, 2)
    inside = lane < 128 - step if step > 0 else lane >= -step
    return jnp.where(inside, rolled, 0.0)


def second(far_low, low, here, high, far_high):
    return (4.0 / 3.0) * (low + high) - (1.0 / 12.0) * (far_low + far_high) - 2.5 * here


def first(far_low, low, high, far_high):
    return (2.0 / 3.0) * (high - low) - (1.0 / 12.0) * (far_high - far_low)


def second_x(tile, count):
    return second(*[tile[i : i + count] for i in range(5)])


def first_x(tile, count):
    return first(*[tile[i : i + count] for i in (0, 1, 3, 4)])


def first_y(tiles, keep):
    low2, low1, high1, high2 = [shift_y(tiles, step, keep) for step in (-2, -1, 1, 2)]
    return [first(low2[i], low1[i], high1[i], high2[i]) for i in range(keep)]


def both(parts_second, parts_first):
    near_even = (4.0 / 3.0) * parts_second
    near_odd = (2.0 / 3.0) * parts_first
    far_even = (-1.0 / 12.0) * parts_second
    far_odd = (1.0 / 12.0) * parts_first
    return (far_even + far_odd, near_even - near_odd, near_even + near_odd, far_even - far_odd)


def adjoint(products, source, count, keep, plus):
    mid = slice(2, 2 + count)
    aa = []
    for axis in range(3):
        scaled = [products[axis][i] * source[i] for i in range(3)]
        aa.append(scaled if plus else [source[i] - scaled[i] for i in range(3)])
    factor = 2.0 if plus else -2.0
    doubled = [factor * tile for tile in source]
    n01 = [products[3][i] * doubled[i] for i in range(3)]
    n02 = [products[4][i] * doubled[i] for i in range(keep)]
    n12 = [products[5][i][mid] * doubled[i][mid] for i in range(3)]
    out = [second_x(aa[0][i], count) for i in range(keep)]
    second_y = [tile[mid] for tile in aa[1]]
    cross_y = [first_x(tile, count) for tile in n01]
    mixed = [both(second_y[i], cross_y[i]) for i in range(3)]
    out = [out[i] - 2.5 * second_y[i] for i in range(keep)]
    for number, step in enumerate((-2, -1, 1, 2)):
        moved = shift_y([mixed[i][number] for i in range(3)], step, keep)
        out = [out[i] + moved[i] for i in range(keep)]
    along_y = first_y(n12, keep)
    for i in range(keep):
        second_z = aa[2][i][mid]
        cross_z = first_x(n02[i], count) + along_y[i]
        terms = both(second_z, cross_z)
        out[i] = out[i] - 2.5 * second_z
        for number, step in enumerate((-2, -1, 1, 2)):
            out[i] = out[i] + shift_z(terms[number], step)
    return out


def forward_image(products, field, count):
    mid = slice(2, 2 + count)
    inner = [tile[mid] for tile in field]
    slope_x = [first_x(tile, count) for tile in field]
    moved = [shift_y(inner, step, 2) for step in (-2, -1, 1, 2)]
    cross = first_y(slope_x, 2)
    out = []
    for i in range(2):
        here = inner[i]
        along = [moved[k][i] for k in range(4)]
        curve_x = second_x(field[i], count)
        curve_y = second(along[0], along[1], here, along[2], along[3])
        slope_y = first(*along)
        depth = [shift_z(here, step) for step in (-2, -1, 1, 2)]
        curve_z = second(depth[0], depth[1], here, depth[2], depth[3])
        total = (1.0 - products[0][i]) * curve_x
        total = total + (1.0 - products[1][i]) * curve_y
        total = total + (1.0 - products[2][i]) * curve_z
        cross_z = []
        for slope in (slope_x[i], slope_y):
            cross_z.append(first(*[shift_z(slope, step) for step in (-2, -1, 1, 2)]))
        mixed = products[3][i] * cross[i] + products[4][i] * cross_z[0] + products[5][i] * cross_z[1]
        out.append(total - 2.0 * mixed)
    return out


def prepare_kernel(p, q, p_old, q_old, f, c, eps, delta, tilt, azimuth, loc, low, high):
    size_x = p.shape[0]
    p_now, q_now, speed = p[...], q[...], c[...]
    p_weight = speed * (1.0 + 2.0 * eps[...])
    q_weight = speed * (1.0 + 2.0 * delta[...])
    sine = jnp.sin(tilt[...])
    wide = (
        p_weight * p_now + q_weight * q_now,
        speed * (p_now + q_now),
        sine * jnp.cos(azimuth[...]),
        sine * jnp.sin(azimuth[...]),
        jnp.cos(tilt[...]),
    )
    narrow = (
        2.0 * p_now - p_old[...],
        2.0 * q_now - q_old[...],
        p_weight,
        q_weight,
        speed,
        f[0],
        f[1],
    )
    for number, cells in enumerate(wide):
        rows = slice(number * size_x, (number + 1) * size_x)
        loc[rows] = cells
        low[rows] = cells
        high[rows] = cells
    for number, cells in enumerate(narrow):
        start = (WIDE + number) * size_x
        loc[start : start + size_x] = cells
        begin = WIDE * size_x + 2 * number
        low[begin : begin + 2] = cells[0:2]
        high[begin : begin + 2] = cells[size_x - 2 : size_x]


def tiles_of(loc, below, above, size_x, part):
    ys = slice(8 * part, 8 * part + 8)
    wide, narrow = [], []
    for number in range(WIDE):
        rows = slice(number * size_x, (number + 1) * size_x)
        wide += [below[rows, ys, :], loc[rows, ys, :], above[rows, ys, :]]
    for number in range(NARROW):
        start = (WIDE + number) * size_x
        begin = WIDE * size_x + 2 * number
        narrow += [
            below[begin : begin + 2, ys, :],
            loc[start : start + size_x, ys, :],
            above[begin : begin + 2, ys, :],
        ]
    return jnp.concatenate(wide, axis=0), jnp.concatenate(narrow, axis=0)


def pack_kernel(loc, below, above, down, up):
    size_x = loc.shape[0] // (WIDE + NARROW)
    for part, target in ((0, down), (1, up)):
        wide, narrow = tiles_of(loc, below, above, size_x, part)
        half = wide.shape[0] // 2
        quarter = narrow.shape[0] // 4
        turned = pltpu.roll(wide, 4, 1)
        mask = row_mask((half, 8, 128), 4)
        if part == 0:
            target[0:half] = jnp.where(mask, wide[:half], turned[half:])
        else:
            target[0:half] = jnp.where(mask, turned[:half], wide[half:])
        out = None
        for group in range(4):
            rows = narrow[group * quarter : (group + 1) * quarter]
            turn = (2 * group - 6 * part) % 8
            rows = pltpu.roll(rows, turn, 1) if turn else rows
            out = rows if out is None else jnp.where(row_mask(rows.shape, 2 * group), out, rows)
        target[half : half + quarter] = out


def unpack(loc, below, above, from_above, from_below):
    size_x = loc.shape[0] // (WIDE + NARROW)
    wide_rows, narrow_rows = 3 * size_x, size_x + 4
    half = WIDE * wide_rows // 2
    quarter = NARROW * narrow_rows // 4
    mask = row_mask((half, 8, 128), 4)
    high, low = from_above[0:half], from_below[0:half]
    wide_edge = jnp.concatenate(
        [jnp.where(mask, high, pltpu.roll(low, 4, 1)), jnp.where(mask, pltpu.roll(high, 4, 1), low)],
        axis=0,
    )
    high, low = from_above[half : half + quarter], from_below[half : half + quarter]
    mask = row_mask((quarter, 8, 128), 4)
    edges = []
    for group in range(4):
        first_turn, second_turn = (-2 * group) % 8, (6 - 2 * group) % 8
        upper = pltpu.roll(high, first_turn, 1) if first_turn else high
        lower = pltpu.roll(low, second_turn, 1) if second_turn else low
        edges.append(jnp.where(mask, upper, lower))
    narrow_edge = jnp.concatenate(edges, axis=0)
    wide0, narrow0 = tiles_of(loc, below, above, size_x, 0)
    wide1, narrow1 = tiles_of(loc, below, above, size_x, 1)
    wide = [
        [t[n * wide_rows : (n + 1) * wide_rows] for t in (wide0, wide1, wide_edge)] for n in range(WIDE)
    ]
    narrow = [
        [t[n * narrow_rows : (n + 1) * narrow_rows] for t in (narrow0, narrow1, narrow_edge)]
        for n in range(NARROW)
    ]
    return wide, narrow


def inject_kernel(grid_y, grid_z, size_x, size_y, recv_cells, recv_values, bound_cells, bound_force, out):
    bits_y, bits_z = grid_y.bit_length() - 1, grid_z.bit_length() - 1
    start_x = lax.axis_index("gx") * size_x
    start_y = lax.axis_index("gy") * size_y
    ring = (size_x + 4) * 24
    inner = size_x * size_y
    chunk = 512
    total = jnp.zeros((3 * (ring + inner), grid_z), jnp.float32)
    for cells_ref, values_ref, shift in ((recv_cells, recv_values, 0), (bound_cells, bound_force, bits_z)):
        for begin in range(0, cells_ref.shape[-1], chunk):
            cells = cells_ref[0:1, begin : begin + chunk]
            across = cells >> shift
            depth = cells & (grid_z - 1) if shift else jnp.zeros_like(cells)
            cell_x = (across >> bits_y) - start_x
            cell_y = (across & (grid_y - 1)) - start_y
            near = (cell_x >= -2) & (cell_x < size_x + 2) & (cell_y >= -2) & (cell_y < size_y + 2)
            wrapped = jnp.where(cell_y < 0, cell_y + 24, cell_y)
            ring_row = jnp.where(near, (cell_x + 2) * 24 + wrapped, -1)
            inside = (cell_x >= 0) & (cell_x < size_x) & (cell_y >= 0) & (cell_y < size_y)
            inner_row = jnp.where(inside, cell_x * size_y + cell_y, -1)
            ring_hit = lax.broadcasted_iota(jnp.int32, (ring, chunk), 0) == ring_row
            inner_hit = lax.broadcasted_iota(jnp.int32, (inner, chunk), 0) == inner_row
            columns = lax.broadcasted_iota(jnp.int32, (grid_z, chunk), 0) == depth
            columns = jnp.where(columns, 1.0, 0.0).astype(jnp.bfloat16)
            pieces = []
            parts = []
            for step in range(2):
                value = values_ref[step : step + 1, begin : begin + chunk]
                split = []
                for _ in range(3):
                    top = value.astype(jnp.bfloat16).astype(jnp.float32)
                    split.append(top)
                    value = value - top
                parts.append(split)
            for number in range(3):
                pieces.append(jnp.where(ring_hit, parts[0][number], 0.0).astype(jnp.bfloat16))
                pieces.append(jnp.where(inner_hit, parts[1][number], 0.0).astype(jnp.bfloat16))
            total = total + lax.dot_general(
                jnp.concatenate(pieces, axis=0),
                columns,
                (((1,), (1,)), ((), ())),
                preferred_element_type=jnp.float32,
            )
    rows = ring + inner
    out[...] = total[0:rows] + total[rows : 2 * rows] + total[2 * rows : 3 * rows]


def first_step_kernel(
    grid_y, source, loc, below, above, from_above, from_below, inject, p, q, grads, now, ahead, weights
):
    size_x, size_y = p.shape[0], p.shape[1]
    wide, narrow = unpack(loc, below, above, from_above, from_below)
    source_tiles, mix_tiles = wide[0], wide[1]
    products = [[wide[2 + a][i] * wide[2 + b][i] for i in range(3)] for a, b in PAIRS]
    p_base, q_base, p_weight, q_weight, speed, f0, f1 = narrow
    count = size_x + 4
    mid = slice(2, 2 + size_x)
    p_next = adjoint(products, source_tiles, count, 3, False)
    q_next = adjoint(products, mix_tiles, count, 3, True)
    ring = inject[0 : count * 24].reshape(count, 24, 128)
    p_next = [p_base[i] + p_next[i] + ring[:, 8 * i : 8 * i + 8] for i in range(3)]
    q_next = [q_base[i] + q_next[i] for i in range(3)]
    near = [[tile[2 : 2 + count] for tile in entry] for entry in products]
    inner = [[tile[mid] for tile in entry] for entry in near]
    bits_y = grid_y.bit_length() - 1
    source_x = (source[0] >> bits_y) - lax.axis_index("gx") * size_x
    source_y = (source[0] & (grid_y - 1)) - lax.axis_index("gy") * size_y
    images = [forward_image(inner, field, size_x) for field in (f0, f1)]
    shape = (size_x, 8, 128)
    offset_x = lax.broadcasted_iota(jnp.int32, shape, 0) - source_x
    for i in range(2):
        ys = slice(8 * i, 8 * i + 8)
        offset_y = lax.broadcasted_iota(jnp.int32, shape, 1) + (8 * i - source_y)
        squared = (offset_x * offset_x + offset_y * offset_y).astype(jnp.float32)
        taper = jnp.minimum(squared * (1.0 / float(TAPER * TAPER)), 1.0)
        scale = taper * (2.0 * speed[i][mid])
        image0, image1 = scale * images[0][i], scale * images[1][i]
        p_mid, q_mid = p_next[i][mid], q_next[i][mid]
        grads[0, :, ys, :] = p[:, ys, :] * image0 + p_mid * image1
        grads[1, :, ys, :] = q[:, ys, :] * image0 + q_mid * image1
        g0, g1 = f0[i][mid], f1[i][mid]
        grads[2, :, ys, :] = g0 * g0 + g1 * g1
        now[0, :, ys, :] = p_mid
        now[1, :, ys, :] = q_mid
    for i in range(3):
        ahead[0, i] = p_weight[i] * p_next[i] + q_weight[i] * q_next[i]
        ahead[1, i] = speed[i] * (p_next[i] + q_next[i])
        for number in range(6):
            weights[number, i] = near[number][i]


def second_step_kernel(now, ahead, weights, inject, p, q, p_out, q_out):
    size_x, size_y = p.shape[0], p.shape[1]
    products = [[weights[number, i] for i in range(3)] for number in range(6)]
    p_next = adjoint(products, [ahead[0, i] for i in range(3)], size_x, 2, False)
    q_next = adjoint(products, [ahead[1, i] for i in range(3)], size_x, 2, True)
    inner = inject[inject.shape[0] - size_x * size_y :].reshape(size_x, size_y, 128)
    for i in range(2):
        ys = slice(8 * i, 8 * i + 8)
        p_out[:, ys, :] = 2.0 * now[0, :, ys, :] - p[:, ys, :] + inner[:, ys] + p_next[i]
        q_out[:, ys, :] = 2.0 * now[1, :, ys, :] - q[:, ys, :] + q_next[i]


def both_ways(low, high, axis):
    count = lax.axis_size(axis)
    below = lax.ppermute(high, axis, [(i, i + 1) for i in range(count - 1)])
    above = lax.ppermute(low, axis, [(i + 1, i) for i in range(count - 1)])
    return below, above


def shot_sum(part):
    count = lax.axis_size("shot")
    if count != 4:
        return lax.psum(part, "shot")
    part = part + lax.ppermute(part, "shot", [(0, 1), (1, 0), (2, 3), (3, 2)])
    return part + lax.ppermute(part, "shot", [(0, 3), (3, 0), (1, 2), (2, 1)])


def body(
    p_adjoint,
    q_adjoint,
    p_previous,
    q_previous,
    forward_p,
    courant,
    epsilon,
    delta_field,
    tilt_angle,
    azimuth,
    receiver_cells,
    receiver_values,
    boundary_cells,
    boundary_force,
    source_cells,
):
    _, size_x, size_y, size_z = p_adjoint.shape
    grid_y = size_y * lax.axis_size("gy")
    p, q, p_old, q_old, f = (
        entry[0] for entry in (p_adjoint, q_adjoint, p_previous, q_previous, forward_p)
    )
    fields = WIDE + NARROW
    message = WIDE * size_x + NARROW * 2
    loc, low, high = call(
        prepare_kernel,
        [(fields * size_x, size_y, size_z)] + [(message, size_y, size_z)] * 2,
        (p, q, p_old, q_old, f, courant, epsilon, delta_field, tilt_angle, azimuth),
    )
    below, above = both_ways(low, high, "gx")
    rows = (size_x + 4) * 24 + size_x * size_y
    (inject,) = call(
        functools.partial(inject_kernel, grid_y, size_z, size_x, size_y),
        [(rows, size_z)],
        (receiver_cells, receiver_values[0], boundary_cells[None], boundary_force[0]),
        flops=800_000_000,
    )
    tiles = WIDE * 3 * size_x // 2 + NARROW * (size_x + 4) // 4
    down, up = call(pack_kernel, [(tiles, 8, size_z)] * 2, (loc, below, above))
    from_below, from_above = both_ways(down, up, "gy")
    count = size_x + 4
    grads, now, ahead, weights = call(
        functools.partial(first_step_kernel, grid_y),
        [
            (3, size_x, size_y, size_z),
            (2, size_x, size_y, size_z),
            (2, 3, count, 8, size_z),
            (6, 3, count, 8, size_z),
        ],
        (source_cells, loc, below, above, from_above, from_below, inject, p, q),
        smem=(0,),
    )
    total = shot_sum(grads)
    p_final, q_final = call(
        second_step_kernel, [(size_x, size_y, size_z)] * 2, (now, ahead, weights, inject, p, q)
    )
    scale = jnp.sqrt(total[2] + 1.0)
    return (p_final[None], q_final[None], total[0] / scale, total[1] / scale)


def solution(mesh):
    in_specs = (
        P("shot", "gx", "gy", None),
        P("shot", "gx", "gy", None),
        P("shot", "gx", "gy", None),
        P("shot", "gx", "gy", None),
        P("shot", None, "gx", "gy", None),
        P("gx", "gy", None),
        P("gx", "gy", None),
        P("gx", "gy", None),
        P("gx", "gy", None),
        P("gx", "gy", None),
        P("shot", None),
        P("shot", None, None),
        P(),
        P("shot", None, None),
        P("shot"),
    )
    out_specs = (
        P("shot", "gx", "gy", None),
        P("shot", "gx", "gy", None),
        P("gx", "gy", None),
        P("gx", "gy", None),
    )
    return jax.shard_map(body, mesh=mesh, in_specs=in_specs, out_specs=out_specs, check_vma=False)
```

time: 177 us -> 55.2 us (0.31)
  the two profiles are of different devices: /device:TPU:4 before, /device:TPU:16 now
where the time goes in v1:
time: 55.2 us; the launch traced here: 54.2 us
  starting transfers between devices  22 us (40%)
  waiting for transfers between devices  18.5 us (34%)
  local copies, waits for them, and re-layouts  7.68 us (14%)
  Pallas kernels  3.95 us (7%)
  between operations  1.45 us (3%)
  other arithmetic  0.67 us (1%)
    ppermute x2, starting transfers between devices, both_ways(): above = lax.ppermute(low, axis, [(i + 1, i) for i in range(count - 1)])  14.5 us
    unnamed x32, local copies, waits for them, and re-layouts  7.68 us
    ppermute x1, waiting for transfers between devices, shot_sum(): return part + lax.ppermute(part, 'shot', [(0, 3), (3, 0), (1, 2), (2, 1)])  5.82 us
    ppermute x1, waiting for transfers between devices, shot_sum(): part = part + lax.ppermute(part, 'shot', [(0, 1), (1, 0), (2, 3), (3, 2)])  5.48 us
    pallas_call x5, Pallas kernels, call(): pl.pallas_call(kernel, out_shape=shapes, in_specs=specs, out_specs=[pl.Bl...  3.95 us
    ppermute x2, waiting for transfers between devices, both_ways(): below = lax.ppermute(high, axis, [(i, i + 1) for i in range(count - 1)])  3.78 us
    ppermute x2, starting transfers between devices, both_ways(): below = lax.ppermute(high, axis, [(i, i + 1) for i in range(count - 1)])  3.68 us
    ppermute x2, waiting for transfers between devices, both_ways(): above = lax.ppermute(low, axis, [(i + 1, i) for i in range(count - 1)])  3.41 us
  transfers between devices with their start and end apart: 6, of which 4 were waited for; matrix products, arithmetic and copies ran while one was open for 0% of the time, Pallas kernels for 5%

profile of v1, /device:TPU:16, one launch (start us, length us, event | category | flops | bytes accessed | tf_op | source)
XLA Modules:
  0.0 54.2 jit_solution(8685375152804480315)
XLA Ops:
  0.6 0.0 copy-start
  0.6 0.7 %copy-done = f32[1,4,16,128]{3,2,1,0:T(8,128)S(1)} copy-done((f32[1,4,16,128]{3,2,1,0:T(8,128)S(1)}, f32[1,4,16,128]{3,2,1,0:T(8,128)}, u32[]{:S(2)}) %copy-start) | copy-done | bytes 32792
  1.4 0.0 copy-start.2
  1.4 0.8 %copy-done.2 = f32[1,4,16,128]{3,2,1,0:T(8,128)S(1)} copy-done((f32[1,4,16,128]{3,2,1,0:T(8,128)S(1)}, f32[1,4,16,128]{3,2,1,0:T(8,128)}, u32[]{:S(2)}) %copy-start.2) | copy-done | bytes 32792
  2.2 0.0 copy-start.4
  2.2 0.8 %copy-done.4 = f32[1,2,4,16,128]{4,3,2,1,0:T(8,128)S(1)} copy-done((f32[1,2,4,16,128]{4,3,2,1,0:T(8,128)S(1)}, f32[1,2,4,16,128]{4,3,2,1,0:T(8,128)}, u32[]{:S(2)}) %copy-start.4) | copy-done | bytes 65560
  3.0 0.0 copy-start.5
  3.0 0.8 %copy-done.5 = f32[1,4,16,128]{3,2,1,0:T(8,128)S(1)} copy-done((f32[1,4,16,128]{3,2,1,0:T(8,128)S(1)}, f32[1,4,16,128]{3,2,1,0:T(8,128)}, u32[]{:S(2)}) %copy-start.5) | copy-done | bytes 32792
  3.8 0.0 copy-start.6
  3.8 0.8 %copy-done.6 = f32[1,4,16,128]{3,2,1,0:T(8,128)S(1)} copy-done((f32[1,4,16,128]{3,2,1,0:T(8,128)S(1)}, f32[1,4,16,128]{3,2,1,0:T(8,128)}, u32[]{:S(2)}) %copy-start.6) | copy-done | bytes 32792
  4.5 0.0 copy-start.7
  4.5 0.8 %copy-done.7 = f32[4,16,128]{2,1,0:T(8,128)S(1)} copy-done((f32[4,16,128]{2,1,0:T(8,128)S(1)}, f32[4,16,128]{2,1,0:T(8,128)}, u32[]{:S(2)}) %copy-start.7) | copy-done | bytes 32792
  5.3 0.0 copy-start.8
  5.3 0.8 %copy-done.8 = f32[4,16,128]{2,1,0:T(8,128)S(1)} copy-done((f32[4,16,128]{2,1,0:T(8,128)S(1)}, f32[4,16,128]{2,1,0:T(8,128)}, u32[]{:S(2)}) %copy-start.8) | copy-done | bytes 32792
  6.0 0.0 copy-start.9
  6.0 0.8 %copy-done.9 = f32[4,16,128]{2,1,0:T(8,128)S(1)} copy-done((f32[4,16,128]{2,1,0:T(8,128)S(1)}, f32[4,16,128]{2,1,0:T(8,128)}, u32[]{:S(2)}) %copy-start.9) | copy-done | bytes 32792
  6.8 0.0 copy-start.10
  6.8 0.8 %copy-done.10 = f32[4,16,128]{2,1,0:T(8,128)S(1)} copy-done((f32[4,16,128]{2,1,0:T(8,128)S(1)}, f32[4,16,128]{2,1,0:T(8,128)}, u32[]{:S(2)}) %copy-start.10) | copy-done | bytes 32792
  7.5 0.0 copy-start.11
  7.5 0.8 %copy-done.11 = f32[4,16,128]{2,1,0:T(8,128)S(1)} copy-done((f32[4,16,128]{2,1,0:T(8,128)S(1)}, f32[4,16,128]{2,1,0:T(8,128)}, u32[]{:S(2)}) %copy-start.11) | copy-done | bytes 32792
  8.3 0.3 shard_map.174
  8.6 1.8 %collective-permute-start = (f32[34,16,128]{2,1,0:T(8,128)S(1)}, f32[34,16,128]{2,1,0:T(8,128)S(1)}, u32[]{:S(2)}, u32[]{:S(2)}) collective-permute-start(f32[34,16,128]{2,1,0:T(8,128)S(1)} %get-tuple-element.16), channel_id=1, source_target_pairs={{0,8},{8,16},{16,24},{24,32},{32,40},{40,48},{48,56},{56,64},{64,7... | collective-permute-start | bytes 835592 | tf_op jit(solution)/shard_map/ppermute | solution.py:348
  10.3 1.3 %collective-permute-start.1 = (f32[34,16,128]{2,1,0:T(8,128)S(1)}, f32[34,16,128]{2,1,0:T(8,128)S(1)}, u32[]{:S(2)}, u32[]{:S(2)}) collective-permute-start(f32[34,16,128]{2,1,0:T(8,128)S(1)} %get-tuple-element.17), channel_id=1, source_target_pairs={{8,0},{16,8},{24,16},{32,24},{40,32},{48,40},{56,48},{64,56},{72,6... | collective-permute-start | bytes 835592 | tf_op jit(solution)/shard_map/ppermute | solution.py:349
  11.6 0.0 collective-permute-done.below
  11.6 3.4 %collective-permute-done.1.above = f32[34,16,128]{2,1,0:T(8,128)S(1)} collective-permute-done((f32[34,16,128]{2,1,0:T(8,128)S(1)}, f32[34,16,128]{2,1,0:T(8,128)S(1)}, u32[]{:S(2)}, u32[]{:S(2)}) %collective-permute-start.1) | collective-permute-done | bytes 278560 | tf_op jit(solution)/shard_map/ppermute | solution.py:349
  15.0 0.0 copy-start.12
  15.1 0.1 shard_map.175
  15.1 0.0 copy-start.14
  15.1 13.2 %collective-permute-start.2 = (f32[44,8,128]{2,1,0:T(8,128)S(1)}, f32[44,8,128]{2,1,0:T(8,128)S(1)}, u32[]{:S(2)}, u32[]{:S(2)}) collective-permute-start(f32[44,8,128]{2,1,0:T(8,128)S(1)} %get-tuple-element.18), channel_id=1, source_target_pairs={{1,0},{2,1},{3,2},{4,3},{5,4},{6,5},{7,6},{9,8},{10,9},{11,10},{12... | collective-permute-start | bytes 540680 | tf_op jit(solution)/shard_map/ppermute | solution.py:349
  28.3 1.9 %collective-permute-start.3 = (f32[44,8,128]{2,1,0:T(8,128)S(1)}, f32[44,8,128]{2,1,0:T(8,128)S(1)}, u32[]{:S(2)}, u32[]{:S(2)}) collective-permute-start(f32[44,8,128]{2,1,0:T(8,128)S(1)} %get-tuple-element.19), channel_id=1, source_target_pairs={{0,1},{1,2},{2,3},{3,4},{4,5},{5,6},{6,7},{8,9},{9,10},{10,11},{11... | collective-permute-start | bytes 540680 | tf_op jit(solution)/shard_map/ppermute | solution.py:348
  30.9 0.0 copy-done.12
  30.9 0.0 copy-done.13
  30.9 0.0 copy-done.15
  30.9 0.0 copy-done.14
  30.9 0.0 copy-start.1
  30.9 0.0 copy-start.3
  31.0 1.8 %shard_map.176.inject = f32[256,128]{1,0:T(8,128)S(1)} custom-call(s32[1,2048]{1,0:T(1,128)S(1)} %copy-done.14, f32[2,2048]{1,0:T(2,128)S(1)} %bitcast.23, s32[1,2048]{1,0:T(1,128)S(1)} %bitcast.25, f32[2,2048]{1,0:T(2,128)S(1)} %bitcast.24), custom_call_target="tpu_custom_call" | custom-call | flops 800000000 | bytes 2000000 | tf_op jit(solution)/shard_map/pallas_call | solution.py:21
  32.7 0.0 collective-permute-done.2.from_above
  32.8 3.8 %collective-permute-done.3.from_below = f32[44,8,128]{2,1,0:T(8,128)S(1)} collective-permute-done((f32[44,8,128]{2,1,0:T(8,128)S(1)}, f32[44,8,128]{2,1,0:T(8,128)S(1)}, u32[]{:S(2)}, u32[]{:S(2)}) %collective-permute-start.3) | collective-permute-done | bytes 180256 | tf_op jit(solution)/shard_map/ppermute | solution.py:348
  36.5 0.0 copy-done.1
  36.5 0.0 copy-done.3
  36.5 1.0 %shard_map.177 = (f32[3,4,16,128]{3,2,1,0:T(8,128)S(1)}, f32[2,4,16,128]{3,2,1,0:T(8,128)S(1)}, f32[2,3,8,8,128]{4,3,2,1,0:T(8,128)S(1)}, f32[6,3,8,8,128]{4,3,2,1,0:T(8,128)S(1)}) custom-call(s32[1]{0:T(128)S(6)} %copy.19.source, f32[48,16,128]{2,1,0:T(8,128)S(1)} %get-tuple-element.15.loc, f32[34,16,128]{2,1,0:T(8,128)S(1)} %collective-permute-done.below, ...), custom_call_target="tpu_custom_call" | custom-call | flops 2000000 | bytes 2000000 | tf_op jit(solution)/shard_map/pallas_call | solution.py:21
  37.5 1.9 %collective-permute-start.4 = (f32[3,4,16,128]{3,2,1,0:T(8,128)S(1)}, f32[3,4,16,128]{3,2,1,0:T(8,128)S(1)}, u32[]{:S(2)}, u32[]{:S(2)}) collective-permute-start(f32[3,4,16,128]{3,2,1,0:T(8,128)S(1)} %get-tuple-element.25), channel_id=1, source_target_pairs={{0,256},{256,0},{512,768},{768,512},{1,257},{257,1},{513,769},{769... | collective-permute-start | bytes 294920 | tf_op jit(solution)/shard_map/ppermute | solution.py:357
  39.4 5.5 %collective-permute-done.4 = f32[3,4,16,128]{3,2,1,0:T(8,128)S(1)} collective-permute-done((f32[3,4,16,128]{3,2,1,0:T(8,128)S(1)}, f32[3,4,16,128]{3,2,1,0:T(8,128)S(1)}, u32[]{:S(2)}, u32[]{:S(2)}) %collective-permute-start.4) | collective-permute-done | bytes 98336 | tf_op jit(solution)/shard_map/ppermute | solution.py:357
  44.9 1.9 %collective-permute-start.5 = (f32[3,4,16,128]{3,2,1,0:T(8,128)S(1)}, f32[3,4,16,128]{3,2,1,0:T(8,128)S(1)}, u32[]{:S(2)}, u32[]{:S(2)}) collective-permute-start(f32[3,4,16,128]{3,2,1,0:T(8,128)S(1)} %add.13), channel_id=1, source_target_pairs={{0,768},{768,0},{256,512},{512,256},{1,769},{769,1},{257,513},{513... | collective-permute-start | bytes 294920 | tf_op jit(solution)/shard_map/ppermute | solution.py:358
  46.9 0.9 %shard_map.178 = (f32[4,16,128]{2,1,0:T(8,128)}, f32[4,16,128]{2,1,0:T(8,128)}) custom-call(f32[2,4,16,128]{3,2,1,0:T(8,128)S(1)} %get-tuple-element.20.now, f32[2,3,8,8,128]{4,3,2,1,0:T(8,128)S(1)} %get-tuple-element.21.ahead, f32[6,3,8,8,128]{4,3,2,1,0:T(8,128)S(1)} %get-tuple-element.22.weights, f32[256,128]{1,0:T(8,128)S(1)} %shard_map.176.inject, ...), custom_call_target="tpu_custom_call" | custom-call | flops 2000000 | bytes 2000000 | tf_op jit(solution)/shard_map/pallas_call | solution.py:21
  47.7 5.8 %collective-permute-done.5 = f32[3,4,16,128]{3,2,1,0:T(8,128)S(1)} collective-permute-done((f32[3,4,16,128]{3,2,1,0:T(8,128)S(1)}, f32[3,4,16,128]{3,2,1,0:T(8,128)S(1)}, u32[]{:S(2)}, u32[]{:S(2)}) %collective-permute-start.5) | collective-permute-done | bytes 98336 | tf_op jit(solution)/shard_map/ppermute | solution.py:358
  53.6 0.6 %fusion = (f32[4,16,128]{2,1,0:T(8,128)}, f32[4,16,128]{2,1,0:T(8,128)}) fusion(f32[3,4,16,128]{3,2,1,0:T(8,128)S(1)} %add.14), kind=kLoop, calls=%fused_computation.1 | loop fusion | flops 24576 | bytes 163840 | tf_op jit(solution)/shard_map/div | solution.py:418
  (4 shorter events, 0.0 us)
Async XLA Ops:
  0.6 0.8 %copy-start = (f32[1,4,16,128]{3,2,1,0:T(8,128)S(1)}, f32[1,4,16,128]{3,2,1,0:T(8,128)}, u32[]{:S(2)}) copy-start(f32[1,4,16,128]{3,2,1,0:T(8,128)} %param.15) | copy-start | bytes 98308
  1.4 0.8 %copy-start.2 = (f32[1,4,16,128]{3,2,1,0:T(8,128)S(1)}, f32[1,4,16,128]{3,2,1,0:T(8,128)}, u32[]{:S(2)}) copy-start(f32[1,4,16,128]{3,2,1,0:T(8,128)} %param.16) | copy-start | bytes 98308
  2.2 0.8 %copy-start.4 = (f32[1,2,4,16,128]{4,3,2,1,0:T(8,128)S(1)}, f32[1,2,4,16,128]{4,3,2,1,0:T(8,128)}, u32[]{:S(2)}) copy-start(f32[1,2,4,16,128]{4,3,2,1,0:T(8,128)} %param.19) | copy-start | bytes 196612
  3.0 0.8 %copy-start.5 = (f32[1,4,16,128]{3,2,1,0:T(8,128)S(1)}, f32[1,4,16,128]{3,2,1,0:T(8,128)}, u32[]{:S(2)}) copy-start(f32[1,4,16,128]{3,2,1,0:T(8,128)} %param.17) | copy-start | bytes 98308
  3.8 0.8 %copy-start.6 = (f32[1,4,16,128]{3,2,1,0:T(8,128)S(1)}, f32[1,4,16,128]{3,2,1,0:T(8,128)}, u32[]{:S(2)}) copy-start(f32[1,4,16,128]{3,2,1,0:T(8,128)} %param.18) | copy-start | bytes 98308
  4.5 0.8 %copy-start.7 = (f32[4,16,128]{2,1,0:T(8,128)S(1)}, f32[4,16,128]{2,1,0:T(8,128)}, u32[]{:S(2)}) copy-start(f32[4,16,128]{2,1,0:T(8,128)} %c.1) | copy-start | bytes 98308
  5.3 0.8 %copy-start.8 = (f32[4,16,128]{2,1,0:T(8,128)S(1)}, f32[4,16,128]{2,1,0:T(8,128)}, u32[]{:S(2)}) copy-start(f32[4,16,128]{2,1,0:T(8,128)} %eps.1) | copy-start | bytes 98308
  6.0 0.8 %copy-start.9 = (f32[4,16,128]{2,1,0:T(8,128)S(1)}, f32[4,16,128]{2,1,0:T(8,128)}, u32[]{:S(2)}) copy-start(f32[4,16,128]{2,1,0:T(8,128)} %delta.1) | copy-start | bytes 98308
  6.8 0.8 %copy-start.10 = (f32[4,16,128]{2,1,0:T(8,128)S(1)}, f32[4,16,128]{2,1,0:T(8,128)}, u32[]{:S(2)}) copy-start(f32[4,16,128]{2,1,0:T(8,128)} %tilt.1) | copy-start | bytes 98308
  7.5 0.8 %copy-start.11 = (f32[4,16,128]{2,1,0:T(8,128)S(1)}, f32[4,16,128]{2,1,0:T(8,128)}, u32[]{:S(2)}) copy-start(f32[4,16,128]{2,1,0:T(8,128)} %azimuth.1) | copy-start | bytes 98308
  8.6 3.1 %collective-permute-start = (f32[34,16,128]{2,1,0:T(8,128)S(1)}, f32[34,16,128]{2,1,0:T(8,128)S(1)}, u32[]{:S(2)}, u32[]{:S(2)}) collective-permute-start(f32[34,16,128]{2,1,0:T(8,128)S(1)} %get-tuple-element.16), channel_id=1, source_target_pairs={{0,8},{8,16},{16,24},{24,32},{32,40},{40,48},{48,56},{56,64},{64,7... | collective-permute-start | bytes 835592 | tf_op jit(solution)/shard_map/ppermute | solution.py:348
  10.3 4.7 %collective-permute-start.1 = (f32[34,16,128]{2,1,0:T(8,128)S(1)}, f32[34,16,128]{2,1,0:T(8,128)S(1)}, u32[]{:S(2)}, u32[]{:S(2)}) collective-permute-start(f32[34,16,128]{2,1,0:T(8,128)S(1)} %get-tuple-element.17), channel_id=1, source_target_pairs={{8,0},{16,8},{24,16},{32,24},{40,32},{48,40},{56,48},{64,56},{72,6... | collective-permute-start | bytes 835592 | tf_op jit(solution)/shard_map/ppermute | solution.py:349
  15.0 15.9 %copy-start.12 = (f32[1,2,2048]{2,1,0:T(2,128)S(1)}, f32[1,2,2048]{2,1,0:T(2,128)}, u32[]{:S(2)}) copy-start(f32[1,2,2048]{2,1,0:T(2,128)} %param.26) | copy-start | bytes 49156
  15.0 15.9 %copy-start.13 = (f32[1,2,2048]{2,1,0:T(2,128)S(1)}, f32[1,2,2048]{2,1,0:T(2,128)}, u32[]{:S(2)}) copy-start(f32[1,2,2048]{2,1,0:T(2,128)} %param.28) | copy-start | bytes 49156
  15.0 15.9 %copy-start.15 = (s32[2048]{0:T(1024)S(1)}, s32[2048]{0:T(1024)}, u32[]{:S(2)}) copy-start(s32[2048]{0:T(1024)} %param.27) | copy-start | bytes 24580
  15.1 15.8 %copy-start.14 = (s32[1,2048]{1,0:T(1,128)S(1)}, s32[1,2048]{1,0:T(1,128)}, u32[]{:S(2)}) copy-start(s32[1,2048]{1,0:T(1,128)} %recv_cells.1) | copy-start | bytes 24580
  15.1 17.6 %collective-permute-start.2 = (f32[44,8,128]{2,1,0:T(8,128)S(1)}, f32[44,8,128]{2,1,0:T(8,128)S(1)}, u32[]{:S(2)}, u32[]{:S(2)}) collective-permute-start(f32[44,8,128]{2,1,0:T(8,128)S(1)} %get-tuple-element.18), channel_id=1, source_target_pairs={{1,0},{2,1},{3,2},{4,3},{5,4},{6,5},{7,6},{9,8},{10,9},{11,10},{12... | collective-permute-start | bytes 540680 | tf_op jit(solution)/shard_map/ppermute | solution.py:349
  28.3 8.2 %collective-permute-start.3 = (f32[44,8,128]{2,1,0:T(8,128)S(1)}, f32[44,8,128]{2,1,0:T(8,128)S(1)}, u32[]{:S(2)}, u32[]{:S(2)}) collective-permute-start(f32[44,8,128]{2,1,0:T(8,128)S(1)} %get-tuple-element.19), channel_id=1, source_target_pairs={{0,1},{1,2},{2,3},{3,4},{4,5},{5,6},{6,7},{8,9},{9,10},{10,11},{11... | collective-permute-start | bytes 540680 | tf_op jit(solution)/shard_map/ppermute | solution.py:348
  30.9 5.6 %copy-start.1 = (f32[1,4,16,128]{3,2,1,0:T(8,128)S(1)}, f32[1,4,16,128]{3,2,1,0:T(8,128)}, u32[]{:S(2)}) copy-start(f32[1,4,16,128]{3,2,1,0:T(8,128)} %param.15) | copy-start | bytes 98308
  30.9 5.6 %copy-start.3 = (f32[1,4,16,128]{3,2,1,0:T(8,128)S(1)}, f32[1,4,16,128]{3,2,1,0:T(8,128)}, u32[]{:S(2)}) copy-start(f32[1,4,16,128]{3,2,1,0:T(8,128)} %param.16) | copy-start | bytes 98308
  37.5 7.4 %collective-permute-start.4 = (f32[3,4,16,128]{3,2,1,0:T(8,128)S(1)}, f32[3,4,16,128]{3,2,1,0:T(8,128)S(1)}, u32[]{:S(2)}, u32[]{:S(2)}) collective-permute-start(f32[3,4,16,128]{3,2,1,0:T(8,128)S(1)} %get-tuple-element.25), channel_id=1, source_target_pairs={{0,256},{256,0},{512,768},{768,512},{1,257},{257,1},{513,769},{769... | collective-permute-start | bytes 294920 | tf_op jit(solution)/shard_map/ppermute | solution.py:357
  44.9 8.6 %collective-permute-start.5 = (f32[3,4,16,128]{3,2,1,0:T(8,128)S(1)}, f32[3,4,16,128]{3,2,1,0:T(8,128)S(1)}, u32[]{:S(2)}, u32[]{:S(2)}) collective-permute-start(f32[3,4,16,128]{3,2,1,0:T(8,128)S(1)} %add.13), channel_id=1, source_target_pairs={{0,768},{768,0},{256,512},{512,256},{1,769},{769,1},{257,513},{513... | collective-permute-start | bytes 294920 | tf_op jit(solution)/shard_map/ppermute | solution.py:358

commit v2 on v1

--- a/solution.py
+++ b/solution.py
@@ -10,12 +10,14 @@
 TAPER = 32
 WIDE = 5
 NARROW = 7
+FIELDS = WIDE + NARROW + 2
+INPUTS = ("p", "q", "p_old", "q_old", "f", "c", "eps", "delta", "tilt", "azimuth")
 PAIRS = ((0, 0), (1, 1), (2, 2), (0, 1), (0, 2), (1, 2))
 
 
-def call(kernel, outs, args, scratch=(), smem=(), flops=2_000_000):
+def call(kernel, outs, args, scratch=(), smem=(), flops=2_000_000, space=pltpu.VMEM):
     specs = [
-        pl.BlockSpec(memory_space=pltpu.SMEM if i in smem else pltpu.VMEM) for i in range(len(args))
+        pl.BlockSpec(memory_space=pltpu.SMEM if i in smem else space) for i in range(len(args))
     ]
     shapes = [jax.ShapeDtypeStruct(shape, jnp.float32) for shape in outs]
     return pl.pallas_call(
@@ -26,7 +28,7 @@
         scratch_shapes=list(scratch),
         compiler_params=pltpu.CompilerParams(vmem_limit_bytes=24 * 1024 * 1024),
         cost_estimate=pl.CostEstimate(flops=flops, bytes_accessed=2_000_000, transcendentals=0),
-    )(*args)
+    )(*(pltpu.with_memory_space_constraint(x, space) if space == pltpu.HBM else x for x in args))
 
 
 def row_mask(shape, below):
@@ -135,7 +137,15 @@
     return out
 
 
-def prepare_kernel(p, q, p_old, q_old, f, c, eps, delta, tilt, azimuth, loc, low, high):
+def prepare_kernel(*refs):
+    count = len(INPUTS)
+    arrays, (loc, far, near), held, arrived = refs[:count], refs[count : count + 3], refs[-count - 1 : -1], refs[-1]
+    copies = [pltpu.make_async_copy(arrays[i], held[i], arrived.at[i]) for i in range(count)]
+    for copy in copies:
+        copy.start()
+    for copy in copies:
+        copy.wait()
+    p, q, p_old, q_old, f, c, eps, delta, tilt, azimuth = held
     size_x = p.shape[0]
     p_now, q_now, speed = p[...], q[...], c[...]
     p_weight = speed * (1.0 + 2.0 * eps[...])
@@ -160,56 +170,72 @@
     for number, cells in enumerate(wide):
         rows = slice(number * size_x, (number + 1) * size_x)
         loc[rows] = cells
-        low[rows] = cells
-        high[rows] = cells
-    for number, cells in enumerate(narrow):
+        near[rows] = cells
+        far[rows] = cells
+    for number, cells in enumerate(narrow + (p_now, q_now)):
         start = (WIDE + number) * size_x
         loc[start : start + size_x] = cells
+    odd = lax.rem(lax.axis_index("gx"), 2)
+    upper, lower = (1 - odd) * (size_x - 2), odd * (size_x - 2)
+    for number in range(NARROW):
+        start = (WIDE + number) * size_x
         begin = WIDE * size_x + 2 * number
-        low[begin : begin + 2] = cells[0:2]
-        high[begin : begin + 2] = cells[size_x - 2 : size_x]
-
-
-def tiles_of(loc, below, above, size_x, part):
+        near[begin : begin + 2] = loc[pl.ds(start + upper, 2)]
+        far[begin : begin + 2] = loc[pl.ds(start + lower, 2)]
+
+
+def tiles_of(loc, near, far, size_x, part):
     ys = slice(8 * part, 8 * part + 8)
+    odd = lax.rem(lax.axis_index("gx"), 2) == 1
+    first, second = near[:, ys, :], far[:, ys, :]
+    below, above = jnp.where(odd, first, second), jnp.where(odd, second, first)
     wide, narrow = [], []
     for number in range(WIDE):
         rows = slice(number * size_x, (number + 1) * size_x)
-        wide += [below[rows, ys, :], loc[rows, ys, :], above[rows, ys, :]]
+        wide += [below[rows], loc[rows, ys, :], above[rows]]
     for number in range(NARROW):
         start = (WIDE + number) * size_x
         begin = WIDE * size_x + 2 * number
         narrow += [
-            below[begin : begin + 2, ys, :],
+            below[begin : begin + 2],
             loc[start : start + size_x, ys, :],
-            above[begin : begin + 2, ys, :],
+            above[begin : begin + 2],
         ]
     return jnp.concatenate(wide, axis=0), jnp.concatenate(narrow, axis=0)
 
 
-def pack_kernel(loc, below, above, down, up):
-    size_x = loc.shape[0] // (WIDE + NARROW)
-    for part, target in ((0, down), (1, up)):
-        wide, narrow = tiles_of(loc, below, above, size_x, part)
+def pack_kernel(loc, far, near, evens, odds):
+    size_x = loc.shape[0] // FIELDS
+    made = []
+    for part in range(2):
+        wide, narrow = tiles_of(loc, near, far, size_x, part)
         half = wide.shape[0] // 2
         quarter = narrow.shape[0] // 4
         turned = pltpu.roll(wide, 4, 1)
         mask = row_mask((half, 8, 128), 4)
         if part == 0:
-            target[0:half] = jnp.where(mask, wide[:half], turned[half:])
+            top = jnp.where(mask, wide[:half], turned[half:])
         else:
-            target[0:half] = jnp.where(mask, turned[:half], wide[half:])
+            top = jnp.where(mask, turned[:half], wide[half:])
         out = None
         for group in range(4):
             rows = narrow[group * quarter : (group + 1) * quarter]
             turn = (2 * group - 6 * part) % 8
             rows = pltpu.roll(rows, turn, 1) if turn else rows
             out = rows if out is None else jnp.where(row_mask(rows.shape, 2 * group), out, rows)
-        target[half : half + quarter] = out
-
-
-def unpack(loc, below, above, from_above, from_below):
-    size_x = loc.shape[0] // (WIDE + NARROW)
+        made.append((top, out))
+    odd = lax.rem(lax.axis_index("gy"), 2) == 1
+    down, up = made
+    for rows, a, b in ((slice(0, half), down[0], up[0]), (slice(half, half + quarter), down[1], up[1])):
+        evens[rows] = jnp.where(odd, a, b)
+        odds[rows] = jnp.where(odd, b, a)
+
+
+def unpack(loc, near, far, evens, odds):
+    size_x = loc.shape[0] // FIELDS
+    odd = lax.rem(lax.axis_index("gy"), 2) == 1
+    from_above = jnp.where(odd, odds[...], evens[...])
+    from_below = jnp.where(odd, evens[...], odds[...])
     wide_rows, narrow_rows = 3 * size_x, size_x + 4
     half = WIDE * wide_rows // 2
     quarter = NARROW * narrow_rows // 4
@@ -228,8 +254,8 @@
         lower = pltpu.roll(low, second_turn, 1) if second_turn else low
         edges.append(jnp.where(mask, upper, lower))
     narrow_edge = jnp.concatenate(edges, axis=0)
-    wide0, narrow0 = tiles_of(loc, below, above, size_x, 0)
-    wide1, narrow1 = tiles_of(loc, below, above, size_x, 1)
+    wide0, narrow0 = tiles_of(loc, near, far, size_x, 0)
+    wide1, narrow1 = tiles_of(loc, near, far, size_x, 1)
     wide = [
         [t[n * wide_rows : (n + 1) * wide_rows] for t in (wide0, wide1, wide_edge)] for n in range(WIDE)
     ]
@@ -288,10 +314,12 @@
 
 
 def first_step_kernel(
-    grid_y, source, loc, below, above, from_above, from_below, inject, p, q, grads, now, ahead, weights
+    grid_y, source, loc, far_x, near_x, evens, odds, inject, grads, now, ahead, weights
 ):
-    size_x, size_y = p.shape[0], p.shape[1]
-    wide, narrow = unpack(loc, below, above, from_above, from_below)
+    size_x, size_y = loc.shape[0] // FIELDS, loc.shape[1]
+    wide, narrow = unpack(loc, near_x, far_x, evens, odds)
+    p = loc[(FIELDS - 2) * size_x : (FIELDS - 1) * size_x]
+    q = loc[(FIELDS - 1) * size_x : FIELDS * size_x]
     source_tiles, mix_tiles = wide[0], wide[1]
     products = [[wide[2 + a][i] * wide[2 + b][i] for i in range(3)] for a, b in PAIRS]
     p_base, q_base, p_weight, q_weight, speed, f0, f1 = narrow
@@ -331,8 +359,10 @@
             weights[number, i] = near[number][i]
 
 
-def second_step_kernel(now, ahead, weights, inject, p, q, p_out, q_out):
-    size_x, size_y = p.shape[0], p.shape[1]
+def second_step_kernel(now, ahead, weights, inject, loc, p_out, q_out):
+    size_x, size_y = p_out.shape[0], p_out.shape[1]
+    p = loc[(FIELDS - 2) * size_x : (FIELDS - 1) * size_x]
+    q = loc[(FIELDS - 1) * size_x : FIELDS * size_x]
     products = [[weights[number, i] for i in range(3)] for number in range(6)]
     p_next = adjoint(products, [ahead[0, i] for i in range(3)], size_x, 2, False)
     q_next = adjoint(products, [ahead[1, i] for i in range(3)], size_x, 2, True)
@@ -343,11 +373,9 @@
         q_out[:, ys, :] = 2.0 * now[1, :, ys, :] - q[:, ys, :] + q_next[i]
 
 
-def both_ways(low, high, axis):
-    count = lax.axis_size(axis)
-    below = lax.ppermute(high, axis, [(i, i + 1) for i in range(count - 1)])
-    above = lax.ppermute(low, axis, [(i + 1, i) for i in range(count - 1)])
-    return below, above
+def swap(part, axis, start):
+    lows = range(start, lax.axis_size(axis) - 1, 2)
+    return lax.ppermute(part, axis, [(i, i + 1) for i in lows] + [(i + 1, i) for i in lows])
 
 
 def shot_sum(part):
@@ -380,14 +408,18 @@
     p, q, p_old, q_old, f = (
         entry[0] for entry in (p_adjoint, q_adjoint, p_previous, q_previous, forward_p)
     )
-    fields = WIDE + NARROW
     message = WIDE * size_x + NARROW * 2
-    loc, low, high = call(
+    inputs = (p, q, p_old, q_old, f, courant, epsilon, delta_field, tilt_angle, azimuth)
+    loc, far, near = call(
         prepare_kernel,
-        [(fields * size_x, size_y, size_z)] + [(message, size_y, size_z)] * 2,
-        (p, q, p_old, q_old, f, courant, epsilon, delta_field, tilt_angle, azimuth),
-    )
-    below, above = both_ways(low, high, "gx")
+        [(FIELDS * size_x, size_y, size_z)] + [(message, size_y, size_z)] * 2,
+        inputs,
+        scratch=[pltpu.VMEM(entry.shape, entry.dtype) for entry in inputs]
+        + [pltpu.SemaphoreType.DMA((len(inputs),))],
+        space=pltpu.HBM,
+    )
+    far = swap(far, "gx", 1)
+    near = swap(near, "gx", 0)
     rows = (size_x + 4) * 24 + size_x * size_y
     (inject,) = call(
         functools.partial(inject_kernel, grid_y, size_z, size_x, size_y),
@@ -396,8 +428,9 @@
         flops=800_000_000,
     )
     tiles = WIDE * 3 * size_x // 2 + NARROW * (size_x + 4) // 4
-    down, up = call(pack_kernel, [(tiles, 8, size_z)] * 2, (loc, below, above))
-    from_below, from_above = both_ways(down, up, "gy")
+    evens, odds = call(pack_kernel, [(tiles, 8, size_z)] * 2, (loc, far, near))
+    evens = swap(evens, "gy", 0)
+    odds = swap(odds, "gy", 1)
     count = size_x + 4
     grads, now, ahead, weights = call(
         functools.partial(first_step_kernel, grid_y),
@@ -407,12 +440,12 @@
             (2, 3, count, 8, size_z),
             (6, 3, count, 8, size_z),
         ],
-        (source_cells, loc, below, above, from_above, from_below, inject, p, q),
+        (source_cells, loc, far, near, evens, odds, inject),
         smem=(0,),
     )
     total = shot_sum(grads)
     p_final, q_final = call(
-        second_step_kernel, [(size_x, size_y, size_z)] * 2, (now, ahead, weights, inject, p, q)
+        second_step_kernel, [(size_x, size_y, size_z)] * 2, (now, ahead, weights, inject, loc)
     )
     scale = jnp.sqrt(total[2] + 1.0)
     return (p_final[None], q_final[None], total[0] / scale, total[1] / scale)

time: 55.2 us -> 47.4 us (0.86); the launches traced: 54.2 us -> 47 us
  local copies, waits for them, and re-layouts: 7.68 us -> 0.02 us
  waiting for transfers between devices: 18.5 us -> 16.3 us
  starting transfers between devices: 22 us -> 23.6 us
  Pallas kernels: 3.95 us -> 5.04 us
    unnamed x32 -> x8, local copies, waits for them, and re-layouts: 7.68 us -> 0.02 us
    ppermute x4, waiting for transfers between devices: 7.18 us -> 4.96 us  [swap(): lax.ppermute(part, axis, [(i, i + 1) for i in lows] + [(i + 1, i) for i i...]
    ppermute x4, starting transfers between devices: 18.2 us -> 19.8 us  [swap(): lax.ppermute(part, axis, [(i, i + 1) for i in lows] + [(i + 1, i) for i i...]
    pallas_call x5, Pallas kernels: 3.95 us -> 5.04 us  [call(): pl.pallas_call(kernel, out_shape=shapes, in_specs=specs, out_specs=[pl.Bl...]
  transfers between devices with their start and end apart: 6 -> 6, of which waited for: 4 -> 5; matrix products, arithmetic and copies ran while one was open for 0% -> 0% of each run, Pallas kernels for 5% -> 6%
where the time goes in v2:
time: 47.4 us; the launch traced here: 47 us
  starting transfers between devices  23.6 us (50%)
  waiting for transfers between devices  16.3 us (34%)
  Pallas kernels  5.04 us (11%)
  between operations  1.41 us (3%)
  other arithmetic  0.67 us (1%)
    ppermute x4, starting transfers between devices, swap(): lax.ppermute(part, axis, [(i, i + 1) for i in lows] + [(i + 1, i) for i i...  19.8 us
    ppermute x1, waiting for transfers between devices, shot_sum(): return part + lax.ppermute(part, 'shot', [(0, 3), (3, 0), (1, 2), (2, 1)])  5.82 us
    ppermute x1, waiting for transfers between devices, shot_sum(): part = part + lax.ppermute(part, 'shot', [(0, 1), (1, 0), (2, 3), (3, 2)])  5.48 us
    pallas_call x5, Pallas kernels, call(): pl.pallas_call(kernel, out_shape=shapes, in_specs=specs, out_specs=[pl.Bl...  5.04 us
    ppermute x4, waiting for transfers between devices, swap(): lax.ppermute(part, axis, [(i, i + 1) for i in lows] + [(i + 1, i) for i i...  4.96 us
    ppermute x1, starting transfers between devices, shot_sum(): return part + lax.ppermute(part, 'shot', [(0, 3), (3, 0), (1, 2), (2, 1)])  1.92 us
    ppermute x1, starting transfers between devices, shot_sum(): part = part + lax.ppermute(part, 'shot', [(0, 1), (1, 0), (2, 3), (3, 2)])  1.92 us
  transfers between devices with their start and end apart: 6, of which 5 were waited for; matrix products, arithmetic and copies ran while one was open for 0% of the time, Pallas kernels for 6%

profile of v2, /device:TPU:16, one launch (start us, length us, event | category | flops | bytes accessed | tf_op | source)
XLA Modules:
  0.0 47.0 jit_solution(5943724489193886998)
XLA Ops:
  0.6 1.3 %shard_map.174 = (f32[56,16,128]{2,1,0:T(8,128)S(1)}, f32[34,16,128]{2,1,0:T(8,128)S(1)}, f32[34,16,128]{2,1,0:T(8,128)S(1)}) custom-call(f32[4,16,128]{2,1,0:T(8,128)} %bitcast.18, f32[4,16,128]{2,1,0:T(8,128)} %bitcast.19, f32[4,16,128]{2,1,0:T(8,128)} %bitcast.20, f32[4,16,128]{2,1,0:T(8,128)} %bitcast.21, f32[2,4,16,128]{3,2,1,0:T(8,128)} %bitcast.17, ...), custom_call_target="tpu_custom_call" | custom-call | flops 2000000 | bytes 2000000 | tf_op jit(solution)/shard_map/pallas_call | solution.py:23
  1.9 0.7 %collective-permute-start = (f32[34,16,128]{2,1,0:T(8,128)S(1)}, f32[34,16,128]{2,1,0:T(8,128)S(1)}, u32[]{:S(2)}, u32[]{:S(2)}) collective-permute-start(f32[34,16,128]{2,1,0:T(8,128)S(1)} %get-tuple-element.16), channel_id=1, source_target_pairs={{8,16},{24,32},{40,48},{56,64},{72,80},{88,96},{104,112},{120,128}... | collective-permute-start | bytes 835592 | tf_op jit(solution)/shard_map/ppermute | solution.py:378
  2.6 4.7 %collective-permute-start.1 = (f32[34,16,128]{2,1,0:T(8,128)S(1)}, f32[34,16,128]{2,1,0:T(8,128)S(1)}, u32[]{:S(2)}, u32[]{:S(2)}) collective-permute-start(f32[34,16,128]{2,1,0:T(8,128)S(1)} %get-tuple-element.17), channel_id=1, source_target_pairs={{0,8},{16,24},{32,40},{48,56},{64,72},{80,88},{96,104},{112,120},{... | collective-permute-start | bytes 835592 | tf_op jit(solution)/shard_map/ppermute | solution.py:378
  7.4 0.0 collective-permute-done.far.far_x
  7.4 1.2 %collective-permute-done.1.near.near_x = f32[34,16,128]{2,1,0:T(8,128)S(1)} collective-permute-done((f32[34,16,128]{2,1,0:T(8,128)S(1)}, f32[34,16,128]{2,1,0:T(8,128)S(1)}, u32[]{:S(2)}, u32[]{:S(2)}) %collective-permute-start.1) | collective-permute-done | bytes 278560 | tf_op jit(solution)/shard_map/ppermute | solution.py:378
  8.5 0.0 copy-start
  8.5 0.0 copy-start.1
  8.5 0.0 copy-start.3
  8.5 0.1 shard_map.175
  8.6 0.0 copy-start.2
  8.6 12.4 %collective-permute-start.2 = (f32[44,8,128]{2,1,0:T(8,128)S(1)}, f32[44,8,128]{2,1,0:T(8,128)S(1)}, u32[]{:S(2)}, u32[]{:S(2)}) collective-permute-start(f32[44,8,128]{2,1,0:T(8,128)S(1)} %get-tuple-element.18), channel_id=1, source_target_pairs={{0,1},{2,3},{4,5},{6,7},{1,0},{3,2},{5,4},{7,6},{8,9},{10,11},{12,... | collective-permute-start | bytes 540680 | tf_op jit(solution)/shard_map/ppermute | solution.py:378
  21.1 1.9 %collective-permute-start.3 = (f32[44,8,128]{2,1,0:T(8,128)S(1)}, f32[44,8,128]{2,1,0:T(8,128)S(1)}, u32[]{:S(2)}, u32[]{:S(2)}) collective-permute-start(f32[44,8,128]{2,1,0:T(8,128)S(1)} %get-tuple-element.19), channel_id=1, source_target_pairs={{1,2},{3,4},{5,6},{2,1},{4,3},{6,5},{9,10},{11,12},{13,14},{10,9},... | collective-permute-start | bytes 540680 | tf_op jit(solution)/shard_map/ppermute | solution.py:378
  23.7 0.0 copy-done
  23.7 0.0 copy-done.1
  23.7 0.0 copy-done.3
  23.7 0.0 copy-done.2
  23.7 1.8 %shard_map.176.inject = f32[256,128]{1,0:T(8,128)S(1)} custom-call(s32[1,2048]{1,0:T(1,128)S(1)} %copy-done.2, f32[2,2048]{1,0:T(2,128)S(1)} %bitcast.14, s32[1,2048]{1,0:T(1,128)S(1)} %bitcast.16, f32[2,2048]{1,0:T(2,128)S(1)} %bitcast.15), custom_call_target="tpu_custom_call" | custom-call | flops 800000000 | bytes 2000000 | tf_op jit(solution)/shard_map/pallas_call | solution.py:23
  25.5 0.4 collective-permute-done.2.evens
  25.9 3.4 %collective-permute-done.3.odds = f32[44,8,128]{2,1,0:T(8,128)S(1)} collective-permute-done((f32[44,8,128]{2,1,0:T(8,128)S(1)}, f32[44,8,128]{2,1,0:T(8,128)S(1)}, u32[]{:S(2)}, u32[]{:S(2)}) %collective-permute-start.3) | collective-permute-done | bytes 180256 | tf_op jit(solution)/shard_map/ppermute | solution.py:378
  29.3 1.0 %shard_map.177 = (f32[3,4,16,128]{3,2,1,0:T(8,128)S(1)}, f32[2,4,16,128]{3,2,1,0:T(8,128)S(1)}, f32[2,3,8,8,128]{4,3,2,1,0:T(8,128)S(1)}, f32[6,3,8,8,128]{4,3,2,1,0:T(8,128)S(1)}) custom-call(s32[1]{0:T(128)S(6)} %copy.19.source, f32[56,16,128]{2,1,0:T(8,128)S(1)} %get-tuple-element.15.loc, f32[34,16,128]{2,1,0:T(8,128)S(1)} %collective-permute-done.far.far_x, ...), custom_call_target="tpu_custom_call" | custom-call | flops 2000000 | bytes 2000000 | tf_op jit(solution)/shard_map/pallas_call | solution.py:23
  30.3 1.9 %collective-permute-start.4 = (f32[3,4,16,128]{3,2,1,0:T(8,128)S(1)}, f32[3,4,16,128]{3,2,1,0:T(8,128)S(1)}, u32[]{:S(2)}, u32[]{:S(2)}) collective-permute-start(f32[3,4,16,128]{3,2,1,0:T(8,128)S(1)} %get-tuple-element.25), channel_id=1, source_target_pairs={{0,256},{256,0},{512,768},{768,512},{1,257},{257,1},{513,769},{769... | collective-permute-start | bytes 294920 | tf_op jit(solution)/shard_map/ppermute | solution.py:385
  32.2 5.5 %collective-permute-done.4 = f32[3,4,16,128]{3,2,1,0:T(8,128)S(1)} collective-permute-done((f32[3,4,16,128]{3,2,1,0:T(8,128)S(1)}, f32[3,4,16,128]{3,2,1,0:T(8,128)S(1)}, u32[]{:S(2)}, u32[]{:S(2)}) %collective-permute-start.4) | collective-permute-done | bytes 98336 | tf_op jit(solution)/shard_map/ppermute | solution.py:385
  37.7 1.9 %collective-permute-start.5 = (f32[3,4,16,128]{3,2,1,0:T(8,128)S(1)}, f32[3,4,16,128]{3,2,1,0:T(8,128)S(1)}, u32[]{:S(2)}, u32[]{:S(2)}) collective-permute-start(f32[3,4,16,128]{3,2,1,0:T(8,128)S(1)} %add.13), channel_id=1, source_target_pairs={{0,768},{768,0},{256,512},{512,256},{1,769},{769,1},{257,513},{513... | collective-permute-start | bytes 294920 | tf_op jit(solution)/shard_map/ppermute | solution.py:386
  39.7 0.9 %shard_map.178 = (f32[4,16,128]{2,1,0:T(8,128)}, f32[4,16,128]{2,1,0:T(8,128)}) custom-call(f32[2,4,16,128]{3,2,1,0:T(8,128)S(1)} %get-tuple-element.20.now, f32[2,3,8,8,128]{4,3,2,1,0:T(8,128)S(1)} %get-tuple-element.21.ahead, f32[6,3,8,8,128]{4,3,2,1,0:T(8,128)S(1)} %get-tuple-element.22.weights, f32[256,128]{1,0:T(8,128)S(1)} %shard_map.176.inject, ...), custom_call_target="tpu_custom_call" | custom-call | flops 2000000 | bytes 2000000 | tf_op jit(solution)/shard_map/pallas_call | solution.py:23
  40.5 5.8 %collective-permute-done.5 = f32[3,4,16,128]{3,2,1,0:T(8,128)S(1)} collective-permute-done((f32[3,4,16,128]{3,2,1,0:T(8,128)S(1)}, f32[3,4,16,128]{3,2,1,0:T(8,128)S(1)}, u32[]{:S(2)}, u32[]{:S(2)}) %collective-permute-start.5) | collective-permute-done | bytes 98336 | tf_op jit(solution)/shard_map/ppermute | solution.py:386
  46.4 0.6 %fusion = (f32[4,16,128]{2,1,0:T(8,128)}, f32[4,16,128]{2,1,0:T(8,128)}) fusion(f32[3,4,16,128]{3,2,1,0:T(8,128)S(1)} %add.14), kind=kLoop, calls=%fused_computation.1 | loop fusion | flops 24576 | bytes 163840 | tf_op jit(solution)/shard_map/div | solution.py:451
  (2 shorter events, 0.0 us)
Async XLA Ops:
  1.9 5.4 %collective-permute-start = (f32[34,16,128]{2,1,0:T(8,128)S(1)}, f32[34,16,128]{2,1,0:T(8,128)S(1)}, u32[]{:S(2)}, u32[]{:S(2)}) collective-permute-start(f32[34,16,128]{2,1,0:T(8,128)S(1)} %get-tuple-element.16), channel_id=1, source_target_pairs={{8,16},{24,32},{40,48},{56,64},{72,80},{88,96},{104,112},{120,128}... | collective-permute-start | bytes 835592 | tf_op jit(solution)/shard_map/ppermute | solution.py:378
  2.6 5.9 %collective-permute-start.1 = (f32[34,16,128]{2,1,0:T(8,128)S(1)}, f32[34,16,128]{2,1,0:T(8,128)S(1)}, u32[]{:S(2)}, u32[]{:S(2)}) collective-permute-start(f32[34,16,128]{2,1,0:T(8,128)S(1)} %get-tuple-element.17), channel_id=1, source_target_pairs={{0,8},{16,24},{32,40},{48,56},{64,72},{80,88},{96,104},{112,120},{... | collective-permute-start | bytes 835592 | tf_op jit(solution)/shard_map/ppermute | solution.py:378
  8.5 15.1 %copy-start = (f32[1,2,2048]{2,1,0:T(2,128)S(1)}, f32[1,2,2048]{2,1,0:T(2,128)}, u32[]{:S(2)}) copy-start(f32[1,2,2048]{2,1,0:T(2,128)} %param.26) | copy-start | bytes 49156
  8.5 15.1 %copy-start.1 = (f32[1,2,2048]{2,1,0:T(2,128)S(1)}, f32[1,2,2048]{2,1,0:T(2,128)}, u32[]{:S(2)}) copy-start(f32[1,2,2048]{2,1,0:T(2,128)} %param.28) | copy-start | bytes 49156
  8.5 15.1 %copy-start.3 = (s32[2048]{0:T(1024)S(1)}, s32[2048]{0:T(1024)}, u32[]{:S(2)}) copy-start(s32[2048]{0:T(1024)} %param.27) | copy-start | bytes 24580
  8.6 15.1 %copy-start.2 = (s32[1,2048]{1,0:T(1,128)S(1)}, s32[1,2048]{1,0:T(1,128)}, u32[]{:S(2)}) copy-start(s32[1,2048]{1,0:T(1,128)} %recv_cells.1) | copy-start | bytes 24580
  8.6 17.3 %collective-permute-start.2 = (f32[44,8,128]{2,1,0:T(8,128)S(1)}, f32[44,8,128]{2,1,0:T(8,128)S(1)}, u32[]{:S(2)}, u32[]{:S(2)}) collective-permute-start(f32[44,8,128]{2,1,0:T(8,128)S(1)} %get-tuple-element.18), channel_id=1, source_target_pairs={{0,1},{2,3},{4,5},{6,7},{1,0},{3,2},{5,4},{7,6},{8,9},{10,11},{12,... | collective-permute-start | bytes 540680 | tf_op jit(solution)/shard_map/ppermute | solution.py:378
  21.1 8.2 %collective-permute-start.3 = (f32[44,8,128]{2,1,0:T(8,128)S(1)}, f32[44,8,128]{2,1,0:T(8,128)S(1)}, u32[]{:S(2)}, u32[]{:S(2)}) collective-permute-start(f32[44,8,128]{2,1,0:T(8,128)S(1)} %get-tuple-element.19), channel_id=1, source_target_pairs={{1,2},{3,4},{5,6},{2,1},{4,3},{6,5},{9,10},{11,12},{13,14},{10,9},... | collective-permute-start | bytes 540680 | tf_op jit(solution)/shard_map/ppermute | solution.py:378
  30.3 7.4 %collective-permute-start.4 = (f32[3,4,16,128]{3,2,1,0:T(8,128)S(1)}, f32[3,4,16,128]{3,2,1,0:T(8,128)S(1)}, u32[]{:S(2)}, u32[]{:S(2)}) collective-permute-start(f32[3,4,16,128]{3,2,1,0:T(8,128)S(1)} %get-tuple-element.25), channel_id=1, source_target_pairs={{0,256},{256,0},{512,768},{768,512},{1,257},{257,1},{513,769},{769... | collective-permute-start | bytes 294920 | tf_op jit(solution)/shard_map/ppermute | solution.py:385
  37.7 8.6 %collective-permute-start.5 = (f32[3,4,16,128]{3,2,1,0:T(8,128)S(1)}, f32[3,4,16,128]{3,2,1,0:T(8,128)S(1)}, u32[]{:S(2)}, u32[]{:S(2)}) collective-permute-start(f32[3,4,16,128]{3,2,1,0:T(8,128)S(1)} %add.13), channel_id=1, source_target_pairs={{0,768},{768,0},{256,512},{512,256},{1,769},{769,1},{257,513},{513... | collective-permute-start | bytes 294920 | tf_op jit(solution)/shard_map/ppermute | solution.py:386

commit v3 on v2

--- a/solution.py
+++ b/solution.py
@@ -204,7 +204,7 @@
     return jnp.concatenate(wide, axis=0), jnp.concatenate(narrow, axis=0)
 
 
-def pack_kernel(loc, far, near, evens, odds):
+def pack_kernel(loc, far, near, odds, evens):
     size_x = loc.shape[0] // FIELDS
     made = []
     for part in range(2):
@@ -314,7 +314,7 @@
 
 
 def first_step_kernel(
-    grid_y, source, loc, far_x, near_x, evens, odds, inject, grads, now, ahead, weights
+    grid_y, source, loc, far_x, near_x, odds, evens, inject, grads, now, ahead, weights
 ):
     size_x, size_y = loc.shape[0] // FIELDS, loc.shape[1]
     wide, narrow = unpack(loc, near_x, far_x, evens, odds)
@@ -378,12 +378,11 @@
     return lax.ppermute(part, axis, [(i, i + 1) for i in lows] + [(i + 1, i) for i in lows])
 
 
-def shot_sum(part):
-    count = lax.axis_size("shot")
-    if count != 4:
-        return lax.psum(part, "shot")
-    part = part + lax.ppermute(part, "shot", [(0, 1), (1, 0), (2, 3), (3, 2)])
-    return part + lax.ppermute(part, "shot", [(0, 3), (3, 0), (1, 2), (2, 1)])
+def finish_kernel(own, across, beside, around, grad_e, grad_d):
+    total = [(own[i] + beside[i]) + (around[i] + across[i]) for i in range(3)]
+    scale = 1.0 / jnp.sqrt(total[2] + 1.0)
+    grad_e[...] = total[0] * scale
+    grad_d[...] = total[1] * scale
 
 
 def body(
@@ -428,9 +427,9 @@
         flops=800_000_000,
     )
     tiles = WIDE * 3 * size_x // 2 + NARROW * (size_x + 4) // 4
-    evens, odds = call(pack_kernel, [(tiles, 8, size_z)] * 2, (loc, far, near))
+    odds, evens = call(pack_kernel, [(tiles, 8, size_z)] * 2, (loc, far, near))
+    odds = swap(odds, "gy", 1)
     evens = swap(evens, "gy", 0)
-    odds = swap(odds, "gy", 1)
     count = size_x + 4
     grads, now, ahead, weights = call(
         functools.partial(first_step_kernel, grid_y),
@@ -440,15 +439,18 @@
             (2, 3, count, 8, size_z),
             (6, 3, count, 8, size_z),
         ],
-        (source_cells, loc, far, near, evens, odds, inject),
+        (source_cells, loc, far, near, odds, evens, inject),
         smem=(0,),
     )
-    total = shot_sum(grads)
+    shots = range(lax.axis_size("shot"))
+    parts = [
+        lax.ppermute(grads, "shot", [(i, i ^ turn) for i in shots]) for turn in (2, 1, 3)
+    ]
     p_final, q_final = call(
         second_step_kernel, [(size_x, size_y, size_z)] * 2, (now, ahead, weights, inject, loc)
     )
-    scale = jnp.sqrt(total[2] + 1.0)
-    return (p_final[None], q_final[None], total[0] / scale, total[1] / scale)
+    grad_e, grad_d = call(finish_kernel, [(size_x, size_y, size_z)] * 2, (grads, *parts))
+    return (p_final[None], q_final[None], grad_e, grad_d)
 
 
 def solution(mesh):

time: 47.4 us -> 50.1 us (1.057)
  the two profiles are of different devices: /device:TPU:16 before, /device:TPU:562 now
where the time goes in v3:
time: 50.1 us; the launch traced here: 49.7 us
  starting transfers between devices  25.2 us (50%)
  waiting for transfers between devices  17.4 us (35%)
  Pallas kernels  5.7 us (11%)
  between operations  1.41 us (3%)
    ppermute x4, starting transfers between devices, swap(): lax.ppermute(part, axis, [(i, i + 1) for i in lows] + [(i + 1, i) for i i...  13 us
    ppermute x3, starting transfers between devices, body(): lax.ppermute(grads, 'shot', [(i, i ^ turn) for i in shots])  12.2 us
    ppermute x3, waiting for transfers between devices, body(): lax.ppermute(grads, 'shot', [(i, i ^ turn) for i in shots])  9.38 us
    ppermute x4, waiting for transfers between devices, swap(): lax.ppermute(part, axis, [(i, i + 1) for i in lows] + [(i + 1, i) for i i...  7.99 us
    pallas_call x6, Pallas kernels, call(): pl.pallas_call(kernel, out_shape=shapes, in_specs=specs, out_specs=[pl.Bl...  5.7 us
  transfers between devices with their start and end apart: 7, of which 5 were waited for; matrix products, arithmetic and copies ran while one was open for 0% of the time, Pallas kernels for 5%

profile of v3, /device:TPU:562, one launch (start us, length us, event | category | flops | bytes accessed | tf_op | source)
XLA Modules:
  0.0 49.7 jit_solution(14621729423309620860)
XLA Ops:
  0.6 1.3 %shard_map.174 = (f32[56,16,128]{2,1,0:T(8,128)S(1)}, f32[34,16,128]{2,1,0:T(8,128)S(1)}, f32[34,16,128]{2,1,0:T(8,128)S(1)}) custom-call(f32[4,16,128]{2,1,0:T(8,128)} %bitcast.14, f32[4,16,128]{2,1,0:T(8,128)} %bitcast.15, f32[4,16,128]{2,1,0:T(8,128)} %bitcast.16, f32[4,16,128]{2,1,0:T(8,128)} %bitcast.17, f32[2,4,16,128]{3,2,1,0:T(8,128)} %bitcast.13, ...), custom_call_target="tpu_custom_call" | custom-call | flops 2000000 | bytes 2000000 | tf_op jit(solution)/shard_map/pallas_call | solution.py:23
  1.9 1.9 %collective-permute-start = (f32[34,16,128]{2,1,0:T(8,128)S(1)}, f32[34,16,128]{2,1,0:T(8,128)S(1)}, u32[]{:S(2)}, u32[]{:S(2)}) collective-permute-start(f32[34,16,128]{2,1,0:T(8,128)S(1)} %get-tuple-element.18), channel_id=1, source_target_pairs={{8,16},{24,32},{40,48},{56,64},{72,80},{88,96},{104,112},{120,128}... | collective-permute-start | bytes 835592 | tf_op jit(solution)/shard_map/ppermute | solution.py:378
  3.9 4.4 %collective-permute-start.1 = (f32[34,16,128]{2,1,0:T(8,128)S(1)}, f32[34,16,128]{2,1,0:T(8,128)S(1)}, u32[]{:S(2)}, u32[]{:S(2)}) collective-permute-start(f32[34,16,128]{2,1,0:T(8,128)S(1)} %get-tuple-element.19), channel_id=1, source_target_pairs={{0,8},{16,24},{32,40},{48,56},{64,72},{80,88},{96,104},{112,120},{... | collective-permute-start | bytes 835592 | tf_op jit(solution)/shard_map/ppermute | solution.py:378
  8.2 3.6 %collective-permute-done.far.far_x = f32[34,16,128]{2,1,0:T(8,128)S(1)} collective-permute-done((f32[34,16,128]{2,1,0:T(8,128)S(1)}, f32[34,16,128]{2,1,0:T(8,128)S(1)}, u32[]{:S(2)}, u32[]{:S(2)}) %collective-permute-start) | collective-permute-done | bytes 278560 | tf_op jit(solution)/shard_map/ppermute | solution.py:378
  11.9 0.0 collective-permute-done.1.near.near_x
  11.9 0.0 copy-start
  11.9 0.0 copy-start.1
  11.9 0.0 copy-start.3
  11.9 0.1 shard_map.175
  12.0 0.0 copy-start.2
  12.0 4.8 %collective-permute-start.2 = (f32[44,8,128]{2,1,0:T(8,128)S(1)}, f32[44,8,128]{2,1,0:T(8,128)S(1)}, u32[]{:S(2)}, u32[]{:S(2)}) collective-permute-start(f32[44,8,128]{2,1,0:T(8,128)S(1)} %get-tuple-element.20), channel_id=1, source_target_pairs={{1,2},{3,4},{5,6},{2,1},{4,3},{6,5},{9,10},{11,12},{13,14},{10,9},... | collective-permute-start | bytes 540680 | tf_op jit(solution)/shard_map/ppermute | solution.py:378
  16.8 1.9 %collective-permute-start.3 = (f32[44,8,128]{2,1,0:T(8,128)S(1)}, f32[44,8,128]{2,1,0:T(8,128)S(1)}, u32[]{:S(2)}, u32[]{:S(2)}) collective-permute-start(f32[44,8,128]{2,1,0:T(8,128)S(1)} %get-tuple-element.21), channel_id=1, source_target_pairs={{0,1},{2,3},{4,5},{6,7},{1,0},{3,2},{5,4},{7,6},{8,9},{10,11},{12,... | collective-permute-start | bytes 540680 | tf_op jit(solution)/shard_map/ppermute | solution.py:378
  19.4 0.0 copy-done
  19.4 0.0 copy-done.1
  19.4 0.0 copy-done.3
  19.4 0.0 copy-done.2
  19.4 1.8 %shard_map.176.inject = f32[256,128]{1,0:T(8,128)S(1)} custom-call(s32[1,2048]{1,0:T(1,128)S(1)} %copy-done.2, f32[2,2048]{1,0:T(2,128)S(1)} %bitcast.10, s32[1,2048]{1,0:T(1,128)S(1)} %bitcast.12, f32[2,2048]{1,0:T(2,128)S(1)} %bitcast.11), custom_call_target="tpu_custom_call" | custom-call | flops 800000000 | bytes 2000000 | tf_op jit(solution)/shard_map/pallas_call | solution.py:23
  21.2 1.0 %collective-permute-done.2.odds = f32[44,8,128]{2,1,0:T(8,128)S(1)} collective-permute-done((f32[44,8,128]{2,1,0:T(8,128)S(1)}, f32[44,8,128]{2,1,0:T(8,128)S(1)}, u32[]{:S(2)}, u32[]{:S(2)}) %collective-permute-start.2) | collective-permute-done | bytes 180256 | tf_op jit(solution)/shard_map/ppermute | solution.py:378
  22.2 3.3 %collective-permute-done.3.evens = f32[44,8,128]{2,1,0:T(8,128)S(1)} collective-permute-done((f32[44,8,128]{2,1,0:T(8,128)S(1)}, f32[44,8,128]{2,1,0:T(8,128)S(1)}, u32[]{:S(2)}, u32[]{:S(2)}) %collective-permute-start.3) | collective-permute-done | bytes 180256 | tf_op jit(solution)/shard_map/ppermute | solution.py:378
  25.6 1.0 %shard_map.177 = (f32[3,4,16,128]{3,2,1,0:T(8,128)S(1)}, f32[2,4,16,128]{3,2,1,0:T(8,128)S(1)}, f32[2,3,8,8,128]{4,3,2,1,0:T(8,128)S(1)}, f32[6,3,8,8,128]{4,3,2,1,0:T(8,128)S(1)}) custom-call(s32[1]{0:T(128)S(6)} %copy.19.source, f32[56,16,128]{2,1,0:T(8,128)S(1)} %get-tuple-element.17.loc, f32[34,16,128]{2,1,0:T(8,128)S(1)} %collective-permute-done.far.far_x, ...), custom_call_target="tpu_custom_call" | custom-call | flops 2000000 | bytes 2000000 | tf_op jit(solution)/shard_map/pallas_call | solution.py:23
  26.6 5.9 %collective-permute-start.6 = (f32[3,4,16,128]{3,2,1,0:T(8,128)S(1)}, f32[3,4,16,128]{3,2,1,0:T(8,128)S(1)}, u32[]{:S(2)}, u32[]{:S(2)}) collective-permute-start(f32[3,4,16,128]{3,2,1,0:T(8,128)S(1)} %get-tuple-element.27.own), channel_id=1, source_target_pairs={{0,768},{256,512},{512,256},{768,0},{1,769},{257,513},{513,257},{7... | collective-permute-start | bytes 294920 | tf_op jit(solution)/shard_map/ppermute | solution.py:447
  32.5 4.2 %collective-permute-start.5 = (f32[3,4,16,128]{3,2,1,0:T(8,128)S(1)}, f32[3,4,16,128]{3,2,1,0:T(8,128)S(1)}, u32[]{:S(2)}, u32[]{:S(2)}) collective-permute-start(f32[3,4,16,128]{3,2,1,0:T(8,128)S(1)} %get-tuple-element.27.own), channel_id=1, source_target_pairs={{0,256},{256,0},{512,768},{768,512},{1,257},{257,1},{513,769},{769... | collective-permute-start | bytes 294920 | tf_op jit(solution)/shard_map/ppermute | solution.py:447
  36.7 2.1 %collective-permute-start.4 = (f32[3,4,16,128]{3,2,1,0:T(8,128)S(1)}, f32[3,4,16,128]{3,2,1,0:T(8,128)S(1)}, u32[]{:S(2)}, u32[]{:S(2)}) collective-permute-start(f32[3,4,16,128]{3,2,1,0:T(8,128)S(1)} %get-tuple-element.27.own), channel_id=1, source_target_pairs={{0,512},{256,768},{512,0},{768,256},{1,513},{257,769},{513,1},{769... | collective-permute-start | bytes 294920 | tf_op jit(solution)/shard_map/ppermute | solution.py:447
  38.8 0.9 %shard_map.178 = (f32[4,16,128]{2,1,0:T(8,128)}, f32[4,16,128]{2,1,0:T(8,128)}) custom-call(f32[2,4,16,128]{3,2,1,0:T(8,128)S(1)} %get-tuple-element.22.now, f32[2,3,8,8,128]{4,3,2,1,0:T(8,128)S(1)} %get-tuple-element.23.ahead, f32[6,3,8,8,128]{4,3,2,1,0:T(8,128)S(1)} %get-tuple-element.24.weights, f32[256,128]{1,0:T(8,128)S(1)} %shard_map.176.inject, ...), custom_call_target="tpu_custom_call" | custom-call | flops 2000000 | bytes 2000000 | tf_op jit(solution)/shard_map/pallas_call | solution.py:23
  39.7 0.0 collective-permute-done.6.around
  39.7 2.4 %collective-permute-done.5.beside = f32[3,4,16,128]{3,2,1,0:T(8,128)S(1)} collective-permute-done((f32[3,4,16,128]{3,2,1,0:T(8,128)S(1)}, f32[3,4,16,128]{3,2,1,0:T(8,128)S(1)}, u32[]{:S(2)}, u32[]{:S(2)}) %collective-permute-start.5) | collective-permute-done | bytes 98336 | tf_op jit(solution)/shard_map/ppermute | solution.py:447
  42.1 6.9 %collective-permute-done.4.across = f32[3,4,16,128]{3,2,1,0:T(8,128)S(1)} collective-permute-done((f32[3,4,16,128]{3,2,1,0:T(8,128)S(1)}, f32[3,4,16,128]{3,2,1,0:T(8,128)S(1)}, u32[]{:S(2)}, u32[]{:S(2)}) %collective-permute-start.4) | collective-permute-done | bytes 98336 | tf_op jit(solution)/shard_map/ppermute | solution.py:447
  49.1 0.7 %shard_map.179 = (f32[4,16,128]{2,1,0:T(8,128)}, f32[4,16,128]{2,1,0:T(8,128)}) custom-call(f32[3,4,16,128]{3,2,1,0:T(8,128)S(1)} %get-tuple-element.27.own, f32[3,4,16,128]{3,2,1,0:T(8,128)S(1)} %collective-permute-done.4.across, f32[3,4,16,128]{3,2,1,0:T(8,128)S(1)} %collective-permute-done.5.beside, f32[3,4,16,128]{3,2,1,0:T(8,128)S(1)} %collective-permute-done.6.around), custom_call_target="tpu_custom_call" | custom-call | flops 2000000 | bytes 2000000 | tf_op jit(solution)/shard_map/pallas_call | solution.py:23
Async XLA Ops:
  1.9 9.9 %collective-permute-start = (f32[34,16,128]{2,1,0:T(8,128)S(1)}, f32[34,16,128]{2,1,0:T(8,128)S(1)}, u32[]{:S(2)}, u32[]{:S(2)}) collective-permute-start(f32[34,16,128]{2,1,0:T(8,128)S(1)} %get-tuple-element.18), channel_id=1, source_target_pairs={{8,16},{24,32},{40,48},{56,64},{72,80},{88,96},{104,112},{120,128}... | collective-permute-start | bytes 835592 | tf_op jit(solution)/shard_map/ppermute | solution.py:378
  3.9 8.0 %collective-permute-start.1 = (f32[34,16,128]{2,1,0:T(8,128)S(1)}, f32[34,16,128]{2,1,0:T(8,128)S(1)}, u32[]{:S(2)}, u32[]{:S(2)}) collective-permute-start(f32[34,16,128]{2,1,0:T(8,128)S(1)} %get-tuple-element.19), channel_id=1, source_target_pairs={{0,8},{16,24},{32,40},{48,56},{64,72},{80,88},{96,104},{112,120},{... | collective-permute-start | bytes 835592 | tf_op jit(solution)/shard_map/ppermute | solution.py:378
  11.9 7.5 %copy-start = (f32[1,2,2048]{2,1,0:T(2,128)S(1)}, f32[1,2,2048]{2,1,0:T(2,128)}, u32[]{:S(2)}) copy-start(f32[1,2,2048]{2,1,0:T(2,128)} %param.26) | copy-start | bytes 49156
  11.9 7.5 %copy-start.1 = (f32[1,2,2048]{2,1,0:T(2,128)S(1)}, f32[1,2,2048]{2,1,0:T(2,128)}, u32[]{:S(2)}) copy-start(f32[1,2,2048]{2,1,0:T(2,128)} %param.28) | copy-start | bytes 49156
  11.9 7.5 %copy-start.3 = (s32[2048]{0:T(1024)S(1)}, s32[2048]{0:T(1024)}, u32[]{:S(2)}) copy-start(s32[2048]{0:T(1024)} %param.27) | copy-start | bytes 24580
  12.0 7.4 %copy-start.2 = (s32[1,2048]{1,0:T(1,128)S(1)}, s32[1,2048]{1,0:T(1,128)}, u32[]{:S(2)}) copy-start(s32[1,2048]{1,0:T(1,128)} %recv_cells.1) | copy-start | bytes 24580
  12.0 10.2 %collective-permute-start.2 = (f32[44,8,128]{2,1,0:T(8,128)S(1)}, f32[44,8,128]{2,1,0:T(8,128)S(1)}, u32[]{:S(2)}, u32[]{:S(2)}) collective-permute-start(f32[44,8,128]{2,1,0:T(8,128)S(1)} %get-tuple-element.20), channel_id=1, source_target_pairs={{1,2},{3,4},{5,6},{2,1},{4,3},{6,5},{9,10},{11,12},{13,14},{10,9},... | collective-permute-start | bytes 540680 | tf_op jit(solution)/shard_map/ppermute | solution.py:378
  16.8 8.7 %collective-permute-start.3 = (f32[44,8,128]{2,1,0:T(8,128)S(1)}, f32[44,8,128]{2,1,0:T(8,128)S(1)}, u32[]{:S(2)}, u32[]{:S(2)}) collective-permute-start(f32[44,8,128]{2,1,0:T(8,128)S(1)} %get-tuple-element.21), channel_id=1, source_target_pairs={{0,1},{2,3},{4,5},{6,7},{1,0},{3,2},{5,4},{7,6},{8,9},{10,11},{12,... | collective-permute-start | bytes 540680 | tf_op jit(solution)/shard_map/ppermute | solution.py:378
  26.6 13.1 %collective-permute-start.6 = (f32[3,4,16,128]{3,2,1,0:T(8,128)S(1)}, f32[3,4,16,128]{3,2,1,0:T(8,128)S(1)}, u32[]{:S(2)}, u32[]{:S(2)}) collective-permute-start(f32[3,4,16,128]{3,2,1,0:T(8,128)S(1)} %get-tuple-element.27.own), channel_id=1, source_target_pairs={{0,768},{256,512},{512,256},{768,0},{1,769},{257,513},{513,257},{7... | collective-permute-start | bytes 294920 | tf_op jit(solution)/shard_map/ppermute | solution.py:447
  32.5 9.6 %collective-permute-start.5 = (f32[3,4,16,128]{3,2,1,0:T(8,128)S(1)}, f32[3,4,16,128]{3,2,1,0:T(8,128)S(1)}, u32[]{:S(2)}, u32[]{:S(2)}) collective-permute-start(f32[3,4,16,128]{3,2,1,0:T(8,128)S(1)} %get-tuple-element.27.own), channel_id=1, source_target_pairs={{0,256},{256,0},{512,768},{768,512},{1,257},{257,1},{513,769},{769... | collective-permute-start | bytes 294920 | tf_op jit(solution)/shard_map/ppermute | solution.py:447
  36.7 12.3 %collective-permute-start.4 = (f32[3,4,16,128]{3,2,1,0:T(8,128)S(1)}, f32[3,4,16,128]{3,2,1,0:T(8,128)S(1)}, u32[]{:S(2)}, u32[]{:S(2)}) collective-permute-start(f32[3,4,16,128]{3,2,1,0:T(8,128)S(1)} %get-tuple-element.27.own), channel_id=1, source_target_pairs={{0,512},{256,768},{512,0},{768,256},{1,513},{257,769},{513,1},{769... | collective-permute-start | bytes 294920 | tf_op jit(solution)/shard_map/ppermute | solution.py:447

commit v4 on v3

--- a/solution.py
+++ b/solution.py
@@ -346,10 +346,15 @@
         scale = taper * (2.0 * speed[i][mid])
         image0, image1 = scale * images[0][i], scale * images[1][i]
         p_mid, q_mid = p_next[i][mid], q_next[i][mid]
-        grads[0, :, ys, :] = p[:, ys, :] * image0 + p_mid * image1
-        grads[1, :, ys, :] = q[:, ys, :] * image0 + q_mid * image1
         g0, g1 = f0[i][mid], f1[i][mid]
-        grads[2, :, ys, :] = g0 * g0 + g1 * g1
+        sums = (
+            p[:, ys, :] * image0 + p_mid * image1,
+            q[:, ys, :] * image0 + q_mid * image1,
+            g0 * g0 + g1 * g1,
+        )
+        for shot in range(grads.shape[0]):
+            for number in range(3):
+                grads[shot, number, :, ys, :] = sums[number]
         now[0, :, ys, :] = p_mid
         now[1, :, ys, :] = q_mid
     for i in range(3):
@@ -378,8 +383,8 @@
     return lax.ppermute(part, axis, [(i, i + 1) for i in lows] + [(i + 1, i) for i in lows])
 
 
-def finish_kernel(own, across, beside, around, grad_e, grad_d):
-    total = [(own[i] + beside[i]) + (around[i] + across[i]) for i in range(3)]
+def finish_kernel(parts, grad_e, grad_d):
+    total = [sum(parts[shot, i] for shot in range(parts.shape[0])) for i in range(3)]
     scale = 1.0 / jnp.sqrt(total[2] + 1.0)
     grad_e[...] = total[0] * scale
     grad_d[...] = total[1] * scale
@@ -434,7 +439,7 @@
     grads, now, ahead, weights = call(
         functools.partial(first_step_kernel, grid_y),
         [
-            (3, size_x, size_y, size_z),
+            (lax.axis_size("shot"), 3, size_x, size_y, size_z),
             (2, size_x, size_y, size_z),
             (2, 3, count, 8, size_z),
             (6, 3, count, 8, size_z),
@@ -442,14 +447,11 @@
         (source_cells, loc, far, near, odds, evens, inject),
         smem=(0,),
     )
-    shots = range(lax.axis_size("shot"))
-    parts = [
-        lax.ppermute(grads, "shot", [(i, i ^ turn) for i in shots]) for turn in (2, 1, 3)
-    ]
+    parts = lax.all_to_all(grads, "shot", 0, 0)
     p_final, q_final = call(
         second_step_kernel, [(size_x, size_y, size_z)] * 2, (now, ahead, weights, inject, loc)
     )
-    grad_e, grad_d = call(finish_kernel, [(size_x, size_y, size_z)] * 2, (grads, *parts))
+    grad_e, grad_d = call(finish_kernel, [(size_x, size_y, size_z)] * 2, (parts,))
     return (p_final[None], q_final[None], grad_e, grad_d)
 
 

time: 50.1 us -> 48 us (0.958)
  starting transfers between devices: 25.2 us -> 20 us
  waiting for transfers between devices: 17.4 us -> 19.8 us
  Pallas kernels: 5.7 us -> 6.46 us
    ppermute x3 -> x0, starting transfers between devices: 12.2 us -> none  [body(): lax.ppermute(grads, 'shot', [(i, i ^ turn) for i in shots])]
    all_to_all x0 -> x1, waiting for transfers between devices: none -> 11.7 us  [body(): parts = lax.all_to_all(grads, 'shot', 0, 0)]
    ppermute x3 -> x0, waiting for transfers between devices: 9.38 us -> none  [body(): lax.ppermute(grads, 'shot', [(i, i ^ turn) for i in shots])]
    all_to_all x0 -> x1, starting transfers between devices: none -> 6.98 us  [body(): parts = lax.all_to_all(grads, 'shot', 0, 0)]
    pallas_call x6, Pallas kernels: 5.7 us -> 6.46 us  [call(): pl.pallas_call(kernel, out_shape=shapes, in_specs=specs, out_specs=[pl.Bl...]
  transfers between devices with their start and end apart: 7 -> 5, of which waited for: 5 -> 4; matrix products, arithmetic and copies ran while one was open for 0% -> 0% of each run, Pallas kernels for 5% -> 6%
where the time goes in v4:
time: 48 us; the launch traced here: 47.6 us
  starting transfers between devices  20 us (42%)
  waiting for transfers between devices  19.8 us (41%)
  Pallas kernels  6.46 us (13%)
  between operations  1.39 us (3%)
    ppermute x4, starting transfers between devices, swap(): lax.ppermute(part, axis, [(i, i + 1) for i in lows] + [(i + 1, i) for i i...  13 us
    all_to_all x1, waiting for transfers between devices, body(): parts = lax.all_to_all(grads, 'shot', 0, 0)  11.7 us
    ppermute x4, waiting for transfers between devices, swap(): lax.ppermute(part, axis, [(i, i + 1) for i in lows] + [(i + 1, i) for i i...  8.02 us
    all_to_all x1, starting transfers between devices, body(): parts = lax.all_to_all(grads, 'shot', 0, 0)  6.98 us
    pallas_call x6, Pallas kernels, call(): pl.pallas_call(kernel, out_shape=shapes, in_specs=specs, out_specs=[pl.Bl...  6.46 us
  transfers between devices with their start and end apart: 5, of which 4 were waited for; matrix products, arithmetic and copies ran while one was open for 0% of the time, Pallas kernels for 6%

profile of v4, /device:TPU:562, one launch (start us, length us, event | category | flops | bytes accessed | tf_op | source)
XLA Modules:
  0.0 47.6 jit_solution(14042663278117932993)
XLA Ops:
  0.6 1.3 %shard_map.174 = (f32[56,16,128]{2,1,0:T(8,128)S(1)}, f32[34,16,128]{2,1,0:T(8,128)S(1)}, f32[34,16,128]{2,1,0:T(8,128)S(1)}) custom-call(f32[4,16,128]{2,1,0:T(8,128)} %bitcast.14, f32[4,16,128]{2,1,0:T(8,128)} %bitcast.15, f32[4,16,128]{2,1,0:T(8,128)} %bitcast.16, f32[4,16,128]{2,1,0:T(8,128)} %bitcast.17, f32[2,4,16,128]{3,2,1,0:T(8,128)} %bitcast.13, ...), custom_call_target="tpu_custom_call" | custom-call | flops 2000000 | bytes 2000000 | tf_op jit(solution)/shard_map/pallas_call | solution.py:23
  1.9 1.9 %collective-permute-start = (f32[34,16,128]{2,1,0:T(8,128)S(1)}, f32[34,16,128]{2,1,0:T(8,128)S(1)}, u32[]{:S(2)}, u32[]{:S(2)}) collective-permute-start(f32[34,16,128]{2,1,0:T(8,128)S(1)} %get-tuple-element.18), channel_id=1, source_target_pairs={{8,16},{24,32},{40,48},{56,64},{72,80},{88,96},{104,112},{120,128}... | collective-permute-start | bytes 835592 | tf_op jit(solution)/shard_map/ppermute | solution.py:383
  3.9 4.4 %collective-permute-start.1 = (f32[34,16,128]{2,1,0:T(8,128)S(1)}, f32[34,16,128]{2,1,0:T(8,128)S(1)}, u32[]{:S(2)}, u32[]{:S(2)}) collective-permute-start(f32[34,16,128]{2,1,0:T(8,128)S(1)} %get-tuple-element.19), channel_id=1, source_target_pairs={{0,8},{16,24},{32,40},{48,56},{64,72},{80,88},{96,104},{112,120},{... | collective-permute-start | bytes 835592 | tf_op jit(solution)/shard_map/ppermute | solution.py:383
  8.2 3.6 %collective-permute-done.far.far_x = f32[34,16,128]{2,1,0:T(8,128)S(1)} collective-permute-done((f32[34,16,128]{2,1,0:T(8,128)S(1)}, f32[34,16,128]{2,1,0:T(8,128)S(1)}, u32[]{:S(2)}, u32[]{:S(2)}) %collective-permute-start) | collective-permute-done | bytes 278560 | tf_op jit(solution)/shard_map/ppermute | solution.py:383
  11.9 0.0 collective-permute-done.1.near.near_x
  11.9 0.0 copy-start
  11.9 0.0 copy-start.1
  11.9 0.0 copy-start.3
  11.9 0.1 shard_map.175
  12.0 0.0 copy-start.2
  12.0 4.8 %collective-permute-start.2 = (f32[44,8,128]{2,1,0:T(8,128)S(1)}, f32[44,8,128]{2,1,0:T(8,128)S(1)}, u32[]{:S(2)}, u32[]{:S(2)}) collective-permute-start(f32[44,8,128]{2,1,0:T(8,128)S(1)} %get-tuple-element.20), channel_id=1, source_target_pairs={{1,2},{3,4},{5,6},{2,1},{4,3},{6,5},{9,10},{11,12},{13,14},{10,9},... | collective-permute-start | bytes 540680 | tf_op jit(solution)/shard_map/ppermute | solution.py:383
  16.8 1.9 %collective-permute-start.3 = (f32[44,8,128]{2,1,0:T(8,128)S(1)}, f32[44,8,128]{2,1,0:T(8,128)S(1)}, u32[]{:S(2)}, u32[]{:S(2)}) collective-permute-start(f32[44,8,128]{2,1,0:T(8,128)S(1)} %get-tuple-element.21), channel_id=1, source_target_pairs={{0,1},{2,3},{4,5},{6,7},{1,0},{3,2},{5,4},{7,6},{8,9},{10,11},{12,... | collective-permute-start | bytes 540680 | tf_op jit(solution)/shard_map/ppermute | solution.py:383
  19.4 0.0 copy-done
  19.4 0.0 copy-done.1
  19.4 0.0 copy-done.3
  19.4 0.0 copy-done.2
  19.4 1.8 %shard_map.176.inject = f32[256,128]{1,0:T(8,128)S(1)} custom-call(s32[1,2048]{1,0:T(1,128)S(1)} %copy-done.2, f32[2,2048]{1,0:T(2,128)S(1)} %bitcast.10, s32[1,2048]{1,0:T(1,128)S(1)} %bitcast.12, f32[2,2048]{1,0:T(2,128)S(1)} %bitcast.11), custom_call_target="tpu_custom_call" | custom-call | flops 800000000 | bytes 2000000 | tf_op jit(solution)/shard_map/pallas_call | solution.py:23
  21.2 1.0 %collective-permute-done.2.odds = f32[44,8,128]{2,1,0:T(8,128)S(1)} collective-permute-done((f32[44,8,128]{2,1,0:T(8,128)S(1)}, f32[44,8,128]{2,1,0:T(8,128)S(1)}, u32[]{:S(2)}, u32[]{:S(2)}) %collective-permute-start.2) | collective-permute-done | bytes 180256 | tf_op jit(solution)/shard_map/ppermute | solution.py:383
  22.2 3.4 %collective-permute-done.3.evens = f32[44,8,128]{2,1,0:T(8,128)S(1)} collective-permute-done((f32[44,8,128]{2,1,0:T(8,128)S(1)}, f32[44,8,128]{2,1,0:T(8,128)S(1)}, u32[]{:S(2)}, u32[]{:S(2)}) %collective-permute-start.3) | collective-permute-done | bytes 180256 | tf_op jit(solution)/shard_map/ppermute | solution.py:383
  25.6 1.8 %shard_map.177 = (f32[4,3,4,16,128]{4,3,2,1,0:T(8,128)}, f32[2,4,16,128]{3,2,1,0:T(8,128)S(1)}, f32[2,3,8,8,128]{4,3,2,1,0:T(8,128)S(1)}, f32[6,3,8,8,128]{4,3,2,1,0:T(8,128)S(1)}) custom-call(s32[1]{0:T(128)S(6)} %copy.19.source, f32[56,16,128]{2,1,0:T(8,128)S(1)} %get-tuple-element.17.loc, f32[34,16,128]{2,1,0:T(8,128)S(1)} %collective-permute-done.far.far_x, ...), custom_call_target="tpu_custom_call" | custom-call | flops 2000000 | bytes 2000000 | tf_op jit(solution)/shard_map/pallas_call | solution.py:23
  27.4 7.0 %all-to-all-start = ((f32[4,3,4,16,128]{4,3,2,1,0:T(8,128)}), f32[4,3,4,16,128]{4,3,2,1,0:T(8,128)S(1)}, u32[]{:S(2)}, u32[]{:S(2)}) async-start(f32[4,3,4,16,128]{4,3,2,1,0:T(8,128)} %get-tuple-element.27), calls=%async_computation | async-start | bytes 786432 | tf_op jit(solution)/shard_map/all_to_all | solution.py:450
  34.4 0.9 %shard_map.178 = (f32[4,16,128]{2,1,0:T(8,128)}, f32[4,16,128]{2,1,0:T(8,128)}) custom-call(f32[2,4,16,128]{3,2,1,0:T(8,128)S(1)} %get-tuple-element.22.now, f32[2,3,8,8,128]{4,3,2,1,0:T(8,128)S(1)} %get-tuple-element.23.ahead, f32[6,3,8,8,128]{4,3,2,1,0:T(8,128)S(1)} %get-tuple-element.24.weights, f32[256,128]{1,0:T(8,128)S(1)} %shard_map.176.inject, ...), custom_call_target="tpu_custom_call" | custom-call | flops 2000000 | bytes 2000000 | tf_op jit(solution)/shard_map/pallas_call | solution.py:23
  35.2 11.7 %all-to-all-done.parts = f32[4,3,4,16,128]{4,3,2,1,0:T(8,128)S(1)} async-done(((f32[4,3,4,16,128]{4,3,2,1,0:T(8,128)}), f32[4,3,4,16,128]{4,3,2,1,0:T(8,128)S(1)}, u32[]{:S(2)}, u32[]{:S(2)}) %all-to-all-start) | async-done | bytes 393248 | tf_op jit(solution)/shard_map/all_to_all | solution.py:450
  47.0 0.7 %shard_map.179 = (f32[4,16,128]{2,1,0:T(8,128)}, f32[4,16,128]{2,1,0:T(8,128)}) custom-call(f32[4,3,4,16,128]{4,3,2,1,0:T(8,128)S(1)} %all-to-all-done.parts), custom_call_target="tpu_custom_call" | custom-call | flops 2000000 | bytes 2000000 | tf_op jit(solution)/shard_map/pallas_call | solution.py:23
Async XLA Ops:
  1.9 9.9 %collective-permute-start = (f32[34,16,128]{2,1,0:T(8,128)S(1)}, f32[34,16,128]{2,1,0:T(8,128)S(1)}, u32[]{:S(2)}, u32[]{:S(2)}) collective-permute-start(f32[34,16,128]{2,1,0:T(8,128)S(1)} %get-tuple-element.18), channel_id=1, source_target_pairs={{8,16},{24,32},{40,48},{56,64},{72,80},{88,96},{104,112},{120,128}... | collective-permute-start | bytes 835592 | tf_op jit(solution)/shard_map/ppermute | solution.py:383
  3.9 8.0 %collective-permute-start.1 = (f32[34,16,128]{2,1,0:T(8,128)S(1)}, f32[34,16,128]{2,1,0:T(8,128)S(1)}, u32[]{:S(2)}, u32[]{:S(2)}) collective-permute-start(f32[34,16,128]{2,1,0:T(8,128)S(1)} %get-tuple-element.19), channel_id=1, source_target_pairs={{0,8},{16,24},{32,40},{48,56},{64,72},{80,88},{96,104},{112,120},{... | collective-permute-start | bytes 835592 | tf_op jit(solution)/shard_map/ppermute | solution.py:383
  11.9 7.5 %copy-start = (f32[1,2,2048]{2,1,0:T(2,128)S(1)}, f32[1,2,2048]{2,1,0:T(2,128)}, u32[]{:S(2)}) copy-start(f32[1,2,2048]{2,1,0:T(2,128)} %param.26) | copy-start | bytes 49156
  11.9 7.5 %copy-start.1 = (f32[1,2,2048]{2,1,0:T(2,128)S(1)}, f32[1,2,2048]{2,1,0:T(2,128)}, u32[]{:S(2)}) copy-start(f32[1,2,2048]{2,1,0:T(2,128)} %param.28) | copy-start | bytes 49156
  11.9 7.5 %copy-start.3 = (s32[2048]{0:T(1024)S(1)}, s32[2048]{0:T(1024)}, u32[]{:S(2)}) copy-start(s32[2048]{0:T(1024)} %param.27) | copy-start | bytes 24580
  12.0 7.4 %copy-start.2 = (s32[1,2048]{1,0:T(1,128)S(1)}, s32[1,2048]{1,0:T(1,128)}, u32[]{:S(2)}) copy-start(s32[1,2048]{1,0:T(1,128)} %recv_cells.1) | copy-start | bytes 24580
  12.0 10.2 %collective-permute-start.2 = (f32[44,8,128]{2,1,0:T(8,128)S(1)}, f32[44,8,128]{2,1,0:T(8,128)S(1)}, u32[]{:S(2)}, u32[]{:S(2)}) collective-permute-start(f32[44,8,128]{2,1,0:T(8,128)S(1)} %get-tuple-element.20), channel_id=1, source_target_pairs={{1,2},{3,4},{5,6},{2,1},{4,3},{6,5},{9,10},{11,12},{13,14},{10,9},... | collective-permute-start | bytes 540680 | tf_op jit(solution)/shard_map/ppermute | solution.py:383
  16.8 8.8 %collective-permute-start.3 = (f32[44,8,128]{2,1,0:T(8,128)S(1)}, f32[44,8,128]{2,1,0:T(8,128)S(1)}, u32[]{:S(2)}, u32[]{:S(2)}) collective-permute-start(f32[44,8,128]{2,1,0:T(8,128)S(1)} %get-tuple-element.21), channel_id=1, source_target_pairs={{0,1},{2,3},{4,5},{6,7},{1,0},{3,2},{5,4},{7,6},{8,9},{10,11},{12,... | collective-permute-start | bytes 540680 | tf_op jit(solution)/shard_map/ppermute | solution.py:383
  27.4 19.6 %all-to-all-start = ((f32[4,3,4,16,128]{4,3,2,1,0:T(8,128)}), f32[4,3,4,16,128]{4,3,2,1,0:T(8,128)S(1)}, u32[]{:S(2)}, u32[]{:S(2)}) async-start(f32[4,3,4,16,128]{4,3,2,1,0:T(8,128)} %get-tuple-element.27), calls=%async_computation | async-start | bytes 786432 | tf_op jit(solution)/shard_map/all_to_all | solution.py:450

commit v5 on v3

--- a/solution.py
+++ b/solution.py
@@ -192,78 +192,79 @@
     wide, narrow = [], []
     for number in range(WIDE):
         rows = slice(number * size_x, (number + 1) * size_x)
-        wide += [below[rows], loc[rows, ys, :], above[rows]]
+        wide.append(jnp.concatenate([below[rows], loc[rows, ys, :], above[rows]], axis=0))
     for number in range(NARROW):
         start = (WIDE + number) * size_x
         begin = WIDE * size_x + 2 * number
-        narrow += [
-            below[begin : begin + 2],
-            loc[start : start + size_x, ys, :],
-            above[begin : begin + 2],
-        ]
-    return jnp.concatenate(wide, axis=0), jnp.concatenate(narrow, axis=0)
-
-
-def pack_kernel(loc, far, near, odds, evens):
+        rows = slice(begin, begin + 2)
+        here = loc[start : start + size_x, ys, :]
+        narrow.append(jnp.concatenate([below[rows], here, above[rows]], axis=0))
+    return wide, narrow
+
+
+def turn(rows, by):
+    by = by % 8
+    return pltpu.roll(rows, by, 1) if by else rows
+
+
+def pack(rows, part, groups):
+    height, count = 8 // groups, rows.shape[0] // groups
+    out = None
+    for group in range(groups):
+        piece = turn(rows[group * count : (group + 1) * count], height * (group - part * (groups - 1)))
+        mask = row_mask(piece.shape, height * group)
+        out = piece if out is None else jnp.where(mask, out, piece)
+    return out
+
+
+def unpack(high, low, groups):
+    height = 8 // groups
+    edges = []
+    for group in range(groups):
+        upper = turn(high, -height * group)
+        lower = turn(low, height * (groups - 1 - group))
+        edges.append(jnp.where(row_mask(high.shape, 4), upper, lower))
+    return jnp.concatenate(edges, axis=0)
+
+
+def early_rows(wide, narrow):
+    return [tile[2 : tile.shape[0] - 2] for tile in wide] + narrow[5:]
+
+
+def send_both(parts, evens, odds, start):
+    odd = lax.rem(lax.axis_index("gy"), 2) == 1
+    rows = slice(start, start + parts[0].shape[0])
+    evens[rows] = jnp.where(odd, parts[0], parts[1])
+    odds[rows] = jnp.where(odd, parts[1], parts[0])
+
+
+def from_both(evens, odds):
+    odd = lax.rem(lax.axis_index("gy"), 2) == 1
+    return jnp.where(odd, odds[...], evens[...]), jnp.where(odd, evens[...], odds[...])
+
+
+def early_kernel(loc, far, near, odds, evens):
     size_x = loc.shape[0] // FIELDS
-    made = []
+    parts = []
     for part in range(2):
         wide, narrow = tiles_of(loc, near, far, size_x, part)
-        half = wide.shape[0] // 2
-        quarter = narrow.shape[0] // 4
-        turned = pltpu.roll(wide, 4, 1)
-        mask = row_mask((half, 8, 128), 4)
-        if part == 0:
-            top = jnp.where(mask, wide[:half], turned[half:])
-        else:
-            top = jnp.where(mask, turned[:half], wide[half:])
-        out = None
-        for group in range(4):
-            rows = narrow[group * quarter : (group + 1) * quarter]
-            turn = (2 * group - 6 * part) % 8
-            rows = pltpu.roll(rows, turn, 1) if turn else rows
-            out = rows if out is None else jnp.where(row_mask(rows.shape, 2 * group), out, rows)
-        made.append((top, out))
-    odd = lax.rem(lax.axis_index("gy"), 2) == 1
-    down, up = made
-    for rows, a, b in ((slice(0, half), down[0], up[0]), (slice(half, half + quarter), down[1], up[1])):
-        evens[rows] = jnp.where(odd, a, b)
-        odds[rows] = jnp.where(odd, b, a)
-
-
-def unpack(loc, near, far, evens, odds):
+        parts.append(pack(jnp.concatenate(early_rows(wide, narrow), axis=0), part, 4))
+    send_both(parts, evens, odds, 0)
+
+
+def late_kernel(loc, far, near, odds, evens):
     size_x = loc.shape[0] // FIELDS
-    odd = lax.rem(lax.axis_index("gy"), 2) == 1
-    from_above = jnp.where(odd, odds[...], evens[...])
-    from_below = jnp.where(odd, evens[...], odds[...])
-    wide_rows, narrow_rows = 3 * size_x, size_x + 4
-    half = WIDE * wide_rows // 2
-    quarter = NARROW * narrow_rows // 4
-    mask = row_mask((half, 8, 128), 4)
-    high, low = from_above[0:half], from_below[0:half]
-    wide_edge = jnp.concatenate(
-        [jnp.where(mask, high, pltpu.roll(low, 4, 1)), jnp.where(mask, pltpu.roll(high, 4, 1), low)],
-        axis=0,
-    )
-    high, low = from_above[half : half + quarter], from_below[half : half + quarter]
-    mask = row_mask((quarter, 8, 128), 4)
-    edges = []
-    for group in range(4):
-        first_turn, second_turn = (-2 * group) % 8, (6 - 2 * group) % 8
-        upper = pltpu.roll(high, first_turn, 1) if first_turn else high
-        lower = pltpu.roll(low, second_turn, 1) if second_turn else low
-        edges.append(jnp.where(mask, upper, lower))
-    narrow_edge = jnp.concatenate(edges, axis=0)
-    wide0, narrow0 = tiles_of(loc, near, far, size_x, 0)
-    wide1, narrow1 = tiles_of(loc, near, far, size_x, 1)
-    wide = [
-        [t[n * wide_rows : (n + 1) * wide_rows] for t in (wide0, wide1, wide_edge)] for n in range(WIDE)
-    ]
-    narrow = [
-        [t[n * narrow_rows : (n + 1) * narrow_rows] for t in (narrow0, narrow1, narrow_edge)]
-        for n in range(NARROW)
-    ]
-    return wide, narrow
+    wides, narrows = [], []
+    for part in range(2):
+        wide, narrow = tiles_of(loc, near, far, size_x, part)
+        wides.append(pack(jnp.concatenate(wide, axis=0), part, 2))
+        narrows.append(pack(jnp.concatenate(narrow[:5], axis=0), part, 4))
+    send_both(wides, evens, odds, 0)
+    send_both(narrows, evens, odds, wides[0].shape[0])
+
+
+def cut(rows, count):
+    return [rows[i : i + count] for i in range(0, rows.shape[0], count)]
 
 
 def inject_kernel(grid_y, grid_z, size_x, size_y, recv_cells, recv_values, bound_cells, bound_force, out):
@@ -313,76 +314,86 @@
     out[...] = total[0:rows] + total[rows : 2 * rows] + total[2 * rows : 3 * rows]
 
 
-def first_step_kernel(
-    grid_y, source, loc, far_x, near_x, odds, evens, inject, grads, now, ahead, weights
-):
+def first_step_kernel(grid_y, source, loc, far_x, near_x, odds, evens, inject, grads):
     size_x, size_y = loc.shape[0] // FIELDS, loc.shape[1]
-    wide, narrow = unpack(loc, near_x, far_x, evens, odds)
-    p = loc[(FIELDS - 2) * size_x : (FIELDS - 1) * size_x]
-    q = loc[(FIELDS - 1) * size_x : FIELDS * size_x]
-    source_tiles, mix_tiles = wide[0], wide[1]
-    products = [[wide[2 + a][i] * wide[2 + b][i] for i in range(3)] for a, b in PAIRS]
-    p_base, q_base, p_weight, q_weight, speed, f0, f1 = narrow
     count = size_x + 4
+    high, low = from_both(evens, odds)
+    edge = cut(unpack(high, low, 4), count)
+    middle = [early_rows(*tiles_of(loc, near_x, far_x, size_x, part)) for part in range(2)]
+    fields = [[middle[0][n], middle[1][n], edge[n]] for n in range(len(edge))]
+    products = [[fields[2 + a][i] * fields[2 + b][i] for i in range(3)] for a, b in PAIRS]
     mid = slice(2, 2 + size_x)
-    p_next = adjoint(products, source_tiles, count, 3, False)
-    q_next = adjoint(products, mix_tiles, count, 3, True)
+    p_next = adjoint(products, fields[0], size_x, 2, False)
+    q_next = adjoint(products, fields[1], size_x, 2, True)
+    inner = [[tile[mid] for tile in entry] for entry in products]
+    images = [forward_image(inner, field, size_x) for field in fields[5:7]]
     ring = inject[0 : count * 24].reshape(count, 24, 128)
-    p_next = [p_base[i] + p_next[i] + ring[:, 8 * i : 8 * i + 8] for i in range(3)]
-    q_next = [q_base[i] + q_next[i] for i in range(3)]
-    near = [[tile[2 : 2 + count] for tile in entry] for entry in products]
-    inner = [[tile[mid] for tile in entry] for entry in near]
     bits_y = grid_y.bit_length() - 1
     source_x = (source[0] >> bits_y) - lax.axis_index("gx") * size_x
     source_y = (source[0] & (grid_y - 1)) - lax.axis_index("gy") * size_y
-    images = [forward_image(inner, field, size_x) for field in (f0, f1)]
     shape = (size_x, 8, 128)
     offset_x = lax.broadcasted_iota(jnp.int32, shape, 0) - source_x
+
+    def block(field, ys):
+        return loc[field * size_x : (field + 1) * size_x, ys, :]
+
     for i in range(2):
         ys = slice(8 * i, 8 * i + 8)
         offset_y = lax.broadcasted_iota(jnp.int32, shape, 1) + (8 * i - source_y)
         squared = (offset_x * offset_x + offset_y * offset_y).astype(jnp.float32)
         taper = jnp.minimum(squared * (1.0 / float(TAPER * TAPER)), 1.0)
-        scale = taper * (2.0 * speed[i][mid])
+        scale = taper * (2.0 * block(WIDE + 4, ys))
         image0, image1 = scale * images[0][i], scale * images[1][i]
-        p_mid, q_mid = p_next[i][mid], q_next[i][mid]
-        grads[0, :, ys, :] = p[:, ys, :] * image0 + p_mid * image1
-        grads[1, :, ys, :] = q[:, ys, :] * image0 + q_mid * image1
-        g0, g1 = f0[i][mid], f1[i][mid]
-        grads[2, :, ys, :] = g0 * g0 + g1 * g1
-        now[0, :, ys, :] = p_mid
-        now[1, :, ys, :] = q_mid
-    for i in range(3):
-        ahead[0, i] = p_weight[i] * p_next[i] + q_weight[i] * q_next[i]
-        ahead[1, i] = speed[i] * (p_next[i] + q_next[i])
-        for number in range(6):
-            weights[number, i] = near[number][i]
-
-
-def second_step_kernel(now, ahead, weights, inject, loc, p_out, q_out):
+        p_mid = block(WIDE, ys) + p_next[i] + ring[mid, ys, :]
+        q_mid = block(WIDE + 1, ys) + q_next[i]
+        grads[0, :, ys, :] = block(FIELDS - 2, ys) * image0 + p_mid * image1
+        grads[1, :, ys, :] = block(FIELDS - 1, ys) * image0 + q_mid * image1
+        f0, f1 = block(WIDE + 5, ys), block(WIDE + 6, ys)
+        grads[2, :, ys, :] = f0 * f0 + f1 * f1
+
+
+def second_step_kernel(loc, far_x, near_x, odds, evens, inject, p_out, q_out):
     size_x, size_y = p_out.shape[0], p_out.shape[1]
+    count = size_x + 4
+    high, low = from_both(evens, odds)
+    half = WIDE * (size_x + 8) // 2
+    wide_edge = cut(unpack(high[:half], low[:half], 2), size_x + 8)
+    narrow_edge = cut(unpack(high[half:], low[half:], 4), count)
+    parts = [tiles_of(loc, near_x, far_x, size_x, part) for part in range(2)]
+    wide = [[parts[0][0][n], parts[1][0][n], wide_edge[n]] for n in range(WIDE)]
+    narrow = [[parts[0][1][n], parts[1][1][n], narrow_edge[n]] for n in range(5)]
+    products = [[wide[2 + a][i] * wide[2 + b][i] for i in range(3)] for a, b in PAIRS]
+    p_base, q_base, p_weight, q_weight, speed = narrow
+    mid = slice(2, 2 + size_x)
+    p_next = adjoint(products, wide[0], count, 3, False)
+    q_next = adjoint(products, wide[1], count, 3, True)
+    ring = inject[0 : count * 24].reshape(count, 24, 128)
+    p_next = [p_base[i] + p_next[i] + ring[:, 8 * i : 8 * i + 8] for i in range(3)]
+    q_next = [q_base[i] + q_next[i] for i in range(3)]
+    source = [p_weight[i] * p_next[i] + q_weight[i] * q_next[i] for i in range(3)]
+    mix = [speed[i] * (p_next[i] + q_next[i]) for i in range(3)]
+    products = [[tile[2 : 2 + count] for tile in entry] for entry in products]
+    p_last = adjoint(products, source, size_x, 2, False)
+    q_last = adjoint(products, mix, size_x, 2, True)
+    inner = inject[count * 24 :].reshape(size_x, size_y, 128)
     p = loc[(FIELDS - 2) * size_x : (FIELDS - 1) * size_x]
     q = loc[(FIELDS - 1) * size_x : FIELDS * size_x]
-    products = [[weights[number, i] for i in range(3)] for number in range(6)]
-    p_next = adjoint(products, [ahead[0, i] for i in range(3)], size_x, 2, False)
-    q_next = adjoint(products, [ahead[1, i] for i in range(3)], size_x, 2, True)
-    inner = inject[inject.shape[0] - size_x * size_y :].reshape(size_x, size_y, 128)
     for i in range(2):
         ys = slice(8 * i, 8 * i + 8)
-        p_out[:, ys, :] = 2.0 * now[0, :, ys, :] - p[:, ys, :] + inner[:, ys] + p_next[i]
-        q_out[:, ys, :] = 2.0 * now[1, :, ys, :] - q[:, ys, :] + q_next[i]
+        p_out[:, ys, :] = 2.0 * p_next[i][mid] - p[:, ys] + inner[:, ys] + p_last[i]
+        q_out[:, ys, :] = 2.0 * q_next[i][mid] - q[:, ys] + q_last[i]
+
+
+def finish_kernel(own, other, grad_e, grad_d):
+    total = [own[i] + other[i] for i in range(3)]
+    scale = 1.0 / jnp.sqrt(total[2] + 1.0)
+    grad_e[...] = total[0] * scale
+    grad_d[...] = total[1] * scale
 
 
 def swap(part, axis, start):
     lows = range(start, lax.axis_size(axis) - 1, 2)
     return lax.ppermute(part, axis, [(i, i + 1) for i in lows] + [(i + 1, i) for i in lows])
-
-
-def finish_kernel(own, across, beside, around, grad_e, grad_d):
-    total = [(own[i] + beside[i]) + (around[i] + across[i]) for i in range(3)]
-    scale = 1.0 / jnp.sqrt(total[2] + 1.0)
-    grad_e[...] = total[0] * scale
-    grad_d[...] = total[1] * scale
 
 
 def body(
@@ -426,30 +437,30 @@
         (receiver_cells, receiver_values[0], boundary_cells[None], boundary_force[0]),
         flops=800_000_000,
     )
-    tiles = WIDE * 3 * size_x // 2 + NARROW * (size_x + 4) // 4
-    odds, evens = call(pack_kernel, [(tiles, 8, size_z)] * 2, (loc, far, near))
-    odds = swap(odds, "gy", 1)
-    evens = swap(evens, "gy", 0)
-    count = size_x + 4
-    grads, now, ahead, weights = call(
+    edges = (loc, far, near)
+    early = (WIDE + 2) * (size_x + 4) // 4
+    late = WIDE * (size_x + 8) // 2 + 5 * (size_x + 4) // 4
+    odds, evens = call(early_kernel, [(early, 8, size_z)] * 2, edges)
+    odds, evens = swap(odds, "gy", 1), swap(evens, "gy", 0)
+    late_odds, late_evens = call(late_kernel, [(late, 8, size_z)] * 2, edges)
+    (grads,) = call(
         functools.partial(first_step_kernel, grid_y),
-        [
-            (3, size_x, size_y, size_z),
-            (2, size_x, size_y, size_z),
-            (2, 3, count, 8, size_z),
-            (6, 3, count, 8, size_z),
-        ],
-        (source_cells, loc, far, near, odds, evens, inject),
+        [(3, size_x, size_y, size_z)],
+        (source_cells, *edges, odds, evens, inject),
         smem=(0,),
     )
+    grads, late_odds, late_evens = lax.optimization_barrier((grads, late_odds, late_evens))
     shots = range(lax.axis_size("shot"))
-    parts = [
-        lax.ppermute(grads, "shot", [(i, i ^ turn) for i in shots]) for turn in (2, 1, 3)
-    ]
+    grads = grads + lax.ppermute(grads, "shot", [(i, i ^ 1) for i in shots])
+    late_odds, late_evens = swap(late_odds, "gy", 1), swap(late_evens, "gy", 0)
+    other = lax.ppermute(grads, "shot", [(i, i ^ 3) for i in shots])
     p_final, q_final = call(
-        second_step_kernel, [(size_x, size_y, size_z)] * 2, (now, ahead, weights, inject, loc)
-    )
-    grad_e, grad_d = call(finish_kernel, [(size_x, size_y, size_z)] * 2, (grads, *parts))
+        second_step_kernel,
+        [(size_x, size_y, size_z)] * 2,
+        (*edges, late_odds, late_evens, inject),
+        flops=20_000_000,
+    )
+    grad_e, grad_d = call(finish_kernel, [(size_x, size_y, size_z)] * 2, (grads, other))
     return (p_final[None], q_final[None], grad_e, grad_d)
 
 

time: 50.1 us -> 46.3 us (0.924)
  the two profiles are of different devices: /device:TPU:562 before, /device:TPU:271 now
where the time goes in v5:
time: 46.3 us; the launch traced here: 45.9 us
  starting transfers between devices  28.6 us (62%)
  waiting for transfers between devices  9.86 us (21%)
  Pallas kernels  5.99 us (13%)
  between operations  1.47 us (3%)
    ppermute x6, starting transfers between devices, swap(): lax.ppermute(part, axis, [(i, i + 1) for i in lows] + [(i + 1, i) for i i...  22.7 us
    ppermute x6, waiting for transfers between devices, swap(): lax.ppermute(part, axis, [(i, i + 1) for i in lows] + [(i + 1, i) for i i...  6.59 us
    pallas_call x7, Pallas kernels, call(): pl.pallas_call(kernel, out_shape=shapes, in_specs=specs, out_specs=[pl.Bl...  5.99 us
    ppermute x1, starting transfers between devices, body(): grads = grads + lax.ppermute(grads, 'shot', [(i, i ^ 1) for i in shots])  3.93 us
    ppermute x1, waiting for transfers between devices, body(): other = lax.ppermute(grads, 'shot', [(i, i ^ 3) for i in shots])  3.26 us
    ppermute x1, starting transfers between devices, body(): other = lax.ppermute(grads, 'shot', [(i, i ^ 3) for i in shots])  1.92 us
  transfers between devices with their start and end apart: 8, of which 3 were waited for; matrix products, arithmetic and copies ran while one was open for 0% of the time, Pallas kernels for 8%

profile of v5, /device:TPU:271, one launch (start us, length us, event | category | flops | bytes accessed | tf_op | source)
XLA Modules:
  0.0 45.9 jit_solution(12634001316398948403)
XLA Ops:
  0.6 1.3 %shard_map.174 = (f32[56,16,128]{2,1,0:T(8,128)S(1)}, f32[34,16,128]{2,1,0:T(8,128)S(1)}, f32[34,16,128]{2,1,0:T(8,128)S(1)}) custom-call(f32[4,16,128]{2,1,0:T(8,128)} %bitcast.14, f32[4,16,128]{2,1,0:T(8,128)} %bitcast.15, f32[4,16,128]{2,1,0:T(8,128)} %bitcast.16, f32[4,16,128]{2,1,0:T(8,128)} %bitcast.17, f32[2,4,16,128]{3,2,1,0:T(8,128)} %bitcast.13, ...), custom_call_target="tpu_custom_call" | custom-call | flops 2000000 | bytes 2000000 | tf_op jit(solution)/shard_map/pallas_call | solution.py:23
  1.9 6.3 %collective-permute-start = (f32[34,16,128]{2,1,0:T(8,128)S(1)}, f32[34,16,128]{2,1,0:T(8,128)S(1)}, u32[]{:S(2)}, u32[]{:S(2)}) collective-permute-start(f32[34,16,128]{2,1,0:T(8,128)S(1)} %get-tuple-element.19), channel_id=1, source_target_pairs={{8,16},{24,32},{40,48},{56,64},{72,80},{88,96},{104,112},{120,128}... | collective-permute-start | bytes 835592 | tf_op jit(solution)/shard_map/ppermute | solution.py:396
  8.3 1.9 %collective-permute-start.1 = (f32[34,16,128]{2,1,0:T(8,128)S(1)}, f32[34,16,128]{2,1,0:T(8,128)S(1)}, u32[]{:S(2)}, u32[]{:S(2)}) collective-permute-start(f32[34,16,128]{2,1,0:T(8,128)S(1)} %get-tuple-element.20), channel_id=1, source_target_pairs={{0,8},{16,24},{32,40},{48,56},{64,72},{80,88},{96,104},{112,120},{... | collective-permute-start | bytes 835592 | tf_op jit(solution)/shard_map/ppermute | solution.py:396
  10.9 4.6 %collective-permute-done.far.far_x = f32[34,16,128]{2,1,0:T(8,128)S(1)} collective-permute-done((f32[34,16,128]{2,1,0:T(8,128)S(1)}, f32[34,16,128]{2,1,0:T(8,128)S(1)}, u32[]{:S(2)}, u32[]{:S(2)}) %collective-permute-start) | collective-permute-done | bytes 278560 | tf_op jit(solution)/shard_map/ppermute | solution.py:396
  15.5 0.0 collective-permute-done.1.near.near_x
  15.5 0.0 copy-start
  15.5 0.0 copy-start.1
  15.5 0.0 copy-start.3
  15.5 0.0 copy-start.2
  15.6 0.7 %collective-permute-start.2 = (f32[14,8,128]{2,1,0:T(8,128)S(1)}, f32[14,8,128]{2,1,0:T(8,128)S(1)}, u32[]{:S(2)}, u32[]{:S(2)}) collective-permute-start(f32[14,8,128]{2,1,0:T(8,128)S(1)} %get-tuple-element.21), channel_id=1, source_target_pairs={{1,2},{3,4},{5,6},{2,1},{4,3},{6,5},{9,10},{11,12},{13,14},{10,9},... | collective-permute-start | bytes 172040 | tf_op jit(solution)/shard_map/ppermute | solution.py:396
  16.2 6.0 %collective-permute-start.3 = (f32[14,8,128]{2,1,0:T(8,128)S(1)}, f32[14,8,128]{2,1,0:T(8,128)S(1)}, u32[]{:S(2)}, u32[]{:S(2)}) collective-permute-start(f32[14,8,128]{2,1,0:T(8,128)S(1)} %get-tuple-element.22), channel_id=1, source_target_pairs={{0,1},{2,3},{4,5},{6,7},{1,0},{3,2},{5,4},{7,6},{8,9},{10,11},{12,... | collective-permute-start | bytes 172040 | tf_op jit(solution)/shard_map/ppermute | solution.py:396
  22.2 0.0 copy-done
  22.2 0.0 copy-done.1
  22.2 0.0 copy-done.3
  22.2 0.0 copy-done.2
  22.3 1.8 %shard_map.176.inject = f32[256,128]{1,0:T(8,128)S(1)} custom-call(s32[1,2048]{1,0:T(1,128)S(1)} %copy-done.2, f32[2,2048]{1,0:T(2,128)S(1)} %bitcast.10, s32[1,2048]{1,0:T(1,128)S(1)} %bitcast.12, f32[2,2048]{1,0:T(2,128)S(1)} %bitcast.11), custom_call_target="tpu_custom_call" | custom-call | flops 800000000 | bytes 2000000 | tf_op jit(solution)/shard_map/pallas_call | solution.py:23
  24.0 0.1 shard_map.178
  24.1 0.0 collective-permute-done.2.odds
  24.1 0.0 collective-permute-done.3.evens
  24.1 0.5 %shard_map.177 = f32[3,4,16,128]{3,2,1,0:T(8,128)S(1)} custom-call(s32[1]{0:T(128)S(6)} %copy.19.source, f32[56,16,128]{2,1,0:T(8,128)S(1)} %get-tuple-element.18.loc, f32[34,16,128]{2,1,0:T(8,128)S(1)} %collective-permute-done.far.far_x, f32[34,16,128]{2,1,0:T(8,128)S(1)} %collective-permute-done.1.near.near_x, ...), custom_call_target="tpu_custom_call" | custom-call | flops 2000000 | bytes 2000000 | tf_op jit(solution)/shard_map/pallas_call | solution.py:23
  24.7 3.9 %collective-permute-start.6 = (f32[3,4,16,128]{3,2,1,0:T(8,128)S(1)}, f32[3,4,16,128]{3,2,1,0:T(8,128)S(1)}, u32[]{:S(2)}, u32[]{:S(2)}) collective-permute-start(f32[3,4,16,128]{3,2,1,0:T(8,128)S(1)} %shard_map.177), channel_id=1, source_target_pairs={{0,256},{256,0},{512,768},{768,512},{1,257},{257,1},{513,769},{769... | collective-permute-start | bytes 294920 | tf_op jit(solution)/shard_map/ppermute | solution.py:454
  28.6 0.7 %collective-permute-start.4 = (f32[40,8,128]{2,1,0:T(8,128)S(1)}, f32[40,8,128]{2,1,0:T(8,128)S(1)}, u32[]{:S(2)}, u32[]{:S(2)}) collective-permute-start(f32[40,8,128]{2,1,0:T(8,128)S(1)} %get-tuple-element.25), channel_id=1, source_target_pairs={{1,2},{3,4},{5,6},{2,1},{4,3},{6,5},{9,10},{11,12},{13,14},{10,9},... | collective-permute-start | bytes 491528 | tf_op jit(solution)/shard_map/ppermute | solution.py:396
  29.3 7.2 %collective-permute-start.5 = (f32[40,8,128]{2,1,0:T(8,128)S(1)}, f32[40,8,128]{2,1,0:T(8,128)S(1)}, u32[]{:S(2)}, u32[]{:S(2)}) collective-permute-start(f32[40,8,128]{2,1,0:T(8,128)S(1)} %get-tuple-element.26), channel_id=1, source_target_pairs={{0,1},{2,3},{4,5},{6,7},{1,0},{3,2},{5,4},{7,6},{8,9},{10,11},{12,... | collective-permute-start | bytes 491528 | tf_op jit(solution)/shard_map/ppermute | solution.py:396
  36.5 0.0 collective-permute-done.6
  36.5 1.9 %collective-permute-start.7 = (f32[3,4,16,128]{3,2,1,0:T(8,128)S(1)}, f32[3,4,16,128]{3,2,1,0:T(8,128)S(1)}, u32[]{:S(2)}, u32[]{:S(2)}) collective-permute-start(f32[3,4,16,128]{3,2,1,0:T(8,128)S(1)} %add.3.own), channel_id=1, source_target_pairs={{0,768},{256,512},{512,256},{768,0},{1,769},{257,513},{513,257},{7... | collective-permute-start | bytes 294920 | tf_op jit(solution)/shard_map/ppermute | solution.py:456
  38.4 0.0 collective-permute-done.4.odds
  38.5 2.0 %collective-permute-done.5.evens = f32[40,8,128]{2,1,0:T(8,128)S(1)} collective-permute-done((f32[40,8,128]{2,1,0:T(8,128)S(1)}, f32[40,8,128]{2,1,0:T(8,128)S(1)}, u32[]{:S(2)}, u32[]{:S(2)}) %collective-permute-start.5) | collective-permute-done | bytes 163872 | tf_op jit(solution)/shard_map/ppermute | solution.py:396
  40.4 1.6 %shard_map.179 = (f32[4,16,128]{2,1,0:T(8,128)}, f32[4,16,128]{2,1,0:T(8,128)}) custom-call(f32[56,16,128]{2,1,0:T(8,128)S(1)} %get-tuple-element.18.loc, f32[34,16,128]{2,1,0:T(8,128)S(1)} %collective-permute-done.far.far_x, f32[34,16,128]{2,1,0:T(8,128)S(1)} %collective-permute-done.1.near.near_x, f32[40,8,128]{2,1,0:T(8,128)S(1)} %collective-permute-done.4.odds, ...), custom_call_target="tpu_custom_call" | custom-call | flops 20000000 | bytes 2000000 | tf_op jit(solution)/shard_map/pallas_call | solution.py:23
  42.0 3.3 %collective-permute-done.7.other = f32[3,4,16,128]{3,2,1,0:T(8,128)S(1)} collective-permute-done((f32[3,4,16,128]{3,2,1,0:T(8,128)S(1)}, f32[3,4,16,128]{3,2,1,0:T(8,128)S(1)}, u32[]{:S(2)}, u32[]{:S(2)}) %collective-permute-start.7) | collective-permute-done | bytes 98336 | tf_op jit(solution)/shard_map/ppermute | solution.py:456
  45.3 0.7 %shard_map.180 = (f32[4,16,128]{2,1,0:T(8,128)}, f32[4,16,128]{2,1,0:T(8,128)}) custom-call(f32[3,4,16,128]{3,2,1,0:T(8,128)S(1)} %add.3.own, f32[3,4,16,128]{3,2,1,0:T(8,128)S(1)} %collective-permute-done.7.other), custom_call_target="tpu_custom_call" | custom-call | flops 2000000 | bytes 2000000 | tf_op jit(solution)/shard_map/pallas_call | solution.py:23
  (2 shorter events, 0.1 us)
Async XLA Ops:
  1.9 13.5 %collective-permute-start = (f32[34,16,128]{2,1,0:T(8,128)S(1)}, f32[34,16,128]{2,1,0:T(8,128)S(1)}, u32[]{:S(2)}, u32[]{:S(2)}) collective-permute-start(f32[34,16,128]{2,1,0:T(8,128)S(1)} %get-tuple-element.19), channel_id=1, source_target_pairs={{8,16},{24,32},{40,48},{56,64},{72,80},{88,96},{104,112},{120,128}... | collective-permute-start | bytes 835592 | tf_op jit(solution)/shard_map/ppermute | solution.py:396
  8.3 7.2 %collective-permute-start.1 = (f32[34,16,128]{2,1,0:T(8,128)S(1)}, f32[34,16,128]{2,1,0:T(8,128)S(1)}, u32[]{:S(2)}, u32[]{:S(2)}) collective-permute-start(f32[34,16,128]{2,1,0:T(8,128)S(1)} %get-tuple-element.20), channel_id=1, source_target_pairs={{0,8},{16,24},{32,40},{48,56},{64,72},{80,88},{96,104},{112,120},{... | collective-permute-start | bytes 835592 | tf_op jit(solution)/shard_map/ppermute | solution.py:396
  15.5 6.7 %copy-start = (f32[1,2,2048]{2,1,0:T(2,128)S(1)}, f32[1,2,2048]{2,1,0:T(2,128)}, u32[]{:S(2)}) copy-start(f32[1,2,2048]{2,1,0:T(2,128)} %param.26) | copy-start | bytes 49156
  15.5 6.7 %copy-start.1 = (f32[1,2,2048]{2,1,0:T(2,128)S(1)}, f32[1,2,2048]{2,1,0:T(2,128)}, u32[]{:S(2)}) copy-start(f32[1,2,2048]{2,1,0:T(2,128)} %param.28) | copy-start | bytes 49156
  15.5 6.8 %copy-start.3 = (s32[2048]{0:T(1024)S(1)}, s32[2048]{0:T(1024)}, u32[]{:S(2)}) copy-start(s32[2048]{0:T(1024)} %param.27) | copy-start | bytes 24580
  15.5 6.7 %copy-start.2 = (s32[1,2048]{1,0:T(1,128)S(1)}, s32[1,2048]{1,0:T(1,128)}, u32[]{:S(2)}) copy-start(s32[1,2048]{1,0:T(1,128)} %recv_cells.1) | copy-start | bytes 24580
  15.6 8.6 %collective-permute-start.2 = (f32[14,8,128]{2,1,0:T(8,128)S(1)}, f32[14,8,128]{2,1,0:T(8,128)S(1)}, u32[]{:S(2)}, u32[]{:S(2)}) collective-permute-start(f32[14,8,128]{2,1,0:T(8,128)S(1)} %get-tuple-element.21), channel_id=1, source_target_pairs={{1,2},{3,4},{5,6},{2,1},{4,3},{6,5},{9,10},{11,12},{13,14},{10,9},... | collective-permute-start | bytes 172040 | tf_op jit(solution)/shard_map/ppermute | solution.py:396
  16.2 7.9 %collective-permute-start.3 = (f32[14,8,128]{2,1,0:T(8,128)S(1)}, f32[14,8,128]{2,1,0:T(8,128)S(1)}, u32[]{:S(2)}, u32[]{:S(2)}) collective-permute-start(f32[14,8,128]{2,1,0:T(8,128)S(1)} %get-tuple-element.22), channel_id=1, source_target_pairs={{0,1},{2,3},{4,5},{6,7},{1,0},{3,2},{5,4},{7,6},{8,9},{10,11},{12,... | collective-permute-start | bytes 172040 | tf_op jit(solution)/shard_map/ppermute | solution.py:396
  24.7 11.8 %collective-permute-start.6 = (f32[3,4,16,128]{3,2,1,0:T(8,128)S(1)}, f32[3,4,16,128]{3,2,1,0:T(8,128)S(1)}, u32[]{:S(2)}, u32[]{:S(2)}) collective-permute-start(f32[3,4,16,128]{3,2,1,0:T(8,128)S(1)} %shard_map.177), channel_id=1, source_target_pairs={{0,256},{256,0},{512,768},{768,512},{1,257},{257,1},{513,769},{769... | collective-permute-start | bytes 294920 | tf_op jit(solution)/shard_map/ppermute | solution.py:454
  28.6 9.8 %collective-permute-start.4 = (f32[40,8,128]{2,1,0:T(8,128)S(1)}, f32[40,8,128]{2,1,0:T(8,128)S(1)}, u32[]{:S(2)}, u32[]{:S(2)}) collective-permute-start(f32[40,8,128]{2,1,0:T(8,128)S(1)} %get-tuple-element.25), channel_id=1, source_target_pairs={{1,2},{3,4},{5,6},{2,1},{4,3},{6,5},{9,10},{11,12},{13,14},{10,9},... | collective-permute-start | bytes 491528 | tf_op jit(solution)/shard_map/ppermute | solution.py:396
  29.3 11.1 %collective-permute-start.5 = (f32[40,8,128]{2,1,0:T(8,128)S(1)}, f32[40,8,128]{2,1,0:T(8,128)S(1)}, u32[]{:S(2)}, u32[]{:S(2)}) collective-permute-start(f32[40,8,128]{2,1,0:T(8,128)S(1)} %get-tuple-element.26), channel_id=1, source_target_pairs={{0,1},{2,3},{4,5},{6,7},{1,0},{3,2},{5,4},{7,6},{8,9},{10,11},{12,... | collective-permute-start | bytes 491528 | tf_op jit(solution)/shard_map/ppermute | solution.py:396
  36.5 8.8 %collective-permute-start.7 = (f32[3,4,16,128]{3,2,1,0:T(8,128)S(1)}, f32[3,4,16,128]{3,2,1,0:T(8,128)S(1)}, u32[]{:S(2)}, u32[]{:S(2)}) collective-permute-start(f32[3,4,16,128]{3,2,1,0:T(8,128)S(1)} %add.3.own), channel_id=1, source_target_pairs={{0,768},{256,512},{512,256},{768,0},{1,769},{257,513},{513,257},{7... | collective-permute-start | bytes 294920 | tf_op jit(solution)/shard_map/ppermute | solution.py:456

commit v6 on v5

--- a/solution.py
+++ b/solution.py
@@ -8,9 +8,10 @@
 from jax.sharding import PartitionSpec as P
 
 TAPER = 32
-WIDE = 5
-NARROW = 7
-FIELDS = WIDE + NARROW + 2
+EDGE = 5
+BOTH = 7
+ALONG = 12
+FIELDS = 14
 INPUTS = ("p", "q", "p_old", "q_old", "f", "c", "eps", "delta", "tilt", "azimuth")
 PAIRS = ((0, 0), (1, 1), (2, 2), (0, 1), (0, 2), (1, 2))
 
@@ -151,55 +152,47 @@
     p_weight = speed * (1.0 + 2.0 * eps[...])
     q_weight = speed * (1.0 + 2.0 * delta[...])
     sine = jnp.sin(tilt[...])
-    wide = (
+    fields = (
         p_weight * p_now + q_weight * q_now,
         speed * (p_now + q_now),
         sine * jnp.cos(azimuth[...]),
         sine * jnp.sin(azimuth[...]),
         jnp.cos(tilt[...]),
-    )
-    narrow = (
+        f[0],
+        f[1],
         2.0 * p_now - p_old[...],
         2.0 * q_now - q_old[...],
         p_weight,
         q_weight,
         speed,
-        f[0],
-        f[1],
-    )
-    for number, cells in enumerate(wide):
-        rows = slice(number * size_x, (number + 1) * size_x)
-        loc[rows] = cells
-        near[rows] = cells
-        far[rows] = cells
-    for number, cells in enumerate(narrow + (p_now, q_now)):
-        start = (WIDE + number) * size_x
-        loc[start : start + size_x] = cells
+        p_now,
+        q_now,
+    )
+    for number, cells in enumerate(fields):
+        loc[number * size_x : (number + 1) * size_x] = cells
+    send_x(loc, near, far, BOTH, size_x)
+
+
+def send_x(loc, near, far, count, size_x):
     odd = lax.rem(lax.axis_index("gx"), 2)
     upper, lower = (1 - odd) * (size_x - 2), odd * (size_x - 2)
-    for number in range(NARROW):
-        start = (WIDE + number) * size_x
-        begin = WIDE * size_x + 2 * number
-        near[begin : begin + 2] = loc[pl.ds(start + upper, 2)]
-        far[begin : begin + 2] = loc[pl.ds(start + lower, 2)]
-
-
-def tiles_of(loc, near, far, size_x, part):
+    for number in range(count):
+        rows = slice(2 * number, 2 * number + 2)
+        near[rows] = loc[pl.ds(number * size_x + upper, 2)]
+        far[rows] = loc[pl.ds(number * size_x + lower, 2)]
+
+
+def with_rows(loc, near, far, count, size_x, part):
     ys = slice(8 * part, 8 * part + 8)
     odd = lax.rem(lax.axis_index("gx"), 2) == 1
     first, second = near[:, ys, :], far[:, ys, :]
     below, above = jnp.where(odd, first, second), jnp.where(odd, second, first)
-    wide, narrow = [], []
-    for number in range(WIDE):
-        rows = slice(number * size_x, (number + 1) * size_x)
-        wide.append(jnp.concatenate([below[rows], loc[rows, ys, :], above[rows]], axis=0))
-    for number in range(NARROW):
-        start = (WIDE + number) * size_x
-        begin = WIDE * size_x + 2 * number
-        rows = slice(begin, begin + 2)
-        here = loc[start : start + size_x, ys, :]
-        narrow.append(jnp.concatenate([below[rows], here, above[rows]], axis=0))
-    return wide, narrow
+    out = []
+    for number in range(count):
+        rows = slice(2 * number, 2 * number + 2)
+        here = loc[number * size_x : (number + 1) * size_x, ys, :]
+        out.append(jnp.concatenate([below[rows], here, above[rows]], axis=0))
+    return out
 
 
 def turn(rows, by):
@@ -227,10 +220,6 @@
     return jnp.concatenate(edges, axis=0)
 
 
-def early_rows(wide, narrow):
-    return [tile[2 : tile.shape[0] - 2] for tile in wide] + narrow[5:]
-
-
 def send_both(parts, evens, odds, start):
     odd = lax.rem(lax.axis_index("gy"), 2) == 1
     rows = slice(start, start + parts[0].shape[0])
@@ -243,24 +232,39 @@
     return jnp.where(odd, odds[...], evens[...]), jnp.where(odd, evens[...], odds[...])
 
 
-def early_kernel(loc, far, near, odds, evens):
+def pack_kernel(loc, far, near, odds, evens):
     size_x = loc.shape[0] // FIELDS
-    parts = []
+    groups = ([], [], [])
     for part in range(2):
-        wide, narrow = tiles_of(loc, near, far, size_x, part)
-        parts.append(pack(jnp.concatenate(early_rows(wide, narrow), axis=0), part, 4))
-    send_both(parts, evens, odds, 0)
-
-
-def late_kernel(loc, far, near, odds, evens):
+        ys = slice(8 * part, 8 * part + 8)
+        tiles = with_rows(loc, near, far, BOTH, size_x, part)
+        groups[0].append(pack(jnp.concatenate(tiles[:EDGE], axis=0), part, 2))
+        groups[1].append(pack(jnp.concatenate(tiles[EDGE:], axis=0), part, 4))
+        groups[2].append(pack(loc[BOTH * size_x : ALONG * size_x, ys, :], part, 4))
+    start = 0
+    for parts in groups:
+        send_both(parts, evens, odds, start)
+        start += parts[0].shape[0]
+
+
+def fields_of(loc, far, near, odds, evens, every):
     size_x = loc.shape[0] // FIELDS
-    wides, narrows = [], []
-    for part in range(2):
-        wide, narrow = tiles_of(loc, near, far, size_x, part)
-        wides.append(pack(jnp.concatenate(wide, axis=0), part, 2))
-        narrows.append(pack(jnp.concatenate(narrow[:5], axis=0), part, 4))
-    send_both(wides, evens, odds, 0)
-    send_both(narrows, evens, odds, wides[0].shape[0])
+    count = size_x + 4
+    high, low = from_both(evens, odds)
+    ends = (EDGE * count // 2, EDGE * count // 2 + (BOTH - EDGE) * count // 4)
+    edge = cut(unpack(high[: ends[0]], low[: ends[0]], 2), count)
+    tiles = [with_rows(loc, near, far, BOTH if every else EDGE, size_x, part) for part in range(2)]
+    if every:
+        edge += cut(unpack(high[ends[0] : ends[1]], low[ends[0] : ends[1]], 4), count)
+    fields = [[tiles[0][n], tiles[1][n], edge[n]] for n in range(len(edge))]
+    along = []
+    if every:
+        edge = cut(unpack(high[ends[1] :], low[ends[1] :], 4), size_x)
+        for number in range(ALONG - BOTH):
+            rows = loc[(BOTH + number) * size_x : (BOTH + number + 1) * size_x]
+            along.append([rows[:, 0:8], rows[:, 8:16], edge[number]])
+    products = [[fields[2 + a][i] * fields[2 + b][i] for i in range(3)] for a, b in PAIRS]
+    return fields, along, products
 
 
 def cut(rows, count):
@@ -271,7 +275,7 @@
     bits_y, bits_z = grid_y.bit_length() - 1, grid_z.bit_length() - 1
     start_x = lax.axis_index("gx") * size_x
     start_y = lax.axis_index("gy") * size_y
-    ring = (size_x + 4) * 24
+    ring = size_x * 24
     inner = size_x * size_y
     chunk = 512
     total = jnp.zeros((3 * (ring + inner), grid_z), jnp.float32)
@@ -282,9 +286,9 @@
             depth = cells & (grid_z - 1) if shift else jnp.zeros_like(cells)
             cell_x = (across >> bits_y) - start_x
             cell_y = (across & (grid_y - 1)) - start_y
-            near = (cell_x >= -2) & (cell_x < size_x + 2) & (cell_y >= -2) & (cell_y < size_y + 2)
+            near = (cell_x >= 0) & (cell_x < size_x) & (cell_y >= -2) & (cell_y < size_y + 2)
             wrapped = jnp.where(cell_y < 0, cell_y + 24, cell_y)
-            ring_row = jnp.where(near, (cell_x + 2) * 24 + wrapped, -1)
+            ring_row = jnp.where(near, cell_x * 24 + wrapped, -1)
             inside = (cell_x >= 0) & (cell_x < size_x) & (cell_y >= 0) & (cell_y < size_y)
             inner_row = jnp.where(inside, cell_x * size_y + cell_y, -1)
             ring_hit = lax.broadcasted_iota(jnp.int32, (ring, chunk), 0) == ring_row
@@ -314,74 +318,57 @@
     out[...] = total[0:rows] + total[rows : 2 * rows] + total[2 * rows : 3 * rows]
 
 
-def first_step_kernel(grid_y, source, loc, far_x, near_x, odds, evens, inject, grads):
-    size_x, size_y = loc.shape[0] // FIELDS, loc.shape[1]
-    count = size_x + 4
-    high, low = from_both(evens, odds)
-    edge = cut(unpack(high, low, 4), count)
-    middle = [early_rows(*tiles_of(loc, near_x, far_x, size_x, part)) for part in range(2)]
-    fields = [[middle[0][n], middle[1][n], edge[n]] for n in range(len(edge))]
-    products = [[fields[2 + a][i] * fields[2 + b][i] for i in range(3)] for a, b in PAIRS]
+def first_step_kernel(grid_y, source, loc, far, near, odds, evens, inject, grads, now, ahead, near_next, far_next):
+    size_x = loc.shape[0] // FIELDS
+    fields, along, products = fields_of(loc, far, near, odds, evens, True)
+    p_base, q_base, p_weight, q_weight, speed = along
     mid = slice(2, 2 + size_x)
-    p_next = adjoint(products, fields[0], size_x, 2, False)
-    q_next = adjoint(products, fields[1], size_x, 2, True)
+    p_next = adjoint(products, fields[0], size_x, 3, False)
+    q_next = adjoint(products, fields[1], size_x, 3, True)
     inner = [[tile[mid] for tile in entry] for entry in products]
-    images = [forward_image(inner, field, size_x) for field in fields[5:7]]
-    ring = inject[0 : count * 24].reshape(count, 24, 128)
+    images = [forward_image(inner, field, size_x) for field in fields[EDGE:BOTH]]
+    ring = inject[0 : size_x * 24].reshape(size_x, 24, 128)
+    p_next = [p_base[i] + p_next[i] + ring[:, 8 * i : 8 * i + 8] for i in range(3)]
+    q_next = [q_base[i] + q_next[i] for i in range(3)]
+    for i in range(3):
+        ys = slice(8 * i, 8 * i + 8)
+        ahead[0:size_x, ys, :] = p_weight[i] * p_next[i] + q_weight[i] * q_next[i]
+        ahead[size_x : 2 * size_x, ys, :] = speed[i] * (p_next[i] + q_next[i])
+    send_x(ahead, near_next, far_next, 2, size_x)
     bits_y = grid_y.bit_length() - 1
     source_x = (source[0] >> bits_y) - lax.axis_index("gx") * size_x
-    source_y = (source[0] & (grid_y - 1)) - lax.axis_index("gy") * size_y
+    source_y = (source[0] & (grid_y - 1)) - lax.axis_index("gy") * loc.shape[1]
     shape = (size_x, 8, 128)
     offset_x = lax.broadcasted_iota(jnp.int32, shape, 0) - source_x
-
-    def block(field, ys):
-        return loc[field * size_x : (field + 1) * size_x, ys, :]
-
     for i in range(2):
         ys = slice(8 * i, 8 * i + 8)
         offset_y = lax.broadcasted_iota(jnp.int32, shape, 1) + (8 * i - source_y)
         squared = (offset_x * offset_x + offset_y * offset_y).astype(jnp.float32)
         taper = jnp.minimum(squared * (1.0 / float(TAPER * TAPER)), 1.0)
-        scale = taper * (2.0 * block(WIDE + 4, ys))
+        scale = taper * (2.0 * speed[i])
         image0, image1 = scale * images[0][i], scale * images[1][i]
-        p_mid = block(WIDE, ys) + p_next[i] + ring[mid, ys, :]
-        q_mid = block(WIDE + 1, ys) + q_next[i]
-        grads[0, :, ys, :] = block(FIELDS - 2, ys) * image0 + p_mid * image1
-        grads[1, :, ys, :] = block(FIELDS - 1, ys) * image0 + q_mid * image1
-        f0, f1 = block(WIDE + 5, ys), block(WIDE + 6, ys)
+        p, q = [loc[n * size_x : (n + 1) * size_x, ys, :] for n in (FIELDS - 2, FIELDS - 1)]
+        f0, f1 = fields[EDGE][i][mid], fields[EDGE + 1][i][mid]
+        grads[0, :, ys, :] = p * image0 + p_next[i] * image1
+        grads[1, :, ys, :] = q * image0 + q_next[i] * image1
         grads[2, :, ys, :] = f0 * f0 + f1 * f1
-
-
-def second_step_kernel(loc, far_x, near_x, odds, evens, inject, p_out, q_out):
+        now[0, :, ys, :] = p_next[i]
+        now[1, :, ys, :] = q_next[i]
+
+
+def second_step_kernel(loc, far, near, odds, evens, now, ahead, far_next, near_next, inject, p_out, q_out):
     size_x, size_y = p_out.shape[0], p_out.shape[1]
-    count = size_x + 4
-    high, low = from_both(evens, odds)
-    half = WIDE * (size_x + 8) // 2
-    wide_edge = cut(unpack(high[:half], low[:half], 2), size_x + 8)
-    narrow_edge = cut(unpack(high[half:], low[half:], 4), count)
-    parts = [tiles_of(loc, near_x, far_x, size_x, part) for part in range(2)]
-    wide = [[parts[0][0][n], parts[1][0][n], wide_edge[n]] for n in range(WIDE)]
-    narrow = [[parts[0][1][n], parts[1][1][n], narrow_edge[n]] for n in range(5)]
-    products = [[wide[2 + a][i] * wide[2 + b][i] for i in range(3)] for a, b in PAIRS]
-    p_base, q_base, p_weight, q_weight, speed = narrow
-    mid = slice(2, 2 + size_x)
-    p_next = adjoint(products, wide[0], count, 3, False)
-    q_next = adjoint(products, wide[1], count, 3, True)
-    ring = inject[0 : count * 24].reshape(count, 24, 128)
-    p_next = [p_base[i] + p_next[i] + ring[:, 8 * i : 8 * i + 8] for i in range(3)]
-    q_next = [q_base[i] + q_next[i] for i in range(3)]
-    source = [p_weight[i] * p_next[i] + q_weight[i] * q_next[i] for i in range(3)]
-    mix = [speed[i] * (p_next[i] + q_next[i]) for i in range(3)]
-    products = [[tile[2 : 2 + count] for tile in entry] for entry in products]
-    p_last = adjoint(products, source, size_x, 2, False)
-    q_last = adjoint(products, mix, size_x, 2, True)
-    inner = inject[count * 24 :].reshape(size_x, size_y, 128)
+    _, _, products = fields_of(loc, far, near, odds, evens, False)
+    tiles = [with_rows(ahead, near_next, far_next, 2, size_x, part) for part in range(3)]
+    p_last = adjoint(products, [tile[0] for tile in tiles], size_x, 2, False)
+    q_last = adjoint(products, [tile[1] for tile in tiles], size_x, 2, True)
+    inner = inject[size_x * 24 :].reshape(size_x, size_y, 128)
     p = loc[(FIELDS - 2) * size_x : (FIELDS - 1) * size_x]
     q = loc[(FIELDS - 1) * size_x : FIELDS * size_x]
     for i in range(2):
         ys = slice(8 * i, 8 * i + 8)
-        p_out[:, ys, :] = 2.0 * p_next[i][mid] - p[:, ys] + inner[:, ys] + p_last[i]
-        q_out[:, ys, :] = 2.0 * q_next[i][mid] - q[:, ys] + q_last[i]
+        p_out[:, ys, :] = 2.0 * now[0, :, ys, :] - p[:, ys] + inner[:, ys] + p_last[i]
+        q_out[:, ys, :] = 2.0 * now[1, :, ys, :] - q[:, ys] + q_last[i]
 
 
 def finish_kernel(own, other, grad_e, grad_d):
@@ -418,7 +405,7 @@
     p, q, p_old, q_old, f = (
         entry[0] for entry in (p_adjoint, q_adjoint, p_previous, q_previous, forward_p)
     )
-    message = WIDE * size_x + NARROW * 2
+    message = 2 * BOTH
     inputs = (p, q, p_old, q_old, f, courant, epsilon, delta_field, tilt_angle, azimuth)
     loc, far, near = call(
         prepare_kernel,
@@ -430,34 +417,38 @@
     )
     far = swap(far, "gx", 1)
     near = swap(near, "gx", 0)
-    rows = (size_x + 4) * 24 + size_x * size_y
+    rows = size_x * 24 + size_x * size_y
     (inject,) = call(
         functools.partial(inject_kernel, grid_y, size_z, size_x, size_y),
         [(rows, size_z)],
         (receiver_cells, receiver_values[0], boundary_cells[None], boundary_force[0]),
         flops=800_000_000,
     )
-    edges = (loc, far, near)
-    early = (WIDE + 2) * (size_x + 4) // 4
-    late = WIDE * (size_x + 8) // 2 + 5 * (size_x + 4) // 4
-    odds, evens = call(early_kernel, [(early, 8, size_z)] * 2, edges)
+    count = EDGE * (size_x + 4) // 2 + (BOTH - EDGE) * (size_x + 4) // 4 + (ALONG - BOTH) * size_x // 4
+    odds, evens = call(pack_kernel, [(count, 8, size_z)] * 2, (loc, far, near))
     odds, evens = swap(odds, "gy", 1), swap(evens, "gy", 0)
-    late_odds, late_evens = call(late_kernel, [(late, 8, size_z)] * 2, edges)
-    (grads,) = call(
+    edges = (loc, far, near, odds, evens)
+    grads, now, ahead, near_next, far_next = call(
         functools.partial(first_step_kernel, grid_y),
-        [(3, size_x, size_y, size_z)],
-        (source_cells, *edges, odds, evens, inject),
+        [
+            (3, size_x, size_y, size_z),
+            (2, size_x, size_y, size_z),
+            (2 * size_x, 24, size_z),
+            (4, 24, size_z),
+            (4, 24, size_z),
+        ],
+        (source_cells, *edges, inject),
         smem=(0,),
     )
-    grads, late_odds, late_evens = lax.optimization_barrier((grads, late_odds, late_evens))
     shots = range(lax.axis_size("shot"))
     grads = grads + lax.ppermute(grads, "shot", [(i, i ^ 1) for i in shots])
-    late_odds, late_evens = swap(late_odds, "gy", 1), swap(late_evens, "gy", 0)
+    far_next, near_next = swap(far_next, "gx", 1), swap(near_next, "gx", 0)
+    grads, far_next, near_next = lax.optimization_barrier((grads, far_next, near_next))
     other = lax.ppermute(grads, "shot", [(i, i ^ 3) for i in shots])
     p_final, q_final = call(
         second_step_kernel,
         [(size_x, size_y, size_z)] * 2,
-        (*edges, late_odds, late_evens, inject),
+        (*edges, now, ahead, far_next, near_next, inject),
         flops=20_000_000,
     )
     grad_e, grad_d = call(finish_kernel, [(size_x, size_y, size_z)] * 2, (grads, other))

time: 46.3 us -> 47.3 us (1.022)
  the two profiles are of different devices: /device:TPU:271 before, /device:TPU:435 now
where the time goes in v6:
time: 47.3 us; the launch traced here: 46.9 us
  starting transfers between devices  32.3 us (68%)
  waiting for transfers between devices  8.35 us (18%)
  Pallas kernels  4.77 us (10%)
  between operations  1.44 us (3%)
    ppermute x6, starting transfers between devices, swap(): lax.ppermute(part, axis, [(i, i + 1) for i in lows] + [(i + 1, i) for i i...  23 us
    ppermute x1, starting transfers between devices, body(): other = lax.ppermute(grads, 'shot', [(i, i ^ 3) for i in shots])  5.25 us
    ppermute x6, waiting for transfers between devices, swap(): lax.ppermute(part, axis, [(i, i + 1) for i in lows] + [(i + 1, i) for i i...  4.9 us
    pallas_call x6, Pallas kernels, call(): pl.pallas_call(kernel, out_shape=shapes, in_specs=specs, out_specs=[pl.Bl...  4.77 us
    ppermute x1, starting transfers between devices, body(): grads = grads + lax.ppermute(grads, 'shot', [(i, i ^ 1) for i in shots])  4.05 us
    ppermute x1, waiting for transfers between devices, body(): other = lax.ppermute(grads, 'shot', [(i, i ^ 3) for i in shots])  3.45 us
  transfers between devices with their start and end apart: 8, of which 5 were waited for; matrix products, arithmetic and copies ran while one was open for 0% of the time, Pallas kernels for 4%

profile of v6, /device:TPU:435, one launch (start us, length us, event | category | flops | bytes accessed | tf_op | source)
XLA Modules:
  0.0 46.9 jit_solution(7084819758093739470)
XLA Ops:
  0.6 1.3 %shard_map.174 = (f32[56,16,128]{2,1,0:T(8,128)S(1)}, f32[14,16,128]{2,1,0:T(8,128)S(1)}, f32[14,16,128]{2,1,0:T(8,128)S(1)}) custom-call(f32[4,16,128]{2,1,0:T(8,128)} %bitcast.14, f32[4,16,128]{2,1,0:T(8,128)} %bitcast.15, f32[4,16,128]{2,1,0:T(8,128)} %bitcast.16, f32[4,16,128]{2,1,0:T(8,128)} %bitcast.17, f32[2,4,16,128]{3,2,1,0:T(8,128)} %bitcast.13, ...), custom_call_target="tpu_custom_call" | custom-call | flops 2000000 | bytes 2000000 | tf_op jit(solution)/shard_map/pallas_call | solution.py:24
  1.9 6.6 %collective-permute-start = (f32[14,16,128]{2,1,0:T(8,128)S(1)}, f32[14,16,128]{2,1,0:T(8,128)S(1)}, u32[]{:S(2)}, u32[]{:S(2)}) collective-permute-start(f32[14,16,128]{2,1,0:T(8,128)S(1)} %get-tuple-element.22), channel_id=1, source_target_pairs={{8,16},{24,32},{40,48},{56,64},{72,80},{88,96},{104,112},{120,128}... | collective-permute-start | bytes 344072 | tf_op jit(solution)/shard_map/ppermute | solution.py:383
  8.6 1.9 %collective-permute-start.1 = (f32[14,16,128]{2,1,0:T(8,128)S(1)}, f32[14,16,128]{2,1,0:T(8,128)S(1)}, u32[]{:S(2)}, u32[]{:S(2)}) collective-permute-start(f32[14,16,128]{2,1,0:T(8,128)S(1)} %get-tuple-element.23), channel_id=1, source_target_pairs={{0,8},{16,24},{32,40},{48,56},{64,72},{80,88},{96,104},{112,120},{... | collective-permute-start | bytes 344072 | tf_op jit(solution)/shard_map/ppermute | solution.py:383
  10.5 0.9 %collective-permute-done.far = f32[14,16,128]{2,1,0:T(8,128)S(1)} collective-permute-done((f32[14,16,128]{2,1,0:T(8,128)S(1)}, f32[14,16,128]{2,1,0:T(8,128)S(1)}, u32[]{:S(2)}, u32[]{:S(2)}) %collective-permute-start) | collective-permute-done | bytes 114720 | tf_op jit(solution)/shard_map/ppermute | solution.py:383
  11.4 0.4 collective-permute-done.1.near
  11.8 0.0 copy-start
  11.8 0.0 copy-start.1
  11.8 0.0 copy-start.3
  11.8 0.1 shard_map.175
  11.9 0.0 copy-start.2
  11.9 4.5 %collective-permute-start.2 = (f32[29,8,128]{2,1,0:T(8,128)S(1)}, f32[29,8,128]{2,1,0:T(8,128)S(1)}, u32[]{:S(2)}, u32[]{:S(2)}) collective-permute-start(f32[29,8,128]{2,1,0:T(8,128)S(1)} %get-tuple-element.24), channel_id=1, source_target_pairs={{1,2},{3,4},{5,6},{2,1},{4,3},{6,5},{9,10},{11,12},{13,14},{10,9},... | collective-permute-start | bytes 356360 | tf_op jit(solution)/shard_map/ppermute | solution.py:383
  16.4 1.9 %collective-permute-start.3 = (f32[29,8,128]{2,1,0:T(8,128)S(1)}, f32[29,8,128]{2,1,0:T(8,128)S(1)}, u32[]{:S(2)}, u32[]{:S(2)}) collective-permute-start(f32[29,8,128]{2,1,0:T(8,128)S(1)} %get-tuple-element.25), channel_id=1, source_target_pairs={{0,1},{2,3},{4,5},{6,7},{1,0},{3,2},{5,4},{7,6},{8,9},{10,11},{12,... | collective-permute-start | bytes 356360 | tf_op jit(solution)/shard_map/ppermute | solution.py:383
  19.0 0.0 copy-done
  19.0 0.0 copy-done.1
  19.0 0.0 copy-done.3
  19.0 0.0 copy-done.2
  19.1 1.2 %shard_map.176.inject = f32[160,128]{1,0:T(8,128)S(1)} custom-call(s32[1,2048]{1,0:T(1,128)S(1)} %copy-done.2, f32[2,2048]{1,0:T(2,128)S(1)} %bitcast.10, s32[1,2048]{1,0:T(1,128)S(1)} %bitcast.12, f32[2,2048]{1,0:T(2,128)S(1)} %bitcast.11), custom_call_target="tpu_custom_call" | custom-call | flops 800000000 | bytes 2000000 | tf_op jit(solution)/shard_map/pallas_call | solution.py:24
  20.2 0.0 collective-permute-done.2.odds
  20.2 2.4 %collective-permute-done.3.evens = f32[29,8,128]{2,1,0:T(8,128)S(1)} collective-permute-done((f32[29,8,128]{2,1,0:T(8,128)S(1)}, f32[29,8,128]{2,1,0:T(8,128)S(1)}, u32[]{:S(2)}, u32[]{:S(2)}) %collective-permute-start.3) | collective-permute-done | bytes 118816 | tf_op jit(solution)/shard_map/ppermute | solution.py:383
  22.7 0.7 %shard_map.177 = (f32[3,4,16,128]{3,2,1,0:T(8,128)S(1)}, f32[2,4,16,128]{3,2,1,0:T(8,128)S(1)}, f32[8,24,128]{2,1,0:T(8,128)S(1)}, f32[4,24,128]{2,1,0:T(8,128)S(1)}, f32[4,24,128]{2,1,0:T(8,128)S(1)}) custom-call(s32[1]{0:T(128)S(6)} %copy.19.source, f32[56,16,128]{2,1,0:T(8,128)S(1)} %get-tuple-element.21.loc, ...), custom_call_target="tpu_custom_call" | custom-call | flops 2000000 | bytes 2000000 | tf_op jit(solution)/shard_map/pallas_call | solution.py:24
  23.4 4.1 %collective-permute-start.4 = (f32[3,4,16,128]{3,2,1,0:T(8,128)S(1)}, f32[3,4,16,128]{3,2,1,0:T(8,128)S(1)}, u32[]{:S(2)}, u32[]{:S(2)}) collective-permute-start(f32[3,4,16,128]{3,2,1,0:T(8,128)S(1)} %get-tuple-element.28), channel_id=1, source_target_pairs={{0,256},{256,0},{512,768},{768,512},{1,257},{257,1},{513,769},{769... | collective-permute-start | bytes 294920 | tf_op jit(solution)/shard_map/ppermute | solution.py:444
  27.4 6.0 %collective-permute-start.5 = (f32[4,24,128]{2,1,0:T(8,128)S(1)}, f32[4,24,128]{2,1,0:T(8,128)S(1)}, u32[]{:S(2)}, u32[]{:S(2)}) collective-permute-start(f32[4,24,128]{2,1,0:T(8,128)S(1)} %get-tuple-element.29), channel_id=1, source_target_pairs={{8,16},{24,32},{40,48},{56,64},{72,80},{88,96},{104,112},{120,128}... | collective-permute-start | bytes 147464 | tf_op jit(solution)/shard_map/ppermute | solution.py:383
  33.5 1.9 %collective-permute-start.6 = (f32[4,24,128]{2,1,0:T(8,128)S(1)}, f32[4,24,128]{2,1,0:T(8,128)S(1)}, u32[]{:S(2)}, u32[]{:S(2)}) collective-permute-start(f32[4,24,128]{2,1,0:T(8,128)S(1)} %get-tuple-element.30), channel_id=1, source_target_pairs={{0,8},{16,24},{32,40},{48,56},{64,72},{80,88},{96,104},{112,120},{... | collective-permute-start | bytes 147464 | tf_op jit(solution)/shard_map/ppermute | solution.py:383
  35.4 0.0 collective-permute-done.4
  35.4 0.0 collective-permute-done.5.far_next
  35.5 1.1 %collective-permute-done.6.near_next = f32[4,24,128]{2,1,0:T(8,128)S(1)} collective-permute-done((f32[4,24,128]{2,1,0:T(8,128)S(1)}, f32[4,24,128]{2,1,0:T(8,128)S(1)}, u32[]{:S(2)}, u32[]{:S(2)}) %collective-permute-start.6) | collective-permute-done | bytes 49184 | tf_op jit(solution)/shard_map/ppermute | solution.py:383
  36.6 5.2 %collective-permute-start.7 = (f32[3,4,16,128]{3,2,1,0:T(8,128)S(1)}, f32[3,4,16,128]{3,2,1,0:T(8,128)S(1)}, u32[]{:S(2)}, u32[]{:S(2)}) collective-permute-start(f32[3,4,16,128]{3,2,1,0:T(8,128)S(1)} %add.3.own), channel_id=1, source_target_pairs={{0,768},{256,512},{512,256},{768,0},{1,769},{257,513},{513,257},{7... | collective-permute-start | bytes 294920 | tf_op jit(solution)/shard_map/ppermute | solution.py:447
  41.9 0.9 %shard_map.178 = (f32[4,16,128]{2,1,0:T(8,128)}, f32[4,16,128]{2,1,0:T(8,128)}) custom-call(f32[56,16,128]{2,1,0:T(8,128)S(1)} %get-tuple-element.21.loc, f32[14,16,128]{2,1,0:T(8,128)S(1)} %collective-permute-done.far, f32[14,16,128]{2,1,0:T(8,128)S(1)} %collective-permute-done.1.near, f32[29,8,128]{2,1,0:T(8,128)S(1)} %collective-permute-done.2.odds, ...), custom_call_target="tpu_custom_call" | custom-call | flops 20000000 | bytes 2000000 | tf_op jit(solution)/shard_map/pallas_call | solution.py:24
  42.8 3.4 %collective-permute-done.7.other = f32[3,4,16,128]{3,2,1,0:T(8,128)S(1)} collective-permute-done((f32[3,4,16,128]{3,2,1,0:T(8,128)S(1)}, f32[3,4,16,128]{3,2,1,0:T(8,128)S(1)}, u32[]{:S(2)}, u32[]{:S(2)}) %collective-permute-start.7) | collective-permute-done | bytes 98336 | tf_op jit(solution)/shard_map/ppermute | solution.py:447
  46.2 0.7 %shard_map.179 = (f32[4,16,128]{2,1,0:T(8,128)}, f32[4,16,128]{2,1,0:T(8,128)}) custom-call(f32[3,4,16,128]{3,2,1,0:T(8,128)S(1)} %add.3.own, f32[3,4,16,128]{3,2,1,0:T(8,128)S(1)} %collective-permute-done.7.other), custom_call_target="tpu_custom_call" | custom-call | flops 2000000 | bytes 2000000 | tf_op jit(solution)/shard_map/pallas_call | solution.py:24
  (1 shorter events, 0.0 us)
Async XLA Ops:
  1.9 9.5 %collective-permute-start = (f32[14,16,128]{2,1,0:T(8,128)S(1)}, f32[14,16,128]{2,1,0:T(8,128)S(1)}, u32[]{:S(2)}, u32[]{:S(2)}) collective-permute-start(f32[14,16,128]{2,1,0:T(8,128)S(1)} %get-tuple-element.22), channel_id=1, source_target_pairs={{8,16},{24,32},{40,48},{56,64},{72,80},{88,96},{104,112},{120,128}... | collective-permute-start | bytes 344072 | tf_op jit(solution)/shard_map/ppermute | solution.py:383
  8.6 3.2 %collective-permute-start.1 = (f32[14,16,128]{2,1,0:T(8,128)S(1)}, f32[14,16,128]{2,1,0:T(8,128)S(1)}, u32[]{:S(2)}, u32[]{:S(2)}) collective-permute-start(f32[14,16,128]{2,1,0:T(8,128)S(1)} %get-tuple-element.23), channel_id=1, source_target_pairs={{0,8},{16,24},{32,40},{48,56},{64,72},{80,88},{96,104},{112,120},{... | collective-permute-start | bytes 344072 | tf_op jit(solution)/shard_map/ppermute | solution.py:383
  11.8 7.2 %copy-start = (f32[1,2,2048]{2,1,0:T(2,128)S(1)}, f32[1,2,2048]{2,1,0:T(2,128)}, u32[]{:S(2)}) copy-start(f32[1,2,2048]{2,1,0:T(2,128)} %param.26) | copy-start | bytes 49156
  11.8 7.2 %copy-start.1 = (f32[1,2,2048]{2,1,0:T(2,128)S(1)}, f32[1,2,2048]{2,1,0:T(2,128)}, u32[]{:S(2)}) copy-start(f32[1,2,2048]{2,1,0:T(2,128)} %param.28) | copy-start | bytes 49156
  11.8 7.2 %copy-start.3 = (s32[2048]{0:T(1024)S(1)}, s32[2048]{0:T(1024)}, u32[]{:S(2)}) copy-start(s32[2048]{0:T(1024)} %param.27) | copy-start | bytes 24580
  11.9 7.2 %copy-start.2 = (s32[1,2048]{1,0:T(1,128)S(1)}, s32[1,2048]{1,0:T(1,128)}, u32[]{:S(2)}) copy-start(s32[1,2048]{1,0:T(1,128)} %recv_cells.1) | copy-start | bytes 24580
  11.9 8.3 %collective-permute-start.2 = (f32[29,8,128]{2,1,0:T(8,128)S(1)}, f32[29,8,128]{2,1,0:T(8,128)S(1)}, u32[]{:S(2)}, u32[]{:S(2)}) collective-permute-start(f32[29,8,128]{2,1,0:T(8,128)S(1)} %get-tuple-element.24), channel_id=1, source_target_pairs={{1,2},{3,4},{5,6},{2,1},{4,3},{6,5},{9,10},{11,12},{13,14},{10,9},... | collective-permute-start | bytes 356360 | tf_op jit(solution)/shard_map/ppermute | solution.py:383
  16.4 6.3 %collective-permute-start.3 = (f32[29,8,128]{2,1,0:T(8,128)S(1)}, f32[29,8,128]{2,1,0:T(8,128)S(1)}, u32[]{:S(2)}, u32[]{:S(2)}) collective-permute-start(f32[29,8,128]{2,1,0:T(8,128)S(1)} %get-tuple-element.25), channel_id=1, source_target_pairs={{0,1},{2,3},{4,5},{6,7},{1,0},{3,2},{5,4},{7,6},{8,9},{10,11},{12,... | collective-permute-start | bytes 356360 | tf_op jit(solution)/shard_map/ppermute | solution.py:383
  23.4 12.0 %collective-permute-start.4 = (f32[3,4,16,128]{3,2,1,0:T(8,128)S(1)}, f32[3,4,16,128]{3,2,1,0:T(8,128)S(1)}, u32[]{:S(2)}, u32[]{:S(2)}) collective-permute-start(f32[3,4,16,128]{3,2,1,0:T(8,128)S(1)} %get-tuple-element.28), channel_id=1, source_target_pairs={{0,256},{256,0},{512,768},{768,512},{1,257},{257,1},{513,769},{769... | collective-permute-start | bytes 294920 | tf_op jit(solution)/shard_map/ppermute | solution.py:444
  27.4 8.0 %collective-permute-start.5 = (f32[4,24,128]{2,1,0:T(8,128)S(1)}, f32[4,24,128]{2,1,0:T(8,128)S(1)}, u32[]{:S(2)}, u32[]{:S(2)}) collective-permute-start(f32[4,24,128]{2,1,0:T(8,128)S(1)} %get-tuple-element.29), channel_id=1, source_target_pairs={{8,16},{24,32},{40,48},{56,64},{72,80},{88,96},{104,112},{120,128}... | collective-permute-start | bytes 147464 | tf_op jit(solution)/shard_map/ppermute | solution.py:383
  33.5 3.1 %collective-permute-start.6 = (f32[4,24,128]{2,1,0:T(8,128)S(1)}, f32[4,24,128]{2,1,0:T(8,128)S(1)}, u32[]{:S(2)}, u32[]{:S(2)}) collective-permute-start(f32[4,24,128]{2,1,0:T(8,128)S(1)} %get-tuple-element.30), channel_id=1, source_target_pairs={{0,8},{16,24},{32,40},{48,56},{64,72},{80,88},{96,104},{112,120},{... | collective-permute-start | bytes 147464 | tf_op jit(solution)/shard_map/ppermute | solution.py:383
  36.6 9.6 %collective-permute-start.7 = (f32[3,4,16,128]{3,2,1,0:T(8,128)S(1)}, f32[3,4,16,128]{3,2,1,0:T(8,128)S(1)}, u32[]{:S(2)}, u32[]{:S(2)}) collective-permute-start(f32[3,4,16,128]{3,2,1,0:T(8,128)S(1)} %add.3.own), channel_id=1, source_target_pairs={{0,768},{256,512},{512,256},{768,0},{1,769},{257,513},{513,257},{7... | collective-permute-start | bytes 294920 | tf_op jit(solution)/shard_map/ppermute | solution.py:447

commit v7 on v5

--- a/solution.py
+++ b/solution.py
@@ -314,7 +314,7 @@
     out[...] = total[0:rows] + total[rows : 2 * rows] + total[2 * rows : 3 * rows]
 
 
-def first_step_kernel(grid_y, source, loc, far_x, near_x, odds, evens, inject, grads):
+def first_step_kernel(grid_y, source, loc, far_x, near_x, evens, odds, inject, grads):
     size_x, size_y = loc.shape[0] // FIELDS, loc.shape[1]
     count = size_x + 4
     high, low = from_both(evens, odds)
@@ -352,7 +352,7 @@
         grads[2, :, ys, :] = f0 * f0 + f1 * f1
 
 
-def second_step_kernel(loc, far_x, near_x, odds, evens, inject, p_out, q_out):
+def second_step_kernel(loc, far_x, near_x, evens, odds, inject, p_out, q_out):
     size_x, size_y = p_out.shape[0], p_out.shape[1]
     count = size_x + 4
     high, low = from_both(evens, odds)
@@ -446,7 +446,7 @@
     (grads,) = call(
         functools.partial(first_step_kernel, grid_y),
         [(3, size_x, size_y, size_z)],
-        (source_cells, *edges, odds, evens, inject),
+        (source_cells, *edges, evens, odds, inject),
         smem=(0,),
     )
     grads, late_odds, late_evens = lax.optimization_barrier((grads, late_odds, late_evens))
@@ -457,7 +457,7 @@
     p_final, q_final = call(
         second_step_kernel,
         [(size_x, size_y, size_z)] * 2,
-        (*edges, late_odds, late_evens, inject),
+        (*edges, late_evens, late_odds, inject),
         flops=20_000_000,
     )
     grad_e, grad_d = call(finish_kernel, [(size_x, size_y, size_z)] * 2, (grads, other))

time: 46.3 us -> 45.4 us (0.981)
  the two profiles are of different devices: /device:TPU:271 before, /device:TPU:287 now
where the time goes in v7:
time: 45.4 us; the launch traced here: 45 us
  starting transfers between devices  27.7 us (61%)
  waiting for transfers between devices  9.85 us (22%)
  Pallas kernels  5.99 us (13%)
  between operations  1.47 us (3%)
    ppermute x6, starting transfers between devices, swap(): lax.ppermute(part, axis, [(i, i + 1) for i in lows] + [(i + 1, i) for i i...  21.8 us
    ppermute x6, waiting for transfers between devices, swap(): lax.ppermute(part, axis, [(i, i + 1) for i in lows] + [(i + 1, i) for i i...  6.59 us
    pallas_call x7, Pallas kernels, call(): pl.pallas_call(kernel, out_shape=shapes, in_specs=specs, out_specs=[pl.Bl...  5.99 us
    ppermute x1, starting transfers between devices, body(): grads = grads + lax.ppermute(grads, 'shot', [(i, i ^ 1) for i in shots])  3.93 us
    ppermute x1, waiting for transfers between devices, body(): other = lax.ppermute(grads, 'shot', [(i, i ^ 3) for i in shots])  3.26 us
    ppermute x1, starting transfers between devices, body(): other = lax.ppermute(grads, 'shot', [(i, i ^ 3) for i in shots])  1.92 us
  transfers between devices with their start and end apart: 8, of which 3 were waited for; matrix products, arithmetic and copies ran while one was open for 0% of the time, Pallas kernels for 8%

profile of v7, /device:TPU:287, one launch (start us, length us, event | category | flops | bytes accessed | tf_op | source)
XLA Modules:
  0.0 45.0 jit_solution(15133024284835410075)
XLA Ops:
  0.6 1.3 %shard_map.174 = (f32[56,16,128]{2,1,0:T(8,128)S(1)}, f32[34,16,128]{2,1,0:T(8,128)S(1)}, f32[34,16,128]{2,1,0:T(8,128)S(1)}) custom-call(f32[4,16,128]{2,1,0:T(8,128)} %bitcast.14, f32[4,16,128]{2,1,0:T(8,128)} %bitcast.15, f32[4,16,128]{2,1,0:T(8,128)} %bitcast.16, f32[4,16,128]{2,1,0:T(8,128)} %bitcast.17, f32[2,4,16,128]{3,2,1,0:T(8,128)} %bitcast.13, ...), custom_call_target="tpu_custom_call" | custom-call | flops 2000000 | bytes 2000000 | tf_op jit(solution)/shard_map/pallas_call | solution.py:23
  1.9 6.3 %collective-permute-start = (f32[34,16,128]{2,1,0:T(8,128)S(1)}, f32[34,16,128]{2,1,0:T(8,128)S(1)}, u32[]{:S(2)}, u32[]{:S(2)}) collective-permute-start(f32[34,16,128]{2,1,0:T(8,128)S(1)} %get-tuple-element.19), channel_id=1, source_target_pairs={{8,16},{24,32},{40,48},{56,64},{72,80},{88,96},{104,112},{120,128}... | collective-permute-start | bytes 835592 | tf_op jit(solution)/shard_map/ppermute | solution.py:396
  8.3 1.9 %collective-permute-start.1 = (f32[34,16,128]{2,1,0:T(8,128)S(1)}, f32[34,16,128]{2,1,0:T(8,128)S(1)}, u32[]{:S(2)}, u32[]{:S(2)}) collective-permute-start(f32[34,16,128]{2,1,0:T(8,128)S(1)} %get-tuple-element.20), channel_id=1, source_target_pairs={{0,8},{16,24},{32,40},{48,56},{64,72},{80,88},{96,104},{112,120},{... | collective-permute-start | bytes 835592 | tf_op jit(solution)/shard_map/ppermute | solution.py:396
  10.9 4.6 %collective-permute-done.far.far_x = f32[34,16,128]{2,1,0:T(8,128)S(1)} collective-permute-done((f32[34,16,128]{2,1,0:T(8,128)S(1)}, f32[34,16,128]{2,1,0:T(8,128)S(1)}, u32[]{:S(2)}, u32[]{:S(2)}) %collective-permute-start) | collective-permute-done | bytes 278560 | tf_op jit(solution)/shard_map/ppermute | solution.py:396
  15.5 0.0 collective-permute-done.1.near.near_x
  15.5 0.0 copy-start
  15.5 0.0 copy-start.1
  15.5 0.0 copy-start.3
  15.5 0.0 copy-start.2
  15.6 2.0 %collective-permute-start.2 = (f32[14,8,128]{2,1,0:T(8,128)S(1)}, f32[14,8,128]{2,1,0:T(8,128)S(1)}, u32[]{:S(2)}, u32[]{:S(2)}) collective-permute-start(f32[14,8,128]{2,1,0:T(8,128)S(1)} %get-tuple-element.21), channel_id=1, source_target_pairs={{0,1},{2,3},{4,5},{6,7},{1,0},{3,2},{5,4},{7,6},{8,9},{10,11},{12,... | collective-permute-start | bytes 172040 | tf_op jit(solution)/shard_map/ppermute | solution.py:396
  17.5 4.7 %collective-permute-start.3 = (f32[14,8,128]{2,1,0:T(8,128)S(1)}, f32[14,8,128]{2,1,0:T(8,128)S(1)}, u32[]{:S(2)}, u32[]{:S(2)}) collective-permute-start(f32[14,8,128]{2,1,0:T(8,128)S(1)} %get-tuple-element.22), channel_id=1, source_target_pairs={{1,2},{3,4},{5,6},{2,1},{4,3},{6,5},{9,10},{11,12},{13,14},{10,9},... | collective-permute-start | bytes 172040 | tf_op jit(solution)/shard_map/ppermute | solution.py:396
  22.2 0.0 copy-done
  22.2 0.0 copy-done.1
  22.2 0.0 copy-done.3
  22.2 0.0 copy-done.2
  22.3 1.8 %shard_map.176.inject = f32[256,128]{1,0:T(8,128)S(1)} custom-call(s32[1,2048]{1,0:T(1,128)S(1)} %copy-done.2, f32[2,2048]{1,0:T(2,128)S(1)} %bitcast.10, s32[1,2048]{1,0:T(1,128)S(1)} %bitcast.12, f32[2,2048]{1,0:T(2,128)S(1)} %bitcast.11), custom_call_target="tpu_custom_call" | custom-call | flops 800000000 | bytes 2000000 | tf_op jit(solution)/shard_map/pallas_call | solution.py:23
  24.0 0.1 shard_map.178
  24.1 0.0 collective-permute-done.2.evens
  24.1 0.0 collective-permute-done.3.odds
  24.1 0.5 %shard_map.177 = f32[3,4,16,128]{3,2,1,0:T(8,128)S(1)} custom-call(s32[1]{0:T(128)S(6)} %copy.19.source, f32[56,16,128]{2,1,0:T(8,128)S(1)} %get-tuple-element.18.loc, f32[34,16,128]{2,1,0:T(8,128)S(1)} %collective-permute-done.far.far_x, f32[34,16,128]{2,1,0:T(8,128)S(1)} %collective-permute-done.1.near.near_x, ...), custom_call_target="tpu_custom_call" | custom-call | flops 2000000 | bytes 2000000 | tf_op jit(solution)/shard_map/pallas_call | solution.py:23
  24.7 3.9 %collective-permute-start.6 = (f32[3,4,16,128]{3,2,1,0:T(8,128)S(1)}, f32[3,4,16,128]{3,2,1,0:T(8,128)S(1)}, u32[]{:S(2)}, u32[]{:S(2)}) collective-permute-start(f32[3,4,16,128]{3,2,1,0:T(8,128)S(1)} %shard_map.177), channel_id=1, source_target_pairs={{0,256},{256,0},{512,768},{768,512},{1,257},{257,1},{513,769},{769... | collective-permute-start | bytes 294920 | tf_op jit(solution)/shard_map/ppermute | solution.py:454
  28.6 1.9 %collective-permute-start.4 = (f32[40,8,128]{2,1,0:T(8,128)S(1)}, f32[40,8,128]{2,1,0:T(8,128)S(1)}, u32[]{:S(2)}, u32[]{:S(2)}) collective-permute-start(f32[40,8,128]{2,1,0:T(8,128)S(1)} %get-tuple-element.25), channel_id=1, source_target_pairs={{0,1},{2,3},{4,5},{6,7},{1,0},{3,2},{5,4},{7,6},{8,9},{10,11},{12,... | collective-permute-start | bytes 491528 | tf_op jit(solution)/shard_map/ppermute | solution.py:396
  30.6 5.0 %collective-permute-start.5 = (f32[40,8,128]{2,1,0:T(8,128)S(1)}, f32[40,8,128]{2,1,0:T(8,128)S(1)}, u32[]{:S(2)}, u32[]{:S(2)}) collective-permute-start(f32[40,8,128]{2,1,0:T(8,128)S(1)} %get-tuple-element.26), channel_id=1, source_target_pairs={{1,2},{3,4},{5,6},{2,1},{4,3},{6,5},{9,10},{11,12},{13,14},{10,9},... | collective-permute-start | bytes 491528 | tf_op jit(solution)/shard_map/ppermute | solution.py:396
  35.6 0.0 collective-permute-done.6
  35.6 1.9 %collective-permute-start.7 = (f32[3,4,16,128]{3,2,1,0:T(8,128)S(1)}, f32[3,4,16,128]{3,2,1,0:T(8,128)S(1)}, u32[]{:S(2)}, u32[]{:S(2)}) collective-permute-start(f32[3,4,16,128]{3,2,1,0:T(8,128)S(1)} %add.3.own), channel_id=1, source_target_pairs={{0,768},{256,512},{512,256},{768,0},{1,769},{257,513},{513,257},{7... | collective-permute-start | bytes 294920 | tf_op jit(solution)/shard_map/ppermute | solution.py:456
  37.5 0.0 collective-permute-done.4.evens
  37.6 2.0 %collective-permute-done.5.odds = f32[40,8,128]{2,1,0:T(8,128)S(1)} collective-permute-done((f32[40,8,128]{2,1,0:T(8,128)S(1)}, f32[40,8,128]{2,1,0:T(8,128)S(1)}, u32[]{:S(2)}, u32[]{:S(2)}) %collective-permute-start.5) | collective-permute-done | bytes 163872 | tf_op jit(solution)/shard_map/ppermute | solution.py:396
  39.5 1.6 %shard_map.179 = (f32[4,16,128]{2,1,0:T(8,128)}, f32[4,16,128]{2,1,0:T(8,128)}) custom-call(f32[56,16,128]{2,1,0:T(8,128)S(1)} %get-tuple-element.18.loc, f32[34,16,128]{2,1,0:T(8,128)S(1)} %collective-permute-done.far.far_x, f32[34,16,128]{2,1,0:T(8,128)S(1)} %collective-permute-done.1.near.near_x, f32[40,8,128]{2,1,0:T(8,128)S(1)} %collective-permute-done.4.evens, ...), custom_call_target="tpu_custom_call" | custom-call | flops 20000000 | bytes 2000000 | tf_op jit(solution)/shard_map/pallas_call | solution.py:23
  41.1 3.3 %collective-permute-done.7.other = f32[3,4,16,128]{3,2,1,0:T(8,128)S(1)} collective-permute-done((f32[3,4,16,128]{3,2,1,0:T(8,128)S(1)}, f32[3,4,16,128]{3,2,1,0:T(8,128)S(1)}, u32[]{:S(2)}, u32[]{:S(2)}) %collective-permute-start.7) | collective-permute-done | bytes 98336 | tf_op jit(solution)/shard_map/ppermute | solution.py:456
  44.4 0.7 %shard_map.180 = (f32[4,16,128]{2,1,0:T(8,128)}, f32[4,16,128]{2,1,0:T(8,128)}) custom-call(f32[3,4,16,128]{3,2,1,0:T(8,128)S(1)} %add.3.own, f32[3,4,16,128]{3,2,1,0:T(8,128)S(1)} %collective-permute-done.7.other), custom_call_target="tpu_custom_call" | custom-call | flops 2000000 | bytes 2000000 | tf_op jit(solution)/shard_map/pallas_call | solution.py:23
  (2 shorter events, 0.1 us)
Async XLA Ops:
  1.9 13.5 %collective-permute-start = (f32[34,16,128]{2,1,0:T(8,128)S(1)}, f32[34,16,128]{2,1,0:T(8,128)S(1)}, u32[]{:S(2)}, u32[]{:S(2)}) collective-permute-start(f32[34,16,128]{2,1,0:T(8,128)S(1)} %get-tuple-element.19), channel_id=1, source_target_pairs={{8,16},{24,32},{40,48},{56,64},{72,80},{88,96},{104,112},{120,128}... | collective-permute-start | bytes 835592 | tf_op jit(solution)/shard_map/ppermute | solution.py:396
  8.3 7.2 %collective-permute-start.1 = (f32[34,16,128]{2,1,0:T(8,128)S(1)}, f32[34,16,128]{2,1,0:T(8,128)S(1)}, u32[]{:S(2)}, u32[]{:S(2)}) collective-permute-start(f32[34,16,128]{2,1,0:T(8,128)S(1)} %get-tuple-element.20), channel_id=1, source_target_pairs={{0,8},{16,24},{32,40},{48,56},{64,72},{80,88},{96,104},{112,120},{... | collective-permute-start | bytes 835592 | tf_op jit(solution)/shard_map/ppermute | solution.py:396
  15.5 6.7 %copy-start = (f32[1,2,2048]{2,1,0:T(2,128)S(1)}, f32[1,2,2048]{2,1,0:T(2,128)}, u32[]{:S(2)}) copy-start(f32[1,2,2048]{2,1,0:T(2,128)} %param.26) | copy-start | bytes 49156
  15.5 6.7 %copy-start.1 = (f32[1,2,2048]{2,1,0:T(2,128)S(1)}, f32[1,2,2048]{2,1,0:T(2,128)}, u32[]{:S(2)}) copy-start(f32[1,2,2048]{2,1,0:T(2,128)} %param.28) | copy-start | bytes 49156
  15.5 6.8 %copy-start.3 = (s32[2048]{0:T(1024)S(1)}, s32[2048]{0:T(1024)}, u32[]{:S(2)}) copy-start(s32[2048]{0:T(1024)} %param.27) | copy-start | bytes 24580
  15.5 6.7 %copy-start.2 = (s32[1,2048]{1,0:T(1,128)S(1)}, s32[1,2048]{1,0:T(1,128)}, u32[]{:S(2)}) copy-start(s32[1,2048]{1,0:T(1,128)} %recv_cells.1) | copy-start | bytes 24580
  15.6 8.6 %collective-permute-start.2 = (f32[14,8,128]{2,1,0:T(8,128)S(1)}, f32[14,8,128]{2,1,0:T(8,128)S(1)}, u32[]{:S(2)}, u32[]{:S(2)}) collective-permute-start(f32[14,8,128]{2,1,0:T(8,128)S(1)} %get-tuple-element.21), channel_id=1, source_target_pairs={{0,1},{2,3},{4,5},{6,7},{1,0},{3,2},{5,4},{7,6},{8,9},{10,11},{12,... | collective-permute-start | bytes 172040 | tf_op jit(solution)/shard_map/ppermute | solution.py:396
  17.5 6.6 %collective-permute-start.3 = (f32[14,8,128]{2,1,0:T(8,128)S(1)}, f32[14,8,128]{2,1,0:T(8,128)S(1)}, u32[]{:S(2)}, u32[]{:S(2)}) collective-permute-start(f32[14,8,128]{2,1,0:T(8,128)S(1)} %get-tuple-element.22), channel_id=1, source_target_pairs={{1,2},{3,4},{5,6},{2,1},{4,3},{6,5},{9,10},{11,12},{13,14},{10,9},... | collective-permute-start | bytes 172040 | tf_op jit(solution)/shard_map/ppermute | solution.py:396
  24.7 10.9 %collective-permute-start.6 = (f32[3,4,16,128]{3,2,1,0:T(8,128)S(1)}, f32[3,4,16,128]{3,2,1,0:T(8,128)S(1)}, u32[]{:S(2)}, u32[]{:S(2)}) collective-permute-start(f32[3,4,16,128]{3,2,1,0:T(8,128)S(1)} %shard_map.177), channel_id=1, source_target_pairs={{0,256},{256,0},{512,768},{768,512},{1,257},{257,1},{513,769},{769... | collective-permute-start | bytes 294920 | tf_op jit(solution)/shard_map/ppermute | solution.py:454
  28.6 8.9 %collective-permute-start.4 = (f32[40,8,128]{2,1,0:T(8,128)S(1)}, f32[40,8,128]{2,1,0:T(8,128)S(1)}, u32[]{:S(2)}, u32[]{:S(2)}) collective-permute-start(f32[40,8,128]{2,1,0:T(8,128)S(1)} %get-tuple-element.25), channel_id=1, source_target_pairs={{0,1},{2,3},{4,5},{6,7},{1,0},{3,2},{5,4},{7,6},{8,9},{10,11},{12,... | collective-permute-start | bytes 491528 | tf_op jit(solution)/shard_map/ppermute | solution.py:396
  30.6 9.0 %collective-permute-start.5 = (f32[40,8,128]{2,1,0:T(8,128)S(1)}, f32[40,8,128]{2,1,0:T(8,128)S(1)}, u32[]{:S(2)}, u32[]{:S(2)}) collective-permute-start(f32[40,8,128]{2,1,0:T(8,128)S(1)} %get-tuple-element.26), channel_id=1, source_target_pairs={{1,2},{3,4},{5,6},{2,1},{4,3},{6,5},{9,10},{11,12},{13,14},{10,9},... | collective-permute-start | bytes 491528 | tf_op jit(solution)/shard_map/ppermute | solution.py:396
  35.6 8.8 %collective-permute-start.7 = (f32[3,4,16,128]{3,2,1,0:T(8,128)S(1)}, f32[3,4,16,128]{3,2,1,0:T(8,128)S(1)}, u32[]{:S(2)}, u32[]{:S(2)}) collective-permute-start(f32[3,4,16,128]{3,2,1,0:T(8,128)S(1)} %add.3.own), channel_id=1, source_target_pairs={{0,768},{256,512},{512,256},{768,0},{1,769},{257,513},{513,257},{7... | collective-permute-start | bytes 294920 | tf_op jit(solution)/shard_map/ppermute | solution.py:456

commit v8 on v3

--- a/solution.py
+++ b/solution.py
@@ -378,8 +378,8 @@
     return lax.ppermute(part, axis, [(i, i + 1) for i in lows] + [(i + 1, i) for i in lows])
 
 
-def finish_kernel(own, across, beside, around, grad_e, grad_d):
-    total = [(own[i] + beside[i]) + (around[i] + across[i]) for i in range(3)]
+def finish_kernel(own, other, grad_e, grad_d):
+    total = [own[i] + other[i] for i in range(3)]
     scale = 1.0 / jnp.sqrt(total[2] + 1.0)
     grad_e[...] = total[0] * scale
     grad_d[...] = total[1] * scale
@@ -443,13 +443,12 @@
         smem=(0,),
     )
     shots = range(lax.axis_size("shot"))
-    parts = [
-        lax.ppermute(grads, "shot", [(i, i ^ turn) for i in shots]) for turn in (2, 1, 3)
-    ]
+    grads = grads + lax.ppermute(grads, "shot", [(i, i ^ 1) for i in shots])
+    other = lax.ppermute(grads, "shot", [(i, i ^ 3) for i in shots])
     p_final, q_final = call(
         second_step_kernel, [(size_x, size_y, size_z)] * 2, (now, ahead, weights, inject, loc)
     )
-    grad_e, grad_d = call(finish_kernel, [(size_x, size_y, size_z)] * 2, (grads, *parts))
+    grad_e, grad_d = call(finish_kernel, [(size_x, size_y, size_z)] * 2, (grads, other))
     return (p_final[None], q_final[None], grad_e, grad_d)
 
 

time: 50.1 us -> 45.4 us (0.906)
  the two profiles are of different devices: /device:TPU:562 before, /device:TPU:574 now
where the time goes in v8:
time: 45.4 us; the launch traced here: 45 us
  starting transfers between devices  20 us (44%)
  waiting for transfers between devices  17.9 us (39%)
  Pallas kernels  5.69 us (13%)
  between operations  1.41 us (3%)
    ppermute x4, starting transfers between devices, swap(): lax.ppermute(part, axis, [(i, i + 1) for i in lows] + [(i + 1, i) for i i...  13.9 us
    ppermute x4, waiting for transfers between devices, swap(): lax.ppermute(part, axis, [(i, i + 1) for i in lows] + [(i + 1, i) for i i...  8.27 us
    ppermute x1, waiting for transfers between devices, body(): other = lax.ppermute(grads, 'shot', [(i, i ^ 3) for i in shots])  5.82 us
    pallas_call x6, Pallas kernels, call(): pl.pallas_call(kernel, out_shape=shapes, in_specs=specs, out_specs=[pl.Bl...  5.69 us
    ppermute x1, starting transfers between devices, body(): grads = grads + lax.ppermute(grads, 'shot', [(i, i ^ 1) for i in shots])  4.19 us
    ppermute x1, waiting for transfers between devices, body(): grads = grads + lax.ppermute(grads, 'shot', [(i, i ^ 1) for i in shots])  3.78 us
    ppermute x1, starting transfers between devices, body(): other = lax.ppermute(grads, 'shot', [(i, i ^ 3) for i in shots])  1.92 us
  transfers between devices with their start and end apart: 6, of which 5 were waited for; matrix products, arithmetic and copies ran while one was open for 0% of the time, Pallas kernels for 6%

profile of v8, /device:TPU:574, one launch (start us, length us, event | category | flops | bytes accessed | tf_op | source)
XLA Modules:
  0.0 45.0 jit_solution(6701803454634453423)
XLA Ops:
  0.6 1.3 %shard_map.174 = (f32[56,16,128]{2,1,0:T(8,128)S(1)}, f32[34,16,128]{2,1,0:T(8,128)S(1)}, f32[34,16,128]{2,1,0:T(8,128)S(1)}) custom-call(f32[4,16,128]{2,1,0:T(8,128)} %bitcast.14, f32[4,16,128]{2,1,0:T(8,128)} %bitcast.15, f32[4,16,128]{2,1,0:T(8,128)} %bitcast.16, f32[4,16,128]{2,1,0:T(8,128)} %bitcast.17, f32[2,4,16,128]{3,2,1,0:T(8,128)} %bitcast.13, ...), custom_call_target="tpu_custom_call" | custom-call | flops 2000000 | bytes 2000000 | tf_op jit(solution)/shard_map/pallas_call | solution.py:23
  1.9 2.8 %collective-permute-start = (f32[34,16,128]{2,1,0:T(8,128)S(1)}, f32[34,16,128]{2,1,0:T(8,128)S(1)}, u32[]{:S(2)}, u32[]{:S(2)}) collective-permute-start(f32[34,16,128]{2,1,0:T(8,128)S(1)} %get-tuple-element.18), channel_id=1, source_target_pairs={{8,16},{24,32},{40,48},{56,64},{72,80},{88,96},{104,112},{120,128}... | collective-permute-start | bytes 835592 | tf_op jit(solution)/shard_map/ppermute | solution.py:378
  4.7 4.4 %collective-permute-start.1 = (f32[34,16,128]{2,1,0:T(8,128)S(1)}, f32[34,16,128]{2,1,0:T(8,128)S(1)}, u32[]{:S(2)}, u32[]{:S(2)}) collective-permute-start(f32[34,16,128]{2,1,0:T(8,128)S(1)} %get-tuple-element.19), channel_id=1, source_target_pairs={{0,8},{16,24},{32,40},{48,56},{64,72},{80,88},{96,104},{112,120},{... | collective-permute-start | bytes 835592 | tf_op jit(solution)/shard_map/ppermute | solution.py:378
  9.1 3.6 %collective-permute-done.far.far_x = f32[34,16,128]{2,1,0:T(8,128)S(1)} collective-permute-done((f32[34,16,128]{2,1,0:T(8,128)S(1)}, f32[34,16,128]{2,1,0:T(8,128)S(1)}, u32[]{:S(2)}, u32[]{:S(2)}) %collective-permute-start) | collective-permute-done | bytes 278560 | tf_op jit(solution)/shard_map/ppermute | solution.py:378
  12.8 0.0 collective-permute-done.1.near.near_x
  12.8 0.0 copy-start
  12.8 0.0 copy-start.1
  12.8 0.0 copy-start.3
  12.8 0.1 shard_map.175
  12.9 0.0 copy-start.2
  12.9 4.8 %collective-permute-start.2 = (f32[44,8,128]{2,1,0:T(8,128)S(1)}, f32[44,8,128]{2,1,0:T(8,128)S(1)}, u32[]{:S(2)}, u32[]{:S(2)}) collective-permute-start(f32[44,8,128]{2,1,0:T(8,128)S(1)} %get-tuple-element.20), channel_id=1, source_target_pairs={{1,2},{3,4},{5,6},{2,1},{4,3},{6,5},{9,10},{11,12},{13,14},{10,9},... | collective-permute-start | bytes 540680 | tf_op jit(solution)/shard_map/ppermute | solution.py:378
  17.7 1.9 %collective-permute-start.3 = (f32[44,8,128]{2,1,0:T(8,128)S(1)}, f32[44,8,128]{2,1,0:T(8,128)S(1)}, u32[]{:S(2)}, u32[]{:S(2)}) collective-permute-start(f32[44,8,128]{2,1,0:T(8,128)S(1)} %get-tuple-element.21), channel_id=1, source_target_pairs={{0,1},{2,3},{4,5},{6,7},{1,0},{3,2},{5,4},{7,6},{8,9},{10,11},{12,... | collective-permute-start | bytes 540680 | tf_op jit(solution)/shard_map/ppermute | solution.py:378
  20.3 0.0 copy-done
  20.3 0.0 copy-done.1
  20.3 0.0 copy-done.3
  20.3 0.0 copy-done.2
  20.3 1.8 %shard_map.176.inject = f32[256,128]{1,0:T(8,128)S(1)} custom-call(s32[1,2048]{1,0:T(1,128)S(1)} %copy-done.2, f32[2,2048]{1,0:T(2,128)S(1)} %bitcast.10, s32[1,2048]{1,0:T(1,128)S(1)} %bitcast.12, f32[2,2048]{1,0:T(2,128)S(1)} %bitcast.11), custom_call_target="tpu_custom_call" | custom-call | flops 800000000 | bytes 2000000 | tf_op jit(solution)/shard_map/pallas_call | solution.py:23
  22.1 0.7 %collective-permute-done.2.odds = f32[44,8,128]{2,1,0:T(8,128)S(1)} collective-permute-done((f32[44,8,128]{2,1,0:T(8,128)S(1)}, f32[44,8,128]{2,1,0:T(8,128)S(1)}, u32[]{:S(2)}, u32[]{:S(2)}) %collective-permute-start.2) | collective-permute-done | bytes 180256 | tf_op jit(solution)/shard_map/ppermute | solution.py:378
  22.8 3.9 %collective-permute-done.3.evens = f32[44,8,128]{2,1,0:T(8,128)S(1)} collective-permute-done((f32[44,8,128]{2,1,0:T(8,128)S(1)}, f32[44,8,128]{2,1,0:T(8,128)S(1)}, u32[]{:S(2)}, u32[]{:S(2)}) %collective-permute-start.3) | collective-permute-done | bytes 180256 | tf_op jit(solution)/shard_map/ppermute | solution.py:378
  26.7 1.0 %shard_map.177 = (f32[3,4,16,128]{3,2,1,0:T(8,128)S(1)}, f32[2,4,16,128]{3,2,1,0:T(8,128)S(1)}, f32[2,3,8,8,128]{4,3,2,1,0:T(8,128)S(1)}, f32[6,3,8,8,128]{4,3,2,1,0:T(8,128)S(1)}) custom-call(s32[1]{0:T(128)S(6)} %copy.19.source, f32[56,16,128]{2,1,0:T(8,128)S(1)} %get-tuple-element.17.loc, f32[34,16,128]{2,1,0:T(8,128)S(1)} %collective-permute-done.far.far_x, ...), custom_call_target="tpu_custom_call" | custom-call | flops 2000000 | bytes 2000000 | tf_op jit(solution)/shard_map/pallas_call | solution.py:23
  27.8 4.2 %collective-permute-start.4 = (f32[3,4,16,128]{3,2,1,0:T(8,128)S(1)}, f32[3,4,16,128]{3,2,1,0:T(8,128)S(1)}, u32[]{:S(2)}, u32[]{:S(2)}) collective-permute-start(f32[3,4,16,128]{3,2,1,0:T(8,128)S(1)} %get-tuple-element.27), channel_id=1, source_target_pairs={{0,256},{256,0},{512,768},{768,512},{1,257},{257,1},{513,769},{769... | collective-permute-start | bytes 294920 | tf_op jit(solution)/shard_map/ppermute | solution.py:446
  32.0 3.8 %collective-permute-done.4 = f32[3,4,16,128]{3,2,1,0:T(8,128)S(1)} collective-permute-done((f32[3,4,16,128]{3,2,1,0:T(8,128)S(1)}, f32[3,4,16,128]{3,2,1,0:T(8,128)S(1)}, u32[]{:S(2)}, u32[]{:S(2)}) %collective-permute-start.4) | collective-permute-done | bytes 98336 | tf_op jit(solution)/shard_map/ppermute | solution.py:446
  35.8 1.9 %collective-permute-start.5 = (f32[3,4,16,128]{3,2,1,0:T(8,128)S(1)}, f32[3,4,16,128]{3,2,1,0:T(8,128)S(1)}, u32[]{:S(2)}, u32[]{:S(2)}) collective-permute-start(f32[3,4,16,128]{3,2,1,0:T(8,128)S(1)} %add.3.own), channel_id=1, source_target_pairs={{0,768},{256,512},{512,256},{768,0},{1,769},{257,513},{513,257},{7... | collective-permute-start | bytes 294920 | tf_op jit(solution)/shard_map/ppermute | solution.py:447
  37.7 0.9 %shard_map.178 = (f32[4,16,128]{2,1,0:T(8,128)}, f32[4,16,128]{2,1,0:T(8,128)}) custom-call(f32[2,4,16,128]{3,2,1,0:T(8,128)S(1)} %get-tuple-element.22.now, f32[2,3,8,8,128]{4,3,2,1,0:T(8,128)S(1)} %get-tuple-element.23.ahead, f32[6,3,8,8,128]{4,3,2,1,0:T(8,128)S(1)} %get-tuple-element.24.weights, f32[256,128]{1,0:T(8,128)S(1)} %shard_map.176.inject, ...), custom_call_target="tpu_custom_call" | custom-call | flops 2000000 | bytes 2000000 | tf_op jit(solution)/shard_map/pallas_call | solution.py:23
  38.6 5.8 %collective-permute-done.5.other = f32[3,4,16,128]{3,2,1,0:T(8,128)S(1)} collective-permute-done((f32[3,4,16,128]{3,2,1,0:T(8,128)S(1)}, f32[3,4,16,128]{3,2,1,0:T(8,128)S(1)}, u32[]{:S(2)}, u32[]{:S(2)}) %collective-permute-start.5) | collective-permute-done | bytes 98336 | tf_op jit(solution)/shard_map/ppermute | solution.py:447
  44.4 0.7 %shard_map.179 = (f32[4,16,128]{2,1,0:T(8,128)}, f32[4,16,128]{2,1,0:T(8,128)}) custom-call(f32[3,4,16,128]{3,2,1,0:T(8,128)S(1)} %add.3.own, f32[3,4,16,128]{3,2,1,0:T(8,128)S(1)} %collective-permute-done.5.other), custom_call_target="tpu_custom_call" | custom-call | flops 2000000 | bytes 2000000 | tf_op jit(solution)/shard_map/pallas_call | solution.py:23
  (1 shorter events, 0.0 us)
Async XLA Ops:
  1.9 10.8 %collective-permute-start = (f32[34,16,128]{2,1,0:T(8,128)S(1)}, f32[34,16,128]{2,1,0:T(8,128)S(1)}, u32[]{:S(2)}, u32[]{:S(2)}) collective-permute-start(f32[34,16,128]{2,1,0:T(8,128)S(1)} %get-tuple-element.18), channel_id=1, source_target_pairs={{8,16},{24,32},{40,48},{56,64},{72,80},{88,96},{104,112},{120,128}... | collective-permute-start | bytes 835592 | tf_op jit(solution)/shard_map/ppermute | solution.py:378
  4.7 8.1 %collective-permute-start.1 = (f32[34,16,128]{2,1,0:T(8,128)S(1)}, f32[34,16,128]{2,1,0:T(8,128)S(1)}, u32[]{:S(2)}, u32[]{:S(2)}) collective-permute-start(f32[34,16,128]{2,1,0:T(8,128)S(1)} %get-tuple-element.19), channel_id=1, source_target_pairs={{0,8},{16,24},{32,40},{48,56},{64,72},{80,88},{96,104},{112,120},{... | collective-permute-start | bytes 835592 | tf_op jit(solution)/shard_map/ppermute | solution.py:378
  12.8 7.5 %copy-start = (f32[1,2,2048]{2,1,0:T(2,128)S(1)}, f32[1,2,2048]{2,1,0:T(2,128)}, u32[]{:S(2)}) copy-start(f32[1,2,2048]{2,1,0:T(2,128)} %param.26) | copy-start | bytes 49156
  12.8 7.5 %copy-start.1 = (f32[1,2,2048]{2,1,0:T(2,128)S(1)}, f32[1,2,2048]{2,1,0:T(2,128)}, u32[]{:S(2)}) copy-start(f32[1,2,2048]{2,1,0:T(2,128)} %param.28) | copy-start | bytes 49156
  12.8 7.5 %copy-start.3 = (s32[2048]{0:T(1024)S(1)}, s32[2048]{0:T(1024)}, u32[]{:S(2)}) copy-start(s32[2048]{0:T(1024)} %param.27) | copy-start | bytes 24580
  12.9 7.4 %copy-start.2 = (s32[1,2048]{1,0:T(1,128)S(1)}, s32[1,2048]{1,0:T(1,128)}, u32[]{:S(2)}) copy-start(s32[1,2048]{1,0:T(1,128)} %recv_cells.1) | copy-start | bytes 24580
  12.9 9.9 %collective-permute-start.2 = (f32[44,8,128]{2,1,0:T(8,128)S(1)}, f32[44,8,128]{2,1,0:T(8,128)S(1)}, u32[]{:S(2)}, u32[]{:S(2)}) collective-permute-start(f32[44,8,128]{2,1,0:T(8,128)S(1)} %get-tuple-element.20), channel_id=1, source_target_pairs={{1,2},{3,4},{5,6},{2,1},{4,3},{6,5},{9,10},{11,12},{13,14},{10,9},... | collective-permute-start | bytes 540680 | tf_op jit(solution)/shard_map/ppermute | solution.py:378
  17.7 9.0 %collective-permute-start.3 = (f32[44,8,128]{2,1,0:T(8,128)S(1)}, f32[44,8,128]{2,1,0:T(8,128)S(1)}, u32[]{:S(2)}, u32[]{:S(2)}) collective-permute-start(f32[44,8,128]{2,1,0:T(8,128)S(1)} %get-tuple-element.21), channel_id=1, source_target_pairs={{0,1},{2,3},{4,5},{6,7},{1,0},{3,2},{5,4},{7,6},{8,9},{10,11},{12,... | collective-permute-start | bytes 540680 | tf_op jit(solution)/shard_map/ppermute | solution.py:378
  27.8 8.0 %collective-permute-start.4 = (f32[3,4,16,128]{3,2,1,0:T(8,128)S(1)}, f32[3,4,16,128]{3,2,1,0:T(8,128)S(1)}, u32[]{:S(2)}, u32[]{:S(2)}) collective-permute-start(f32[3,4,16,128]{3,2,1,0:T(8,128)S(1)} %get-tuple-element.27), channel_id=1, source_target_pairs={{0,256},{256,0},{512,768},{768,512},{1,257},{257,1},{513,769},{769... | collective-permute-start | bytes 294920 | tf_op jit(solution)/shard_map/ppermute | solution.py:446
  35.8 8.6 %collective-permute-start.5 = (f32[3,4,16,128]{3,2,1,0:T(8,128)S(1)}, f32[3,4,16,128]{3,2,1,0:T(8,128)S(1)}, u32[]{:S(2)}, u32[]{:S(2)}) collective-permute-start(f32[3,4,16,128]{3,2,1,0:T(8,128)S(1)} %add.3.own), channel_id=1, source_target_pairs={{0,768},{256,512},{512,256},{768,0},{1,769},{257,513},{513,257},{7... | collective-permute-start | bytes 294920 | tf_op jit(solution)/shard_map/ppermute | solution.py:447

commit v9 on v7

--- a/solution.py
+++ b/solution.py
@@ -8,7 +8,7 @@
 from jax.sharding import PartitionSpec as P
 
 TAPER = 32
-WIDE = 5
+WIDE = 4
 NARROW = 7
 FIELDS = WIDE + NARROW + 2
 INPUTS = ("p", "q", "p_old", "q_old", "f", "c", "eps", "delta", "tilt", "azimuth")
@@ -150,13 +150,11 @@
     p_now, q_now, speed = p[...], q[...], c[...]
     p_weight = speed * (1.0 + 2.0 * eps[...])
     q_weight = speed * (1.0 + 2.0 * delta[...])
-    sine = jnp.sin(tilt[...])
     wide = (
         p_weight * p_now + q_weight * q_now,
         speed * (p_now + q_now),
-        sine * jnp.cos(azimuth[...]),
-        sine * jnp.sin(azimuth[...]),
-        jnp.cos(tilt[...]),
+        tilt[...],
+        azimuth[...],
     )
     narrow = (
         2.0 * p_now - p_old[...],
@@ -227,10 +225,6 @@
     return jnp.concatenate(edges, axis=0)
 
 
-def early_rows(wide, narrow):
-    return [tile[2 : tile.shape[0] - 2] for tile in wide] + narrow[5:]
-
-
 def send_both(parts, evens, odds, start):
     odd = lax.rem(lax.axis_index("gy"), 2) == 1
     rows = slice(start, start + parts[0].shape[0])
@@ -243,24 +237,28 @@
     return jnp.where(odd, odds[...], evens[...]), jnp.where(odd, evens[...], odds[...])
 
 
-def early_kernel(loc, far, near, odds, evens):
-    size_x = loc.shape[0] // FIELDS
-    parts = []
-    for part in range(2):
-        wide, narrow = tiles_of(loc, near, far, size_x, part)
-        parts.append(pack(jnp.concatenate(early_rows(wide, narrow), axis=0), part, 4))
-    send_both(parts, evens, odds, 0)
-
-
-def late_kernel(loc, far, near, odds, evens):
+def pack_kernel(loc, far, near, odds, evens):
     size_x = loc.shape[0] // FIELDS
     wides, narrows = [], []
     for part in range(2):
         wide, narrow = tiles_of(loc, near, far, size_x, part)
         wides.append(pack(jnp.concatenate(wide, axis=0), part, 2))
-        narrows.append(pack(jnp.concatenate(narrow[:5], axis=0), part, 4))
+        narrows.append(pack(jnp.concatenate(narrow, axis=0), part, 4))
     send_both(wides, evens, odds, 0)
     send_both(narrows, evens, odds, wides[0].shape[0])
+
+
+def normal_of(tilt, azimuth):
+    sine = jnp.sin(tilt)
+    return sine * jnp.cos(azimuth), sine * jnp.sin(azimuth), jnp.cos(tilt)
+
+
+def normal_kernel(loc, far, near, out):
+    size_x = loc.shape[0] // FIELDS
+    for part in range(2):
+        wide, _ = tiles_of(loc, near, far, size_x, part)
+        for axis, cells in enumerate(normal_of(wide[2], wide[3])):
+            out[axis, part] = cells
 
 
 def cut(rows, count):
@@ -314,19 +312,36 @@
     out[...] = total[0:rows] + total[rows : 2 * rows] + total[2 * rows : 3 * rows]
 
 
-def first_step_kernel(grid_y, source, loc, far_x, near_x, evens, odds, inject, grads):
+def fields_of(loc, far, near, odds, evens):
+    size_x = loc.shape[0] // FIELDS
+    high, low = from_both(evens, odds)
+    half = WIDE * (size_x + 8) // 2
+    wide_edge = cut(unpack(high[:half], low[:half], 2), size_x + 8)
+    narrow_edge = cut(unpack(high[half:], low[half:], 4), size_x + 4)
+    parts = [tiles_of(loc, near, far, size_x, part) for part in range(2)]
+    wide = [[parts[0][0][n], parts[1][0][n], wide_edge[n]] for n in range(WIDE)]
+    narrow = [[parts[0][1][n], parts[1][1][n], narrow_edge[n]] for n in range(NARROW)]
+    return wide, narrow, wide_edge[2:4]
+
+
+def first_step_kernel(grid_y, source, loc, far_x, near_x, odds, evens, normal, inject, grads, edge_normal):
     size_x, size_y = loc.shape[0] // FIELDS, loc.shape[1]
     count = size_x + 4
-    high, low = from_both(evens, odds)
-    edge = cut(unpack(high, low, 4), count)
-    middle = [early_rows(*tiles_of(loc, near_x, far_x, size_x, part)) for part in range(2)]
-    fields = [[middle[0][n], middle[1][n], edge[n]] for n in range(len(edge))]
-    products = [[fields[2 + a][i] * fields[2 + b][i] for i in range(3)] for a, b in PAIRS]
+    wide, narrow, angles = fields_of(loc, far_x, near_x, odds, evens)
+    fields = [[tile[2 : 2 + count] for tile in wide[n]] for n in range(2)]
+    edge = normal_of(*angles)
+    for axis in range(3):
+        edge_normal[axis] = edge[axis]
+    normals = [
+        [normal[axis, 0, 2 : 2 + count], normal[axis, 1, 2 : 2 + count], edge[axis][2 : 2 + count]]
+        for axis in range(3)
+    ]
+    products = [[normals[a][i] * normals[b][i] for i in range(3)] for a, b in PAIRS]
     mid = slice(2, 2 + size_x)
     p_next = adjoint(products, fields[0], size_x, 2, False)
     q_next = adjoint(products, fields[1], size_x, 2, True)
     inner = [[tile[mid] for tile in entry] for entry in products]
-    images = [forward_image(inner, field, size_x) for field in fields[5:7]]
+    images = [forward_image(inner, field, size_x) for field in narrow[5:7]]
     ring = inject[0 : count * 24].reshape(count, 24, 128)
     bits_y = grid_y.bit_length() - 1
     source_x = (source[0] >> bits_y) - lax.axis_index("gx") * size_x
@@ -352,18 +367,13 @@
         grads[2, :, ys, :] = f0 * f0 + f1 * f1
 
 
-def second_step_kernel(loc, far_x, near_x, evens, odds, inject, p_out, q_out):
+def second_step_kernel(loc, far_x, near_x, odds, evens, normal, edge_normal, inject, p_out, q_out):
     size_x, size_y = p_out.shape[0], p_out.shape[1]
     count = size_x + 4
-    high, low = from_both(evens, odds)
-    half = WIDE * (size_x + 8) // 2
-    wide_edge = cut(unpack(high[:half], low[:half], 2), size_x + 8)
-    narrow_edge = cut(unpack(high[half:], low[half:], 4), count)
-    parts = [tiles_of(loc, near_x, far_x, size_x, part) for part in range(2)]
-    wide = [[parts[0][0][n], parts[1][0][n], wide_edge[n]] for n in range(WIDE)]
-    narrow = [[parts[0][1][n], parts[1][1][n], narrow_edge[n]] for n in range(5)]
-    products = [[wide[2 + a][i] * wide[2 + b][i] for i in range(3)] for a, b in PAIRS]
-    p_base, q_base, p_weight, q_weight, speed = narrow
+    wide, narrow, _ = fields_of(loc, far_x, near_x, odds, evens)
+    normals = [[normal[axis, 0], normal[axis, 1], edge_normal[axis]] for axis in range(3)]
+    products = [[normals[a][i] * normals[b][i] for i in range(3)] for a, b in PAIRS]
+    p_base, q_base, p_weight, q_weight, speed = narrow[:5]
     mid = slice(2, 2 + size_x)
     p_next = adjoint(products, wide[0], count, 3, False)
     q_next = adjoint(products, wide[1], count, 3, True)
@@ -438,26 +448,23 @@
         flops=800_000_000,
     )
     edges = (loc, far, near)
-    early = (WIDE + 2) * (size_x + 4) // 4
-    late = WIDE * (size_x + 8) // 2 + 5 * (size_x + 4) // 4
-    odds, evens = call(early_kernel, [(early, 8, size_z)] * 2, edges)
+    tiles = WIDE * (size_x + 8) // 2 + NARROW * (size_x + 4) // 4
+    odds, evens = call(pack_kernel, [(tiles, 8, size_z)] * 2, edges)
     odds, evens = swap(odds, "gy", 1), swap(evens, "gy", 0)
-    late_odds, late_evens = call(late_kernel, [(late, 8, size_z)] * 2, edges)
-    (grads,) = call(
+    (normal,) = call(normal_kernel, [(3, 2, size_x + 8, 8, size_z)], edges)
+    grads, edge_normal = call(
         functools.partial(first_step_kernel, grid_y),
-        [(3, size_x, size_y, size_z)],
-        (source_cells, *edges, evens, odds, inject),
+        [(3, size_x, size_y, size_z), (3, size_x + 8, 8, size_z)],
+        (source_cells, *edges, odds, evens, normal, inject),
         smem=(0,),
     )
-    grads, late_odds, late_evens = lax.optimization_barrier((grads, late_odds, late_evens))
     shots = range(lax.axis_size("shot"))
     grads = grads + lax.ppermute(grads, "shot", [(i, i ^ 1) for i in shots])
-    late_odds, late_evens = swap(late_odds, "gy", 1), swap(late_evens, "gy", 0)
     other = lax.ppermute(grads, "shot", [(i, i ^ 3) for i in shots])
     p_final, q_final = call(
         second_step_kernel,
         [(size_x, size_y, size_z)] * 2,
-        (*edges, late_evens, late_odds, inject),
+        (*edges, odds, evens, normal, edge_normal, inject),
         flops=20_000_000,
     )
     grad_e, grad_d = call(finish_kernel, [(size_x, size_y, size_z)] * 2, (grads, other))

time: 45.4 us -> 44.5 us (0.980)
  the two profiles are of different devices: /device:TPU:287 before, /device:TPU:562 now
where the time goes in v9:
time: 44.5 us; the launch traced here: 44.2 us
  starting transfers between devices  24.5 us (55%)
  waiting for transfers between devices  11.4 us (26%)
  Pallas kernels  6.78 us (15%)
  between operations  1.42 us (3%)
    ppermute x4, starting transfers between devices, swap(): lax.ppermute(part, axis, [(i, i + 1) for i in lows] + [(i + 1, i) for i i...  13 us
    ppermute x1, starting transfers between devices, body(): other = lax.ppermute(grads, 'shot', [(i, i ^ 3) for i in shots])  7.06 us
    pallas_call x7, Pallas kernels, call(): pl.pallas_call(kernel, out_shape=shapes, in_specs=specs, out_specs=[pl.Bl...  6.78 us
    ppermute x4, waiting for transfers between devices, swap(): lax.ppermute(part, axis, [(i, i + 1) for i in lows] + [(i + 1, i) for i i...  6.02 us
    ppermute x1, starting transfers between devices, body(): grads = grads + lax.ppermute(grads, 'shot', [(i, i ^ 1) for i in shots])  4.47 us
    ppermute x1, waiting for transfers between devices, body(): grads = grads + lax.ppermute(grads, 'shot', [(i, i ^ 1) for i in shots])  3 us
    ppermute x1, waiting for transfers between devices, body(): other = lax.ppermute(grads, 'shot', [(i, i ^ 3) for i in shots])  2.38 us
  transfers between devices with their start and end apart: 6, of which 4 were waited for; matrix products, arithmetic and copies ran while one was open for 0% of the time, Pallas kernels for 9%

profile of v9, /device:TPU:562, one launch (start us, length us, event | category | flops | bytes accessed | tf_op | source)
XLA Modules:
  0.0 44.2 jit_solution(4937337363700412399)
XLA Ops:
  0.6 1.1 %shard_map.174 = (f32[52,16,128]{2,1,0:T(8,128)S(1)}, f32[30,16,128]{2,1,0:T(8,128)S(1)}, f32[30,16,128]{2,1,0:T(8,128)S(1)}) custom-call(f32[4,16,128]{2,1,0:T(8,128)} %bitcast.14, f32[4,16,128]{2,1,0:T(8,128)} %bitcast.15, f32[4,16,128]{2,1,0:T(8,128)} %bitcast.16, f32[4,16,128]{2,1,0:T(8,128)} %bitcast.17, f32[2,4,16,128]{3,2,1,0:T(8,128)} %bitcast.13, ...), custom_call_target="tpu_custom_call" | custom-call | flops 2000000 | bytes 2000000 | tf_op jit(solution)/shard_map/pallas_call | solution.py:23
  1.7 1.9 %collective-permute-start = (f32[30,16,128]{2,1,0:T(8,128)S(1)}, f32[30,16,128]{2,1,0:T(8,128)S(1)}, u32[]{:S(2)}, u32[]{:S(2)}) collective-permute-start(f32[30,16,128]{2,1,0:T(8,128)S(1)} %get-tuple-element.16), channel_id=1, source_target_pairs={{8,16},{24,32},{40,48},{56,64},{72,80},{88,96},{104,112},{120,128}... | collective-permute-start | bytes 737288 | tf_op jit(solution)/shard_map/ppermute | solution.py:406
  3.6 4.4 %collective-permute-start.1 = (f32[30,16,128]{2,1,0:T(8,128)S(1)}, f32[30,16,128]{2,1,0:T(8,128)S(1)}, u32[]{:S(2)}, u32[]{:S(2)}) collective-permute-start(f32[30,16,128]{2,1,0:T(8,128)S(1)} %get-tuple-element.17), channel_id=1, source_target_pairs={{0,8},{16,24},{32,40},{48,56},{64,72},{80,88},{96,104},{112,120},{... | collective-permute-start | bytes 737288 | tf_op jit(solution)/shard_map/ppermute | solution.py:406
  8.0 2.9 %collective-permute-done.far.far_x = f32[30,16,128]{2,1,0:T(8,128)S(1)} collective-permute-done((f32[30,16,128]{2,1,0:T(8,128)S(1)}, f32[30,16,128]{2,1,0:T(8,128)S(1)}, u32[]{:S(2)}, u32[]{:S(2)}) %collective-permute-start) | collective-permute-done | bytes 245792 | tf_op jit(solution)/shard_map/ppermute | solution.py:406
  11.0 0.0 collective-permute-done.1.near.near_x
  11.0 0.0 copy-start
  11.0 0.0 copy-start.1
  11.0 0.0 copy-start.3
  11.0 0.1 shard_map.175
  11.1 0.0 copy-start.2
  11.1 4.8 %collective-permute-start.2 = (f32[38,8,128]{2,1,0:T(8,128)S(1)}, f32[38,8,128]{2,1,0:T(8,128)S(1)}, u32[]{:S(2)}, u32[]{:S(2)}) collective-permute-start(f32[38,8,128]{2,1,0:T(8,128)S(1)} %get-tuple-element.18), channel_id=1, source_target_pairs={{1,2},{3,4},{5,6},{2,1},{4,3},{6,5},{9,10},{11,12},{13,14},{10,9},... | collective-permute-start | bytes 466952 | tf_op jit(solution)/shard_map/ppermute | solution.py:406
  15.9 1.9 %collective-permute-start.3 = (f32[38,8,128]{2,1,0:T(8,128)S(1)}, f32[38,8,128]{2,1,0:T(8,128)S(1)}, u32[]{:S(2)}, u32[]{:S(2)}) collective-permute-start(f32[38,8,128]{2,1,0:T(8,128)S(1)} %get-tuple-element.19), channel_id=1, source_target_pairs={{0,1},{2,3},{4,5},{6,7},{1,0},{3,2},{5,4},{7,6},{8,9},{10,11},{12,... | collective-permute-start | bytes 466952 | tf_op jit(solution)/shard_map/ppermute | solution.py:406
  18.5 0.0 copy-done
  18.5 0.0 copy-done.1
  18.5 0.0 copy-done.3
  18.5 0.0 copy-done.2
  18.5 1.8 %shard_map.177.inject = f32[256,128]{1,0:T(8,128)S(1)} custom-call(s32[1,2048]{1,0:T(1,128)S(1)} %copy-done.2, f32[2,2048]{1,0:T(2,128)S(1)} %bitcast.10, s32[1,2048]{1,0:T(1,128)S(1)} %bitcast.12, f32[2,2048]{1,0:T(2,128)S(1)} %bitcast.11), custom_call_target="tpu_custom_call" | custom-call | flops 800000000 | bytes 2000000 | tf_op jit(solution)/shard_map/pallas_call | solution.py:23
  20.3 0.7 %shard_map.176.normal = f32[3,2,12,8,128]{4,3,2,1,0:T(8,128)S(1)} custom-call(f32[52,16,128]{2,1,0:T(8,128)S(1)} %get-tuple-element.15.loc, f32[30,16,128]{2,1,0:T(8,128)S(1)} %collective-permute-done.far.far_x, f32[30,16,128]{2,1,0:T(8,128)S(1)} %collective-permute-done.1.near.near_x), custom_call_target="tpu_custom_call" | custom-call | flops 2000000 | bytes 2000000 | tf_op jit(solution)/shard_map/pallas_call | solution.py:23
  21.0 0.0 collective-permute-done.2.odds
  21.0 3.1 %collective-permute-done.3.evens = f32[38,8,128]{2,1,0:T(8,128)S(1)} collective-permute-done((f32[38,8,128]{2,1,0:T(8,128)S(1)}, f32[38,8,128]{2,1,0:T(8,128)S(1)}, u32[]{:S(2)}, u32[]{:S(2)}) %collective-permute-start.3) | collective-permute-done | bytes 155680 | tf_op jit(solution)/shard_map/ppermute | solution.py:406
  24.1 0.9 %shard_map.178 = (f32[3,4,16,128]{3,2,1,0:T(8,128)S(1)}, f32[3,12,8,128]{3,2,1,0:T(8,128)S(1)}) custom-call(s32[1]{0:T(128)S(6)} %copy.19.source, f32[52,16,128]{2,1,0:T(8,128)S(1)} %get-tuple-element.15.loc, f32[30,16,128]{2,1,0:T(8,128)S(1)} %collective-permute-done.far.far_x, f32[30,16,128]{2,1,0:T(8,128)S(1)} %collective-permute-done.1.near.near_x, ...), custom_call_target="tpu_custom_call" | custom-call | flops 2000000 | bytes 2000000 | tf_op jit(solution)/shard_map/pallas_call | solution.py:23
  25.0 4.5 %collective-permute-start.4 = (f32[3,4,16,128]{3,2,1,0:T(8,128)S(1)}, f32[3,4,16,128]{3,2,1,0:T(8,128)S(1)}, u32[]{:S(2)}, u32[]{:S(2)}) collective-permute-start(f32[3,4,16,128]{3,2,1,0:T(8,128)S(1)} %get-tuple-element.23), channel_id=1, source_target_pairs={{0,256},{256,0},{512,768},{768,512},{1,257},{257,1},{513,769},{769... | collective-permute-start | bytes 294920 | tf_op jit(solution)/shard_map/ppermute | solution.py:462
  29.5 3.0 %collective-permute-done.4 = f32[3,4,16,128]{3,2,1,0:T(8,128)S(1)} collective-permute-done((f32[3,4,16,128]{3,2,1,0:T(8,128)S(1)}, f32[3,4,16,128]{3,2,1,0:T(8,128)S(1)}, u32[]{:S(2)}, u32[]{:S(2)}) %collective-permute-start.4) | collective-permute-done | bytes 98336 | tf_op jit(solution)/shard_map/ppermute | solution.py:462
  32.5 7.1 %collective-permute-start.5 = (f32[3,4,16,128]{3,2,1,0:T(8,128)S(1)}, f32[3,4,16,128]{3,2,1,0:T(8,128)S(1)}, u32[]{:S(2)}, u32[]{:S(2)}) collective-permute-start(f32[3,4,16,128]{3,2,1,0:T(8,128)S(1)} %add.3.own), channel_id=1, source_target_pairs={{0,768},{256,512},{512,256},{768,0},{1,769},{257,513},{513,257},{7... | collective-permute-start | bytes 294920 | tf_op jit(solution)/shard_map/ppermute | solution.py:463
  39.6 1.6 %shard_map.179 = (f32[4,16,128]{2,1,0:T(8,128)}, f32[4,16,128]{2,1,0:T(8,128)}) custom-call(f32[52,16,128]{2,1,0:T(8,128)S(1)} %get-tuple-element.15.loc, f32[30,16,128]{2,1,0:T(8,128)S(1)} %collective-permute-done.far.far_x, f32[30,16,128]{2,1,0:T(8,128)S(1)} %collective-permute-done.1.near.near_x, f32[38,8,128]{2,1,0:T(8,128)S(1)} %collective-permute-done.2.odds, ...), custom_call_target="tpu_custom_call" | custom-call | flops 20000000 | bytes 2000000 | tf_op jit(solution)/shard_map/pallas_call | solution.py:23
  41.1 2.4 %collective-permute-done.5.other = f32[3,4,16,128]{3,2,1,0:T(8,128)S(1)} collective-permute-done((f32[3,4,16,128]{3,2,1,0:T(8,128)S(1)}, f32[3,4,16,128]{3,2,1,0:T(8,128)S(1)}, u32[]{:S(2)}, u32[]{:S(2)}) %collective-permute-start.5) | collective-permute-done | bytes 98336 | tf_op jit(solution)/shard_map/ppermute | solution.py:463
  43.5 0.7 %shard_map.180 = (f32[4,16,128]{2,1,0:T(8,128)}, f32[4,16,128]{2,1,0:T(8,128)}) custom-call(f32[3,4,16,128]{3,2,1,0:T(8,128)S(1)} %add.3.own, f32[3,4,16,128]{3,2,1,0:T(8,128)S(1)} %collective-permute-done.5.other), custom_call_target="tpu_custom_call" | custom-call | flops 2000000 | bytes 2000000 | tf_op jit(solution)/shard_map/pallas_call | solution.py:23
  (1 shorter events, 0.0 us)
Async XLA Ops:
  1.7 9.2 %collective-permute-start = (f32[30,16,128]{2,1,0:T(8,128)S(1)}, f32[30,16,128]{2,1,0:T(8,128)S(1)}, u32[]{:S(2)}, u32[]{:S(2)}) collective-permute-start(f32[30,16,128]{2,1,0:T(8,128)S(1)} %get-tuple-element.16), channel_id=1, source_target_pairs={{8,16},{24,32},{40,48},{56,64},{72,80},{88,96},{104,112},{120,128}... | collective-permute-start | bytes 737288 | tf_op jit(solution)/shard_map/ppermute | solution.py:406
  3.6 7.3 %collective-permute-start.1 = (f32[30,16,128]{2,1,0:T(8,128)S(1)}, f32[30,16,128]{2,1,0:T(8,128)S(1)}, u32[]{:S(2)}, u32[]{:S(2)}) collective-permute-start(f32[30,16,128]{2,1,0:T(8,128)S(1)} %get-tuple-element.17), channel_id=1, source_target_pairs={{0,8},{16,24},{32,40},{48,56},{64,72},{80,88},{96,104},{112,120},{... | collective-permute-start | bytes 737288 | tf_op jit(solution)/shard_map/ppermute | solution.py:406
  11.0 7.5 %copy-start = (f32[1,2,2048]{2,1,0:T(2,128)S(1)}, f32[1,2,2048]{2,1,0:T(2,128)}, u32[]{:S(2)}) copy-start(f32[1,2,2048]{2,1,0:T(2,128)} %param.26) | copy-start | bytes 49156
  11.0 7.5 %copy-start.1 = (f32[1,2,2048]{2,1,0:T(2,128)S(1)}, f32[1,2,2048]{2,1,0:T(2,128)}, u32[]{:S(2)}) copy-start(f32[1,2,2048]{2,1,0:T(2,128)} %param.28) | copy-start | bytes 49156
  11.0 7.5 %copy-start.3 = (s32[2048]{0:T(1024)S(1)}, s32[2048]{0:T(1024)}, u32[]{:S(2)}) copy-start(s32[2048]{0:T(1024)} %param.27) | copy-start | bytes 24580
  11.1 7.4 %copy-start.2 = (s32[1,2048]{1,0:T(1,128)S(1)}, s32[1,2048]{1,0:T(1,128)}, u32[]{:S(2)}) copy-start(s32[1,2048]{1,0:T(1,128)} %recv_cells.1) | copy-start | bytes 24580
  11.1 9.9 %collective-permute-start.2 = (f32[38,8,128]{2,1,0:T(8,128)S(1)}, f32[38,8,128]{2,1,0:T(8,128)S(1)}, u32[]{:S(2)}, u32[]{:S(2)}) collective-permute-start(f32[38,8,128]{2,1,0:T(8,128)S(1)} %get-tuple-element.18), channel_id=1, source_target_pairs={{1,2},{3,4},{5,6},{2,1},{4,3},{6,5},{9,10},{11,12},{13,14},{10,9},... | collective-permute-start | bytes 466952 | tf_op jit(solution)/shard_map/ppermute | solution.py:406
  15.9 8.2 %collective-permute-start.3 = (f32[38,8,128]{2,1,0:T(8,128)S(1)}, f32[38,8,128]{2,1,0:T(8,128)S(1)}, u32[]{:S(2)}, u32[]{:S(2)}) collective-permute-start(f32[38,8,128]{2,1,0:T(8,128)S(1)} %get-tuple-element.19), channel_id=1, source_target_pairs={{0,1},{2,3},{4,5},{6,7},{1,0},{3,2},{5,4},{7,6},{8,9},{10,11},{12,... | collective-permute-start | bytes 466952 | tf_op jit(solution)/shard_map/ppermute | solution.py:406
  25.0 7.5 %collective-permute-start.4 = (f32[3,4,16,128]{3,2,1,0:T(8,128)S(1)}, f32[3,4,16,128]{3,2,1,0:T(8,128)S(1)}, u32[]{:S(2)}, u32[]{:S(2)}) collective-permute-start(f32[3,4,16,128]{3,2,1,0:T(8,128)S(1)} %get-tuple-element.23), channel_id=1, source_target_pairs={{0,256},{256,0},{512,768},{768,512},{1,257},{257,1},{513,769},{769... | collective-permute-start | bytes 294920 | tf_op jit(solution)/shard_map/ppermute | solution.py:462
  32.5 11.0 %collective-permute-start.5 = (f32[3,4,16,128]{3,2,1,0:T(8,128)S(1)}, f32[3,4,16,128]{3,2,1,0:T(8,128)S(1)}, u32[]{:S(2)}, u32[]{:S(2)}) collective-permute-start(f32[3,4,16,128]{3,2,1,0:T(8,128)S(1)} %add.3.own), channel_id=1, source_target_pairs={{0,768},{256,512},{512,256},{768,0},{1,769},{257,513},{513,257},{7... | collective-permute-start | bytes 294920 | tf_op jit(solution)/shard_map/ppermute | solution.py:463

commit v10 on v9

--- a/solution.py
+++ b/solution.py
@@ -394,6 +394,16 @@
         q_out[:, ys, :] = 2.0 * q_next[i][mid] - q[:, ys] + q_last[i]
 
 
+def shot_round(part, even, odd):
+    count = lax.axis_size("gx")
+    pairs = []
+    for shot in range(lax.axis_size("shot")):
+        for place in range(count):
+            other = shot ^ (odd if place % 2 else even)
+            pairs.append((shot * count + place, other * count + place))
+    return lax.ppermute(part, ("shot", "gx"), pairs)
+
+
 def finish_kernel(own, other, grad_e, grad_d):
     total = [own[i] + other[i] for i in range(3)]
     scale = 1.0 / jnp.sqrt(total[2] + 1.0)
@@ -458,9 +468,8 @@
         (source_cells, *edges, odds, evens, normal, inject),
         smem=(0,),
     )
-    shots = range(lax.axis_size("shot"))
-    grads = grads + lax.ppermute(grads, "shot", [(i, i ^ 1) for i in shots])
-    other = lax.ppermute(grads, "shot", [(i, i ^ 3) for i in shots])
+    grads = grads + shot_round(grads, 1, 3)
+    other = shot_round(grads, 3, 1)
     p_final, q_final = call(
         second_step_kernel,
         [(size_x, size_y, size_z)] * 2,

time: 44.5 us -> 44.1 us (level)
  the two profiles are of different devices: /device:TPU:562 before, /device:TPU:826 now
where the time goes in v10:
time: 44.1 us; the launch traced here: 43.7 us
  starting transfers between devices  18.7 us (42%)
  waiting for transfers between devices  16.8 us (38%)
  Pallas kernels  6.78 us (15%)
  between operations  1.42 us (3%)
    ppermute x4, starting transfers between devices, swap(): lax.ppermute(part, axis, [(i, i + 1) for i in lows] + [(i + 1, i) for i i...  13.9 us
    ppermute x2, waiting for transfers between devices, shot_round(): return lax.ppermute(part, ('shot', 'gx'), pairs)  10.5 us
    pallas_call x7, Pallas kernels, call(): pl.pallas_call(kernel, out_shape=shapes, in_specs=specs, out_specs=[pl.Bl...  6.78 us
    ppermute x4, waiting for transfers between devices, swap(): lax.ppermute(part, axis, [(i, i + 1) for i in lows] + [(i + 1, i) for i i...  6.3 us
    ppermute x2, starting transfers between devices, shot_round(): return lax.ppermute(part, ('shot', 'gx'), pairs)  4.77 us
  transfers between devices with their start and end apart: 6, of which 4 were waited for; matrix products, arithmetic and copies ran while one was open for 0% of the time, Pallas kernels for 9%

profile of v10, /device:TPU:826, one launch (start us, length us, event | category | flops | bytes accessed | tf_op | source)
XLA Modules:
  0.0 43.7 jit_solution(9629302315081501409)
XLA Ops:
  0.6 1.1 %shard_map.174 = (f32[52,16,128]{2,1,0:T(8,128)S(1)}, f32[30,16,128]{2,1,0:T(8,128)S(1)}, f32[30,16,128]{2,1,0:T(8,128)S(1)}) custom-call(f32[4,16,128]{2,1,0:T(8,128)} %bitcast.14, f32[4,16,128]{2,1,0:T(8,128)} %bitcast.15, f32[4,16,128]{2,1,0:T(8,128)} %bitcast.16, f32[4,16,128]{2,1,0:T(8,128)} %bitcast.17, f32[2,4,16,128]{3,2,1,0:T(8,128)} %bitcast.13, ...), custom_call_target="tpu_custom_call" | custom-call | flops 2000000 | bytes 2000000 | tf_op jit(solution)/shard_map/pallas_call | solution.py:23
  1.7 2.8 %collective-permute-start = (f32[30,16,128]{2,1,0:T(8,128)S(1)}, f32[30,16,128]{2,1,0:T(8,128)S(1)}, u32[]{:S(2)}, u32[]{:S(2)}) collective-permute-start(f32[30,16,128]{2,1,0:T(8,128)S(1)} %get-tuple-element.16), channel_id=1, source_target_pairs={{8,16},{24,32},{40,48},{56,64},{72,80},{88,96},{104,112},{120,128}... | collective-permute-start | bytes 737288 | tf_op jit(solution)/shard_map/ppermute | solution.py:416
  4.5 4.4 %collective-permute-start.1 = (f32[30,16,128]{2,1,0:T(8,128)S(1)}, f32[30,16,128]{2,1,0:T(8,128)S(1)}, u32[]{:S(2)}, u32[]{:S(2)}) collective-permute-start(f32[30,16,128]{2,1,0:T(8,128)S(1)} %get-tuple-element.17), channel_id=1, source_target_pairs={{0,8},{16,24},{32,40},{48,56},{64,72},{80,88},{96,104},{112,120},{... | collective-permute-start | bytes 737288 | tf_op jit(solution)/shard_map/ppermute | solution.py:416
  8.9 2.9 %collective-permute-done.far.far_x = f32[30,16,128]{2,1,0:T(8,128)S(1)} collective-permute-done((f32[30,16,128]{2,1,0:T(8,128)S(1)}, f32[30,16,128]{2,1,0:T(8,128)S(1)}, u32[]{:S(2)}, u32[]{:S(2)}) %collective-permute-start) | collective-permute-done | bytes 245792 | tf_op jit(solution)/shard_map/ppermute | solution.py:416
  11.9 0.0 collective-permute-done.1.near.near_x
  11.9 0.0 copy-start
  11.9 0.0 copy-start.1
  11.9 0.0 copy-start.3
  11.9 0.1 shard_map.175
  12.0 0.0 copy-start.2
  12.0 4.8 %collective-permute-start.2 = (f32[38,8,128]{2,1,0:T(8,128)S(1)}, f32[38,8,128]{2,1,0:T(8,128)S(1)}, u32[]{:S(2)}, u32[]{:S(2)}) collective-permute-start(f32[38,8,128]{2,1,0:T(8,128)S(1)} %get-tuple-element.18), channel_id=1, source_target_pairs={{1,2},{3,4},{5,6},{2,1},{4,3},{6,5},{9,10},{11,12},{13,14},{10,9},... | collective-permute-start | bytes 466952 | tf_op jit(solution)/shard_map/ppermute | solution.py:416
  16.8 1.9 %collective-permute-start.3 = (f32[38,8,128]{2,1,0:T(8,128)S(1)}, f32[38,8,128]{2,1,0:T(8,128)S(1)}, u32[]{:S(2)}, u32[]{:S(2)}) collective-permute-start(f32[38,8,128]{2,1,0:T(8,128)S(1)} %get-tuple-element.19), channel_id=1, source_target_pairs={{0,1},{2,3},{4,5},{6,7},{1,0},{3,2},{5,4},{7,6},{8,9},{10,11},{12,... | collective-permute-start | bytes 466952 | tf_op jit(solution)/shard_map/ppermute | solution.py:416
  19.4 0.0 copy-done
  19.4 0.0 copy-done.1
  19.4 0.0 copy-done.3
  19.4 0.0 copy-done.2
  19.4 1.8 %shard_map.177.inject = f32[256,128]{1,0:T(8,128)S(1)} custom-call(s32[1,2048]{1,0:T(1,128)S(1)} %copy-done.2, f32[2,2048]{1,0:T(2,128)S(1)} %bitcast.10, s32[1,2048]{1,0:T(1,128)S(1)} %bitcast.12, f32[2,2048]{1,0:T(2,128)S(1)} %bitcast.11), custom_call_target="tpu_custom_call" | custom-call | flops 800000000 | bytes 2000000 | tf_op jit(solution)/shard_map/pallas_call | solution.py:23
  21.2 0.7 %shard_map.176.normal = f32[3,2,12,8,128]{4,3,2,1,0:T(8,128)S(1)} custom-call(f32[52,16,128]{2,1,0:T(8,128)S(1)} %get-tuple-element.15.loc, f32[30,16,128]{2,1,0:T(8,128)S(1)} %collective-permute-done.far.far_x, f32[30,16,128]{2,1,0:T(8,128)S(1)} %collective-permute-done.1.near.near_x), custom_call_target="tpu_custom_call" | custom-call | flops 2000000 | bytes 2000000 | tf_op jit(solution)/shard_map/pallas_call | solution.py:23
  21.9 0.0 collective-permute-done.2.odds
  21.9 3.4 %collective-permute-done.3.evens = f32[38,8,128]{2,1,0:T(8,128)S(1)} collective-permute-done((f32[38,8,128]{2,1,0:T(8,128)S(1)}, f32[38,8,128]{2,1,0:T(8,128)S(1)}, u32[]{:S(2)}, u32[]{:S(2)}) %collective-permute-start.3) | collective-permute-done | bytes 155680 | tf_op jit(solution)/shard_map/ppermute | solution.py:416
  25.3 0.9 %shard_map.178 = (f32[3,4,16,128]{3,2,1,0:T(8,128)S(1)}, f32[3,12,8,128]{3,2,1,0:T(8,128)S(1)}) custom-call(s32[1]{0:T(128)S(6)} %copy.19.source, f32[52,16,128]{2,1,0:T(8,128)S(1)} %get-tuple-element.15.loc, f32[30,16,128]{2,1,0:T(8,128)S(1)} %collective-permute-done.far.far_x, f32[30,16,128]{2,1,0:T(8,128)S(1)} %collective-permute-done.1.near.near_x, ...), custom_call_target="tpu_custom_call" | custom-call | flops 2000000 | bytes 2000000 | tf_op jit(solution)/shard_map/pallas_call | solution.py:23
  26.2 2.5 %collective-permute-start.4 = (f32[3,4,16,128]{3,2,1,0:T(8,128)S(1)}, f32[3,4,16,128]{3,2,1,0:T(8,128)S(1)}, u32[]{:S(2)}, u32[]{:S(2)}) collective-permute-start(f32[3,4,16,128]{3,2,1,0:T(8,128)S(1)} %get-tuple-element.23), channel_id=1, source_target_pairs={{0,256},{8,776},{16,272},{24,792},{32,288},{40,808},{48,304},{56,8... | collective-permute-start | bytes 294920 | tf_op jit(solution)/shard_map/ppermute | solution.py:404
  28.7 4.9 %collective-permute-done.4 = f32[3,4,16,128]{3,2,1,0:T(8,128)S(1)} collective-permute-done((f32[3,4,16,128]{3,2,1,0:T(8,128)S(1)}, f32[3,4,16,128]{3,2,1,0:T(8,128)S(1)}, u32[]{:S(2)}, u32[]{:S(2)}) %collective-permute-start.4) | collective-permute-done | bytes 98336 | tf_op jit(solution)/shard_map/ppermute | solution.py:404
  33.6 2.2 %collective-permute-start.5 = (f32[3,4,16,128]{3,2,1,0:T(8,128)S(1)}, f32[3,4,16,128]{3,2,1,0:T(8,128)S(1)}, u32[]{:S(2)}, u32[]{:S(2)}) collective-permute-start(f32[3,4,16,128]{3,2,1,0:T(8,128)S(1)} %add.3.own), channel_id=1, source_target_pairs={{0,768},{8,264},{16,784},{24,280},{32,800},{40,296},{48,816},{56,3... | collective-permute-start | bytes 294920 | tf_op jit(solution)/shard_map/ppermute | solution.py:404
  35.8 1.6 %shard_map.179 = (f32[4,16,128]{2,1,0:T(8,128)}, f32[4,16,128]{2,1,0:T(8,128)}) custom-call(f32[52,16,128]{2,1,0:T(8,128)S(1)} %get-tuple-element.15.loc, f32[30,16,128]{2,1,0:T(8,128)S(1)} %collective-permute-done.far.far_x, f32[30,16,128]{2,1,0:T(8,128)S(1)} %collective-permute-done.1.near.near_x, f32[38,8,128]{2,1,0:T(8,128)S(1)} %collective-permute-done.2.odds, ...), custom_call_target="tpu_custom_call" | custom-call | flops 20000000 | bytes 2000000 | tf_op jit(solution)/shard_map/pallas_call | solution.py:23
  37.4 5.6 %collective-permute-done.5.other = f32[3,4,16,128]{3,2,1,0:T(8,128)S(1)} collective-permute-done((f32[3,4,16,128]{3,2,1,0:T(8,128)S(1)}, f32[3,4,16,128]{3,2,1,0:T(8,128)S(1)}, u32[]{:S(2)}, u32[]{:S(2)}) %collective-permute-start.5) | collective-permute-done | bytes 98336 | tf_op jit(solution)/shard_map/ppermute | solution.py:404
  43.1 0.7 %shard_map.180 = (f32[4,16,128]{2,1,0:T(8,128)}, f32[4,16,128]{2,1,0:T(8,128)}) custom-call(f32[3,4,16,128]{3,2,1,0:T(8,128)S(1)} %add.3.own, f32[3,4,16,128]{3,2,1,0:T(8,128)S(1)} %collective-permute-done.5.other), custom_call_target="tpu_custom_call" | custom-call | flops 2000000 | bytes 2000000 | tf_op jit(solution)/shard_map/pallas_call | solution.py:23
  (1 shorter events, 0.0 us)
Async XLA Ops:
  1.7 10.1 %collective-permute-start = (f32[30,16,128]{2,1,0:T(8,128)S(1)}, f32[30,16,128]{2,1,0:T(8,128)S(1)}, u32[]{:S(2)}, u32[]{:S(2)}) collective-permute-start(f32[30,16,128]{2,1,0:T(8,128)S(1)} %get-tuple-element.16), channel_id=1, source_target_pairs={{8,16},{24,32},{40,48},{56,64},{72,80},{88,96},{104,112},{120,128}... | collective-permute-start | bytes 737288 | tf_op jit(solution)/shard_map/ppermute | solution.py:416
  4.5 7.4 %collective-permute-start.1 = (f32[30,16,128]{2,1,0:T(8,128)S(1)}, f32[30,16,128]{2,1,0:T(8,128)S(1)}, u32[]{:S(2)}, u32[]{:S(2)}) collective-permute-start(f32[30,16,128]{2,1,0:T(8,128)S(1)} %get-tuple-element.17), channel_id=1, source_target_pairs={{0,8},{16,24},{32,40},{48,56},{64,72},{80,88},{96,104},{112,120},{... | collective-permute-start | bytes 737288 | tf_op jit(solution)/shard_map/ppermute | solution.py:416
  11.9 7.5 %copy-start = (f32[1,2,2048]{2,1,0:T(2,128)S(1)}, f32[1,2,2048]{2,1,0:T(2,128)}, u32[]{:S(2)}) copy-start(f32[1,2,2048]{2,1,0:T(2,128)} %param.26) | copy-start | bytes 49156
  11.9 7.5 %copy-start.1 = (f32[1,2,2048]{2,1,0:T(2,128)S(1)}, f32[1,2,2048]{2,1,0:T(2,128)}, u32[]{:S(2)}) copy-start(f32[1,2,2048]{2,1,0:T(2,128)} %param.28) | copy-start | bytes 49156
  11.9 7.5 %copy-start.3 = (s32[2048]{0:T(1024)S(1)}, s32[2048]{0:T(1024)}, u32[]{:S(2)}) copy-start(s32[2048]{0:T(1024)} %param.27) | copy-start | bytes 24580
  12.0 7.4 %copy-start.2 = (s32[1,2048]{1,0:T(1,128)S(1)}, s32[1,2048]{1,0:T(1,128)}, u32[]{:S(2)}) copy-start(s32[1,2048]{1,0:T(1,128)} %recv_cells.1) | copy-start | bytes 24580
  12.0 9.9 %collective-permute-start.2 = (f32[38,8,128]{2,1,0:T(8,128)S(1)}, f32[38,8,128]{2,1,0:T(8,128)S(1)}, u32[]{:S(2)}, u32[]{:S(2)}) collective-permute-start(f32[38,8,128]{2,1,0:T(8,128)S(1)} %get-tuple-element.18), channel_id=1, source_target_pairs={{1,2},{3,4},{5,6},{2,1},{4,3},{6,5},{9,10},{11,12},{13,14},{10,9},... | collective-permute-start | bytes 466952 | tf_op jit(solution)/shard_map/ppermute | solution.py:416
  16.8 8.5 %collective-permute-start.3 = (f32[38,8,128]{2,1,0:T(8,128)S(1)}, f32[38,8,128]{2,1,0:T(8,128)S(1)}, u32[]{:S(2)}, u32[]{:S(2)}) collective-permute-start(f32[38,8,128]{2,1,0:T(8,128)S(1)} %get-tuple-element.19), channel_id=1, source_target_pairs={{0,1},{2,3},{4,5},{6,7},{1,0},{3,2},{5,4},{7,6},{8,9},{10,11},{12,... | collective-permute-start | bytes 466952 | tf_op jit(solution)/shard_map/ppermute | solution.py:416
  26.2 7.4 %collective-permute-start.4 = (f32[3,4,16,128]{3,2,1,0:T(8,128)S(1)}, f32[3,4,16,128]{3,2,1,0:T(8,128)S(1)}, u32[]{:S(2)}, u32[]{:S(2)}) collective-permute-start(f32[3,4,16,128]{3,2,1,0:T(8,128)S(1)} %get-tuple-element.23), channel_id=1, source_target_pairs={{0,256},{8,776},{16,272},{24,792},{32,288},{40,808},{48,304},{56,8... | collective-permute-start | bytes 294920 | tf_op jit(solution)/shard_map/ppermute | solution.py:404
  33.6 9.5 %collective-permute-start.5 = (f32[3,4,16,128]{3,2,1,0:T(8,128)S(1)}, f32[3,4,16,128]{3,2,1,0:T(8,128)S(1)}, u32[]{:S(2)}, u32[]{:S(2)}) collective-permute-start(f32[3,4,16,128]{3,2,1,0:T(8,128)S(1)} %add.3.own), channel_id=1, source_target_pairs={{0,768},{8,264},{16,784},{24,280},{32,800},{40,296},{48,816},{56,3... | collective-permute-start | bytes 294920 | tf_op jit(solution)/shard_map/ppermute | solution.py:404

commit v11 on v10

--- a/solution.py
+++ b/solution.py
@@ -226,14 +226,14 @@
 
 
 def send_both(parts, evens, odds, start):
-    odd = lax.rem(lax.axis_index("gy"), 2) == 1
+    odd = lax.rem(lax.axis_index("gx") + lax.axis_index("gy"), 2) == 1
     rows = slice(start, start + parts[0].shape[0])
     evens[rows] = jnp.where(odd, parts[0], parts[1])
     odds[rows] = jnp.where(odd, parts[1], parts[0])
 
 
 def from_both(evens, odds):
-    odd = lax.rem(lax.axis_index("gy"), 2) == 1
+    odd = lax.rem(lax.axis_index("gx") + lax.axis_index("gy"), 2) == 1
     return jnp.where(odd, odds[...], evens[...]), jnp.where(odd, evens[...], odds[...])
 
 
@@ -394,6 +394,16 @@
         q_out[:, ys, :] = 2.0 * q_next[i][mid] - q[:, ys] + q_last[i]
 
 
+def swap_y(part, start):
+    count = lax.axis_size("gy")
+    pairs = []
+    for place in range(lax.axis_size("gx")):
+        for low in range((start + place) % 2, count - 1, 2):
+            low = place * count + low
+            pairs += [(low, low + 1), (low + 1, low)]
+    return lax.ppermute(part, ("gx", "gy"), pairs)
+
+
 def shot_round(part, even, odd):
     count = lax.axis_size("gx")
     pairs = []
@@ -460,7 +470,7 @@
     edges = (loc, far, near)
     tiles = WIDE * (size_x + 8) // 2 + NARROW * (size_x + 4) // 4
     odds, evens = call(pack_kernel, [(tiles, 8, size_z)] * 2, edges)
-    odds, evens = swap(odds, "gy", 1), swap(evens, "gy", 0)
+    odds, evens = swap_y(odds, 1), swap_y(evens, 0)
     (normal,) = call(normal_kernel, [(3, 2, size_x + 8, 8, size_z)], edges)
     grads, edge_normal = call(
         functools.partial(first_step_kernel, grid_y),

time: 44.1 us -> 44.2 us (level)
  the two profiles are of different devices: /device:TPU:826 before, /device:TPU:16 now
where the time goes in v11:
time: 44.2 us; the launch traced here: 43.9 us
  starting transfers between devices  22.4 us (51%)
  waiting for transfers between devices  13.3 us (30%)
  Pallas kernels  6.79 us (15%)
  between operations  1.43 us (3%)
    ppermute x2, starting transfers between devices, swap_y(): return lax.ppermute(part, ('gx', 'gy'), pairs)  13.1 us
    ppermute x2, waiting for transfers between devices, shot_round(): return lax.ppermute(part, ('shot', 'gx'), pairs)  11.7 us
    pallas_call x7, Pallas kernels, call(): pl.pallas_call(kernel, out_shape=shapes, in_specs=specs, out_specs=[pl.Bl...  6.79 us
    ppermute x2, starting transfers between devices, swap(): lax.ppermute(part, axis, [(i, i + 1) for i in lows] + [(i + 1, i) for i i...  5.42 us
    ppermute x2, starting transfers between devices, shot_round(): return lax.ppermute(part, ('shot', 'gx'), pairs)  3.84 us
    ppermute x2, waiting for transfers between devices, swap(): lax.ppermute(part, axis, [(i, i + 1) for i in lows] + [(i + 1, i) for i i...  1.11 us
  transfers between devices with their start and end apart: 6, of which 4 were waited for; matrix products, arithmetic and copies ran while one was open for 0% of the time, Pallas kernels for 9%

profile of v11, /device:TPU:16, one launch (start us, length us, event | category | flops | bytes accessed | tf_op | source)
XLA Modules:
  0.0 43.9 jit_solution(78253514675033826)
XLA Ops:
  0.6 1.1 %shard_map.174 = (f32[52,16,128]{2,1,0:T(8,128)S(1)}, f32[30,16,128]{2,1,0:T(8,128)S(1)}, f32[30,16,128]{2,1,0:T(8,128)S(1)}) custom-call(f32[4,16,128]{2,1,0:T(8,128)} %bitcast.14, f32[4,16,128]{2,1,0:T(8,128)} %bitcast.15, f32[4,16,128]{2,1,0:T(8,128)} %bitcast.16, f32[4,16,128]{2,1,0:T(8,128)} %bitcast.17, f32[2,4,16,128]{3,2,1,0:T(8,128)} %bitcast.13, ...), custom_call_target="tpu_custom_call" | custom-call | flops 2000000 | bytes 2000000 | tf_op jit(solution)/shard_map/pallas_call | solution.py:23
  1.7 0.7 %collective-permute-start = (f32[30,16,128]{2,1,0:T(8,128)S(1)}, f32[30,16,128]{2,1,0:T(8,128)S(1)}, u32[]{:S(2)}, u32[]{:S(2)}) collective-permute-start(f32[30,16,128]{2,1,0:T(8,128)S(1)} %get-tuple-element.16), channel_id=1, source_target_pairs={{8,16},{24,32},{40,48},{56,64},{72,80},{88,96},{104,112},{120,128}... | collective-permute-start | bytes 737288 | tf_op jit(solution)/shard_map/ppermute | solution.py:426
  2.4 4.7 %collective-permute-start.1 = (f32[30,16,128]{2,1,0:T(8,128)S(1)}, f32[30,16,128]{2,1,0:T(8,128)S(1)}, u32[]{:S(2)}, u32[]{:S(2)}) collective-permute-start(f32[30,16,128]{2,1,0:T(8,128)S(1)} %get-tuple-element.17), channel_id=1, source_target_pairs={{0,8},{16,24},{32,40},{48,56},{64,72},{80,88},{96,104},{112,120},{... | collective-permute-start | bytes 737288 | tf_op jit(solution)/shard_map/ppermute | solution.py:426
  7.2 0.0 collective-permute-done.far.far_x
  7.2 1.1 %collective-permute-done.1.near.near_x = f32[30,16,128]{2,1,0:T(8,128)S(1)} collective-permute-done((f32[30,16,128]{2,1,0:T(8,128)S(1)}, f32[30,16,128]{2,1,0:T(8,128)S(1)}, u32[]{:S(2)}, u32[]{:S(2)}) %collective-permute-start.1) | collective-permute-done | bytes 245792 | tf_op jit(solution)/shard_map/ppermute | solution.py:426
  8.3 0.0 copy-start
  8.3 0.0 copy-start.1
  8.3 0.0 copy-start.3
  8.3 0.1 shard_map.175
  8.4 0.0 copy-start.2
  8.4 3.6 %collective-permute-start.2 = (f32[38,8,128]{2,1,0:T(8,128)S(1)}, f32[38,8,128]{2,1,0:T(8,128)S(1)}, u32[]{:S(2)}, u32[]{:S(2)}) collective-permute-start(f32[38,8,128]{2,1,0:T(8,128)S(1)} %get-tuple-element.18), channel_id=1, source_target_pairs={{1,2},{2,1},{3,4},{4,3},{5,6},{6,5},{8,9},{9,8},{10,11},{11,10},{1... | collective-permute-start | bytes 466952 | tf_op jit(solution)/shard_map/ppermute | solution.py:404
  12.0 9.5 %collective-permute-start.3 = (f32[38,8,128]{2,1,0:T(8,128)S(1)}, f32[38,8,128]{2,1,0:T(8,128)S(1)}, u32[]{:S(2)}, u32[]{:S(2)}) collective-permute-start(f32[38,8,128]{2,1,0:T(8,128)S(1)} %get-tuple-element.19), channel_id=1, source_target_pairs={{0,1},{1,0},{2,3},{3,2},{4,5},{5,4},{6,7},{7,6},{9,10},{10,9},{11,... | collective-permute-start | bytes 466952 | tf_op jit(solution)/shard_map/ppermute | solution.py:404
  22.1 0.0 copy-done
  22.1 0.0 copy-done.1
  22.2 0.0 copy-done.3
  22.2 0.0 copy-done.2
  22.2 1.8 %shard_map.177.inject = f32[256,128]{1,0:T(8,128)S(1)} custom-call(s32[1,2048]{1,0:T(1,128)S(1)} %copy-done.2, f32[2,2048]{1,0:T(2,128)S(1)} %bitcast.10, s32[1,2048]{1,0:T(1,128)S(1)} %bitcast.12, f32[2,2048]{1,0:T(2,128)S(1)} %bitcast.11), custom_call_target="tpu_custom_call" | custom-call | flops 800000000 | bytes 2000000 | tf_op jit(solution)/shard_map/pallas_call | solution.py:23
  24.0 0.7 %shard_map.176.normal = f32[3,2,12,8,128]{4,3,2,1,0:T(8,128)S(1)} custom-call(f32[52,16,128]{2,1,0:T(8,128)S(1)} %get-tuple-element.15.loc, f32[30,16,128]{2,1,0:T(8,128)S(1)} %collective-permute-done.far.far_x, f32[30,16,128]{2,1,0:T(8,128)S(1)} %collective-permute-done.1.near.near_x), custom_call_target="tpu_custom_call" | custom-call | flops 2000000 | bytes 2000000 | tf_op jit(solution)/shard_map/pallas_call | solution.py:23
  24.7 0.0 collective-permute-done.2.odds
  24.7 0.4 collective-permute-done.3.evens
  25.1 0.9 %shard_map.178 = (f32[3,4,16,128]{3,2,1,0:T(8,128)S(1)}, f32[3,12,8,128]{3,2,1,0:T(8,128)S(1)}) custom-call(s32[1]{0:T(128)S(6)} %copy.19.source, f32[52,16,128]{2,1,0:T(8,128)S(1)} %get-tuple-element.15.loc, f32[30,16,128]{2,1,0:T(8,128)S(1)} %collective-permute-done.far.far_x, f32[30,16,128]{2,1,0:T(8,128)S(1)} %collective-permute-done.1.near.near_x, ...), custom_call_target="tpu_custom_call" | custom-call | flops 2000000 | bytes 2000000 | tf_op jit(solution)/shard_map/pallas_call | solution.py:23
  26.0 1.9 %collective-permute-start.4 = (f32[3,4,16,128]{3,2,1,0:T(8,128)S(1)}, f32[3,4,16,128]{3,2,1,0:T(8,128)S(1)}, u32[]{:S(2)}, u32[]{:S(2)}) collective-permute-start(f32[3,4,16,128]{3,2,1,0:T(8,128)S(1)} %get-tuple-element.23), channel_id=1, source_target_pairs={{0,256},{8,776},{16,272},{24,792},{32,288},{40,808},{48,304},{56,8... | collective-permute-start | bytes 294920 | tf_op jit(solution)/shard_map/ppermute | solution.py:414
  27.9 5.6 %collective-permute-done.4 = f32[3,4,16,128]{3,2,1,0:T(8,128)S(1)} collective-permute-done((f32[3,4,16,128]{3,2,1,0:T(8,128)S(1)}, f32[3,4,16,128]{3,2,1,0:T(8,128)S(1)}, u32[]{:S(2)}, u32[]{:S(2)}) %collective-permute-start.4) | collective-permute-done | bytes 98336 | tf_op jit(solution)/shard_map/ppermute | solution.py:414
  33.5 1.9 %collective-permute-start.5 = (f32[3,4,16,128]{3,2,1,0:T(8,128)S(1)}, f32[3,4,16,128]{3,2,1,0:T(8,128)S(1)}, u32[]{:S(2)}, u32[]{:S(2)}) collective-permute-start(f32[3,4,16,128]{3,2,1,0:T(8,128)S(1)} %add.3.own), channel_id=1, source_target_pairs={{0,768},{8,264},{16,784},{24,280},{32,800},{40,296},{48,816},{56,3... | collective-permute-start | bytes 294920 | tf_op jit(solution)/shard_map/ppermute | solution.py:414
  35.5 1.6 %shard_map.179 = (f32[4,16,128]{2,1,0:T(8,128)}, f32[4,16,128]{2,1,0:T(8,128)}) custom-call(f32[52,16,128]{2,1,0:T(8,128)S(1)} %get-tuple-element.15.loc, f32[30,16,128]{2,1,0:T(8,128)S(1)} %collective-permute-done.far.far_x, f32[30,16,128]{2,1,0:T(8,128)S(1)} %collective-permute-done.1.near.near_x, f32[38,8,128]{2,1,0:T(8,128)S(1)} %collective-permute-done.2.odds, ...), custom_call_target="tpu_custom_call" | custom-call | flops 20000000 | bytes 2000000 | tf_op jit(solution)/shard_map/pallas_call | solution.py:23
  37.1 6.1 %collective-permute-done.5.other = f32[3,4,16,128]{3,2,1,0:T(8,128)S(1)} collective-permute-done((f32[3,4,16,128]{3,2,1,0:T(8,128)S(1)}, f32[3,4,16,128]{3,2,1,0:T(8,128)S(1)}, u32[]{:S(2)}, u32[]{:S(2)}) %collective-permute-start.5) | collective-permute-done | bytes 98336 | tf_op jit(solution)/shard_map/ppermute | solution.py:414
  43.2 0.7 %shard_map.180 = (f32[4,16,128]{2,1,0:T(8,128)}, f32[4,16,128]{2,1,0:T(8,128)}) custom-call(f32[3,4,16,128]{3,2,1,0:T(8,128)S(1)} %add.3.own, f32[3,4,16,128]{3,2,1,0:T(8,128)S(1)} %collective-permute-done.5.other), custom_call_target="tpu_custom_call" | custom-call | flops 2000000 | bytes 2000000 | tf_op jit(solution)/shard_map/pallas_call | solution.py:23
  (1 shorter events, 0.0 us)
Async XLA Ops:
  1.7 5.4 %collective-permute-start = (f32[30,16,128]{2,1,0:T(8,128)S(1)}, f32[30,16,128]{2,1,0:T(8,128)S(1)}, u32[]{:S(2)}, u32[]{:S(2)}) collective-permute-start(f32[30,16,128]{2,1,0:T(8,128)S(1)} %get-tuple-element.16), channel_id=1, source_target_pairs={{8,16},{24,32},{40,48},{56,64},{72,80},{88,96},{104,112},{120,128}... | collective-permute-start | bytes 737288 | tf_op jit(solution)/shard_map/ppermute | solution.py:426
  2.4 5.9 %collective-permute-start.1 = (f32[30,16,128]{2,1,0:T(8,128)S(1)}, f32[30,16,128]{2,1,0:T(8,128)S(1)}, u32[]{:S(2)}, u32[]{:S(2)}) collective-permute-start(f32[30,16,128]{2,1,0:T(8,128)S(1)} %get-tuple-element.17), channel_id=1, source_target_pairs={{0,8},{16,24},{32,40},{48,56},{64,72},{80,88},{96,104},{112,120},{... | collective-permute-start | bytes 737288 | tf_op jit(solution)/shard_map/ppermute | solution.py:426
  8.3 13.9 %copy-start = (f32[1,2,2048]{2,1,0:T(2,128)S(1)}, f32[1,2,2048]{2,1,0:T(2,128)}, u32[]{:S(2)}) copy-start(f32[1,2,2048]{2,1,0:T(2,128)} %param.26) | copy-start | bytes 49156
  8.3 13.9 %copy-start.1 = (f32[1,2,2048]{2,1,0:T(2,128)S(1)}, f32[1,2,2048]{2,1,0:T(2,128)}, u32[]{:S(2)}) copy-start(f32[1,2,2048]{2,1,0:T(2,128)} %param.28) | copy-start | bytes 49156
  8.3 13.9 %copy-start.3 = (s32[2048]{0:T(1024)S(1)}, s32[2048]{0:T(1024)}, u32[]{:S(2)}) copy-start(s32[2048]{0:T(1024)} %param.27) | copy-start | bytes 24580
  8.4 13.8 %copy-start.2 = (s32[1,2048]{1,0:T(1,128)S(1)}, s32[1,2048]{1,0:T(1,128)}, u32[]{:S(2)}) copy-start(s32[1,2048]{1,0:T(1,128)} %recv_cells.1) | copy-start | bytes 24580
  8.4 16.3 %collective-permute-start.2 = (f32[38,8,128]{2,1,0:T(8,128)S(1)}, f32[38,8,128]{2,1,0:T(8,128)S(1)}, u32[]{:S(2)}, u32[]{:S(2)}) collective-permute-start(f32[38,8,128]{2,1,0:T(8,128)S(1)} %get-tuple-element.18), channel_id=1, source_target_pairs={{1,2},{2,1},{3,4},{4,3},{5,6},{6,5},{8,9},{9,8},{10,11},{11,10},{1... | collective-permute-start | bytes 466952 | tf_op jit(solution)/shard_map/ppermute | solution.py:404
  12.0 13.1 %collective-permute-start.3 = (f32[38,8,128]{2,1,0:T(8,128)S(1)}, f32[38,8,128]{2,1,0:T(8,128)S(1)}, u32[]{:S(2)}, u32[]{:S(2)}) collective-permute-start(f32[38,8,128]{2,1,0:T(8,128)S(1)} %get-tuple-element.19), channel_id=1, source_target_pairs={{0,1},{1,0},{2,3},{3,2},{4,5},{5,4},{6,7},{7,6},{9,10},{10,9},{11,... | collective-permute-start | bytes 466952 | tf_op jit(solution)/shard_map/ppermute | solution.py:404
  26.0 7.5 %collective-permute-start.4 = (f32[3,4,16,128]{3,2,1,0:T(8,128)S(1)}, f32[3,4,16,128]{3,2,1,0:T(8,128)S(1)}, u32[]{:S(2)}, u32[]{:S(2)}) collective-permute-start(f32[3,4,16,128]{3,2,1,0:T(8,128)S(1)} %get-tuple-element.23), channel_id=1, source_target_pairs={{0,256},{8,776},{16,272},{24,792},{32,288},{40,808},{48,304},{56,8... | collective-permute-start | bytes 294920 | tf_op jit(solution)/shard_map/ppermute | solution.py:414
  33.5 9.7 %collective-permute-start.5 = (f32[3,4,16,128]{3,2,1,0:T(8,128)S(1)}, f32[3,4,16,128]{3,2,1,0:T(8,128)S(1)}, u32[]{:S(2)}, u32[]{:S(2)}) collective-permute-start(f32[3,4,16,128]{3,2,1,0:T(8,128)S(1)} %add.3.own), channel_id=1, source_target_pairs={{0,768},{8,264},{16,784},{24,280},{32,800},{40,296},{48,816},{56,3... | collective-permute-start | bytes 294920 | tf_op jit(solution)/shard_map/ppermute | solution.py:414
